TPU v7x, 256 devices: a whole 4x4x8 slice. The times are simulated.
256 devices in a mesh: row: 16 (over x, y), col: 8 (over z), layer: 2 (over core).
Axes of the slice: x: 4, y: 4, z: 8, core: 2. Of those that a mesh axis runs over, the one named last changes fastest.
Arguments:
- a_blocks: bfloat16 [8, 16, 16, 128, 128], P('col', 'row'), may hold values from -6 to 6
- a_rows: int32 [8, 16, 16], P('col', 'row'), may hold values from 0 to 8, as said below
- a_cols: int32 [8, 16, 16], P('col', 'row'), may hold values from 0 to 3, as said below
- b_blocks: bfloat16 [16, 16, 8, 128, 128], P('col', 'row'), may hold values from -0.09375 to 0.09375
- b_rows: int32 [16, 16, 8], P('col', 'row'), may hold values from 0 to 4, as said below
- b_cols: int32 [16, 16, 8], P('col', 'row'), may hold values from 0 to 3, as said below
- prod_keep: int32 [64, 16, 64], P('col', None, 'row'), may hold values 0 or 1
- res_keep: int32 [64, 64], P('col', ('row', 'layer')), may hold values 0 or 1
Outputs:
- c_blocks: bfloat16 [8192, 8192], P('col', ('row', 'layer'))
Inputs may be any that keep to these rules, and one draw needn't show every extreme that they name: `a_rows`: within one tile the live slots name distinct blocks; a row of 8 marks an empty slot, whose column is 0 and whose block is ignored. Every tile has at least one live slot, some tile is full and some tile has empty slots. `a_cols`: column of each slot of A; 0 in empty slots. `b_rows`: within one tile the live slots name distinct blocks; a row of 4 marks an empty slot, whose column is 0 and whose block is ignored. Every tile has at least one live slot, some tile is full and some tile has empty slots. `b_cols`: column of each slot of B; 0 in empty slots.
All inputs are finite; a program needn't handle non-finite values. No bound on the sum of `prod_keep` or of `res_keep` on one device may be relied on, other than what follows from the above.
Results may differ from a plain program's by a relative error of at most 0.001.
Values may be sent and summed in bfloat16 or wider, within the bound.
No kernel may reach another device: no remote copies, remote signals or barrier semaphores. Data moves between devices by JAX's collectives and lax.ppermute only.
A program may use at most 64 MiB of HBM per device.

v0:
```python
import jax
import jax.numpy as jnp
from jax import lax
from jax.sharding import PartitionSpec as P

RB = 8
CB = 4
KP = 4


def as_sent(x):
    return jax.tree.map(lambda a: a.astype(jnp.bfloat16) if a.dtype == jnp.float32 else a, x)


def from_behind(block, axis, distance):
    devices = range(lax.axis_size(axis))
    route = [((i - distance) % len(devices), i) for i in devices]
    return lax.ppermute(block, axis, route)


def dense_panel(blocks, position, height, width, first_col, col_span):
    number = position.astype(jnp.int32)
    row_of = number // width
    col_of = number % width
    inside = (col_of >= first_col) & (col_of < first_col + col_span) & (row_of < height)
    target = jnp.where(inside, row_of * col_span + col_of - first_col, height * col_span)
    picker = (target[:, None] == jnp.arange(height * col_span, dtype=jnp.int32)[None, :]).astype(
        jnp.bfloat16
    )
    placed = jnp.einsum("sp,sxy->pxy", picker, blocks, preferred_element_type=jnp.float32).astype(
        jnp.bfloat16
    )
    block_edge = blocks.shape[1]
    placed = placed.reshape(height, col_span, block_edge, block_edge).transpose(0, 2, 1, 3)
    return placed.reshape(height * block_edge, col_span * block_edge)


def body(a_blocks, a_rows, a_cols, b_blocks, b_rows, b_cols, prod_keep, res_keep):
    rows_total = lax.axis_size("row")
    cols_total = lax.axis_size("col")
    layers = lax.axis_size("layer")
    per_device = rows_total // cols_total
    row_band = lax.axis_index("col")
    column_band = lax.axis_index("row")
    layer_index = lax.axis_index("layer")
    block_edge = a_blocks.shape[3]
    a_state = (a_blocks[0, 0], (a_rows[0, 0] * KP + a_cols[0, 0]).astype(jnp.bfloat16))
    b_state = (b_blocks[:, 0], (b_rows[:, 0] * CB + b_cols[:, 0]).astype(jnp.bfloat16))

    def advance(carried, group_start, first_col, col_span, last_group):
        a_now, b_now, running = carried
        for offset in range(per_device):
            panel_index = (column_band + row_band * per_device + group_start + offset) % rows_total
            left_dense = dense_panel(a_now[0], a_now[1], RB, KP, 0, KP)
            right_dense = dense_panel(
                b_now[0][offset], b_now[1][offset], KP, CB, first_col, col_span
            )
            product = jnp.dot(left_dense, right_dense, preferred_element_type=jnp.float32)
            keep_now = lax.dynamic_index_in_dim(prod_keep, panel_index, 1, keepdims=False)
            keep_now = lax.dynamic_slice_in_dim(keep_now, first_col, col_span, 1).astype(
                jnp.float32
            )
            product = (
                product.reshape(RB, block_edge, col_span, block_edge) * keep_now[:, None, :, None]
            )
            running = running + product.reshape(RB * block_edge, col_span * block_edge)
            if not (last_group and offset == per_device - 1):
                a_now = jax.tree.map(
                    lambda part, own: part.astype(own.dtype),
                    from_behind(as_sent(a_now), "row", -1),
                    a_now,
                )
        if not last_group:
            b_now = jax.tree.map(
                lambda part, own: part.astype(own.dtype),
                from_behind(as_sent(b_now), "col", -1),
                b_now,
            )
        return (a_now, b_now, running)

    col_span = CB // layers
    first_col = layer_index * col_span
    running = jnp.zeros((RB * block_edge, col_span * block_edge), jnp.float32)

    def scan_step(carried, group_number):
        return (advance(carried, group_number * per_device, first_col, col_span, False), None)

    carried, unused = lax.scan(
        scan_step, (a_state, b_state, running), jnp.arange(cols_total - 1, dtype=jnp.int32)
    )
    carried = advance(carried, (cols_total - 1) * per_device, first_col, col_span, True)
    result = carried[2]
    out_span = result.shape[1] // block_edge
    masked = (
        result.reshape(RB, block_edge, out_span, block_edge)
        * res_keep.astype(jnp.float32)[:, None, :, None]
    )
    return masked.reshape(RB * block_edge, out_span * block_edge).astype(jnp.bfloat16)


def solution(mesh):
    return jax.shard_map(
        body,
        mesh=mesh,
        in_specs=(
            P("col", "row", None, None, None),
            P("col", "row", None),
            P("col", "row", None),
            P("col", "row", None, None, None),
            P("col", "row", None),
            P("col", "row", None),
            P("col", None, "row"),
            P("col", ("row", "layer")),
        ),
        out_specs=P("col", ("row", "layer")),
        check_vma=False,
    )
```

profile of v0, /device:TPU:30, one launch (start us, length us, event | category | flops | bytes accessed | tf_op | source)
XLA Modules:
  0.0 264.9 jit_solution(8019030281743106246)
XLA Ops:
  4.3 241.5 %while.22 = (s32[]{:T(128)}, bf16[16,128,128]{2,0,1:T(8,128)(2,1)}, bf16[16]{0:T(256)(128)(2,1)S(1)}, bf16[2,8,128,128]{3,1,2,0:T(8,128)(2,1)}, bf16[2,8]{1,0:T(...) while((s32[]{:T(128)}, bf16[16,128,128]{2,0,1:T(8,128)(2,1)}, ...), condition=%wide.region_1.2_spmd.clone, body=%wide.region_0.1_spmd.clone.sunk | while | flops 577243648 | bytes 31983928 | solution.py:88
  7.5 5.9 %collective-permute-start.4 = (bf16[2,8,128,128]{3,1,2,0:T(8,128)(2,1)}, bf16[2,8,128,128]{3,1,2,0:T(8,128)(2,1)}, u32[]{:S(2)}, u32[]{:S(2)}) collective-permute-start(bf16[2,8,128,128]{3,1,2,0:T(8,128)(2,1)} %copy.169), channel_id=1, source_target_pairs={{2,0},{4,2},{6,4},{8,6},{10,8},{12,10},{14,12},{0,14},{3,1},{5,3},... | collective-permute-start | bytes 1572872 | tf_op jit(solution)/shard_map/while/body/eval_jaxpr/ppermute | solution.py:18
  26.3 3.4 %collective-permute-start.1 = (bf16[16,128,128]{2,0,1:T(8,128)(2,1)}, bf16[16,128,128]{2,0,1:T(8,128)(2,1)}, u32[]{:S(2)}, u32[]{:S(2)}) collective-permute-start(bf16[16,128,128]{2,0,1:T(8,128)(2,1)} %collective-permute-done), channel_id=1, source_target_pairs={{16,0},{32,16},{48,32},{64,48},{80,64},{96,80},{112,96},{128,112},... | collective-permute-start | bytes 1572872 | tf_op jit(solution)/shard_map/while/body/eval_jaxpr/ppermute | solution.py:18
  32.4 9.9 %collective-permute-done.1 = bf16[16,128,128]{2,0,1:T(8,128)(2,1)} collective-permute-done((bf16[16,128,128]{2,0,1:T(8,128)(2,1)}, bf16[16,128,128]{2,0,1:T(8,128)(2,1)}, u32[]{:S(2)}, u32[]{:S(2)}) %collective-permute-start.1) | collective-permute-done | bytes 524320 | tf_op jit(solution)/shard_map/while/body/eval_jaxpr/ppermute | solution.py:18
  44.9 3.2 %collective-permute-start.4 = (bf16[2,8,128,128]{3,1,2,0:T(8,128)(2,1)}, bf16[2,8,128,128]{3,1,2,0:T(8,128)(2,1)}, u32[]{:S(2)}, u32[]{:S(2)}) collective-permute-start(bf16[2,8,128,128]{3,1,2,0:T(8,128)(2,1)} %copy.169), channel_id=1, source_target_pairs={{2,0},{4,2},{6,4},{8,6},{10,8},{12,10},{14,12},{0,14},{3,1},{5,3},... | collective-permute-start | bytes 1572872 | tf_op jit(solution)/shard_map/while/body/eval_jaxpr/ppermute | solution.py:18
  60.7 2.5 collective-permute-start.1
  64.3 2.8 %bitcast_add_fusion.5 = f32[1024,256]{0,1:T(8,128)} fusion(f32[32,8,8,128]{3,2,1,0:T(8,128)S(1)} %bitcast.285, f32[32,8,8,128]{3,2,1,0:T(8,128)S(1)} %bitcast.284, f32[1024,256]{0,1:T(8,128)} %get-tuple-element.447, pred[]{:T(512)S(6)} %compare.83), kind=kLoop, calls=%fused_computation.6.clone.1 | loop fusion | flops 786432 | bytes 4194305 | tf_op jit(solution)/shard_map/while/body/eval_jaxpr/add | solution.py:66
  67.1 8.5 %collective-permute-done.1 = bf16[16,128,128]{2,0,1:T(8,128)(2,1)} collective-permute-done((bf16[16,128,128]{2,0,1:T(8,128)(2,1)}, bf16[16,128,128]{2,0,1:T(8,128)(2,1)}, u32[]{:S(2)}, u32[]{:S(2)}) %collective-permute-start.1) | collective-permute-done | bytes 524320 | tf_op jit(solution)/shard_map/while/body/eval_jaxpr/ppermute | solution.py:18
  77.5 2.7 %collective-permute-start.4 = (bf16[2,8,128,128]{3,1,2,0:T(8,128)(2,1)}, bf16[2,8,128,128]{3,1,2,0:T(8,128)(2,1)}, u32[]{:S(2)}, u32[]{:S(2)}) collective-permute-start(bf16[2,8,128,128]{3,1,2,0:T(8,128)(2,1)} %copy.169), channel_id=1, source_target_pairs={{2,0},{4,2},{6,4},{8,6},{10,8},{12,10},{14,12},{0,14},{3,1},{5,3},... | collective-permute-start | bytes 1572872 | tf_op jit(solution)/shard_map/while/body/eval_jaxpr/ppermute | solution.py:18
  94.6 2.8 %bitcast_add_fusion.5 = f32[1024,256]{0,1:T(8,128)} fusion(f32[32,8,8,128]{3,2,1,0:T(8,128)S(1)} %bitcast.285, f32[32,8,8,128]{3,2,1,0:T(8,128)S(1)} %bitcast.284, f32[1024,256]{0,1:T(8,128)} %get-tuple-element.447, pred[]{:T(512)S(6)} %compare.83), kind=kLoop, calls=%fused_computation.6.clone.1 | loop fusion | flops 786432 | bytes 4194305 | tf_op jit(solution)/shard_map/while/body/eval_jaxpr/add | solution.py:66
  97.7 8.3 %collective-permute-done.1 = bf16[16,128,128]{2,0,1:T(8,128)(2,1)} collective-permute-done((bf16[16,128,128]{2,0,1:T(8,128)(2,1)}, bf16[16,128,128]{2,0,1:T(8,128)(2,1)}, u32[]{:S(2)}, u32[]{:S(2)}) %collective-permute-start.1) | collective-permute-done | bytes 524320 | tf_op jit(solution)/shard_map/while/body/eval_jaxpr/ppermute | solution.py:18
  123.0 3.1 %collective-permute-start.1 = (bf16[16,128,128]{2,0,1:T(8,128)(2,1)}, bf16[16,128,128]{2,0,1:T(8,128)(2,1)}, u32[]{:S(2)}, u32[]{:S(2)}) collective-permute-start(bf16[16,128,128]{2,0,1:T(8,128)(2,1)} %collective-permute-done), channel_id=1, source_target_pairs={{16,0},{32,16},{48,32},{64,48},{80,64},{96,80},{112,96},{128,112},... | collective-permute-start | bytes 1572872 | tf_op jit(solution)/shard_map/while/body/eval_jaxpr/ppermute | solution.py:18
  127.2 2.8 %bitcast_add_fusion.5 = f32[1024,256]{0,1:T(8,128)} fusion(f32[32,8,8,128]{3,2,1,0:T(8,128)S(1)} %bitcast.285, f32[32,8,8,128]{3,2,1,0:T(8,128)S(1)} %bitcast.284, f32[1024,256]{0,1:T(8,128)} %get-tuple-element.447, pred[]{:T(512)S(6)} %compare.83), kind=kLoop, calls=%fused_computation.6.clone.1 | loop fusion | flops 786432 | bytes 4194305 | tf_op jit(solution)/shard_map/while/body/eval_jaxpr/add | solution.py:66
  130.0 8.5 %collective-permute-done.1 = bf16[16,128,128]{2,0,1:T(8,128)(2,1)} collective-permute-done((bf16[16,128,128]{2,0,1:T(8,128)(2,1)}, bf16[16,128,128]{2,0,1:T(8,128)(2,1)}, u32[]{:S(2)}, u32[]{:S(2)}) %collective-permute-start.1) | collective-permute-done | bytes 524320 | tf_op jit(solution)/shard_map/while/body/eval_jaxpr/ppermute | solution.py:18
  143.0 4.1 %collective-permute-start.4 = (bf16[2,8,128,128]{3,1,2,0:T(8,128)(2,1)}, bf16[2,8,128,128]{3,1,2,0:T(8,128)(2,1)}, u32[]{:S(2)}, u32[]{:S(2)}) collective-permute-start(bf16[2,8,128,128]{3,1,2,0:T(8,128)(2,1)} %copy.169), channel_id=1, source_target_pairs={{2,0},{4,2},{6,4},{8,6},{10,8},{12,10},{14,12},{0,14},{3,1},{5,3},... | collective-permute-start | bytes 1572872 | tf_op jit(solution)/shard_map/while/body/eval_jaxpr/ppermute | solution.py:18
  160.9 2.8 %bitcast_add_fusion.5 = f32[1024,256]{0,1:T(8,128)} fusion(f32[32,8,8,128]{3,2,1,0:T(8,128)S(1)} %bitcast.285, f32[32,8,8,128]{3,2,1,0:T(8,128)S(1)} %bitcast.284, f32[1024,256]{0,1:T(8,128)} %get-tuple-element.447, pred[]{:T(512)S(6)} %compare.83), kind=kLoop, calls=%fused_computation.6.clone.1 | loop fusion | flops 786432 | bytes 4194305 | tf_op jit(solution)/shard_map/while/body/eval_jaxpr/add | solution.py:66
  164.5 9.8 %collective-permute-done.1 = bf16[16,128,128]{2,0,1:T(8,128)(2,1)} collective-permute-done((bf16[16,128,128]{2,0,1:T(8,128)(2,1)}, bf16[16,128,128]{2,0,1:T(8,128)(2,1)}, u32[]{:S(2)}, u32[]{:S(2)}) %collective-permute-start.1) | collective-permute-done | bytes 524320 | tf_op jit(solution)/shard_map/while/body/eval_jaxpr/ppermute | solution.py:18
  176.2 6.6 %collective-permute-start.4 = (bf16[2,8,128,128]{3,1,2,0:T(8,128)(2,1)}, bf16[2,8,128,128]{3,1,2,0:T(8,128)(2,1)}, u32[]{:S(2)}, u32[]{:S(2)}) collective-permute-start(bf16[2,8,128,128]{3,1,2,0:T(8,128)(2,1)} %copy.169), channel_id=1, source_target_pairs={{2,0},{4,2},{6,4},{8,6},{10,8},{12,10},{14,12},{0,14},{3,1},{5,3},... | collective-permute-start | bytes 1572872 | tf_op jit(solution)/shard_map/while/body/eval_jaxpr/ppermute | solution.py:18
  196.6 2.8 %bitcast_add_fusion.5 = f32[1024,256]{0,1:T(8,128)} fusion(f32[32,8,8,128]{3,2,1,0:T(8,128)S(1)} %bitcast.285, f32[32,8,8,128]{3,2,1,0:T(8,128)S(1)} %bitcast.284, f32[1024,256]{0,1:T(8,128)} %get-tuple-element.447, pred[]{:T(512)S(6)} %compare.83), kind=kLoop, calls=%fused_computation.6.clone.1 | loop fusion | flops 786432 | bytes 4194305 | tf_op jit(solution)/shard_map/while/body/eval_jaxpr/add | solution.py:66
  200.3 9.8 %collective-permute-done.1 = bf16[16,128,128]{2,0,1:T(8,128)(2,1)} collective-permute-done((bf16[16,128,128]{2,0,1:T(8,128)(2,1)}, bf16[16,128,128]{2,0,1:T(8,128)(2,1)}, u32[]{:S(2)}, u32[]{:S(2)}) %collective-permute-start.1) | collective-permute-done | bytes 524320 | tf_op jit(solution)/shard_map/while/body/eval_jaxpr/ppermute | solution.py:18
  211.9 5.5 %collective-permute-start.4 = (bf16[2,8,128,128]{3,1,2,0:T(8,128)(2,1)}, bf16[2,8,128,128]{3,1,2,0:T(8,128)(2,1)}, u32[]{:S(2)}, u32[]{:S(2)}) collective-permute-start(bf16[2,8,128,128]{3,1,2,0:T(8,128)(2,1)} %copy.169), channel_id=1, source_target_pairs={{2,0},{4,2},{6,4},{8,6},{10,8},{12,10},{14,12},{0,14},{3,1},{5,3},... | collective-permute-start | bytes 1572872 | tf_op jit(solution)/shard_map/while/body/eval_jaxpr/ppermute | solution.py:18
  231.2 2.8 %bitcast_add_fusion.5 = f32[1024,256]{0,1:T(8,128)} fusion(f32[32,8,8,128]{3,2,1,0:T(8,128)S(1)} %bitcast.285, f32[32,8,8,128]{3,2,1,0:T(8,128)S(1)} %bitcast.284, f32[1024,256]{0,1:T(8,128)} %get-tuple-element.447, pred[]{:T(512)S(6)} %compare.83), kind=kLoop, calls=%fused_computation.6.clone.1 | loop fusion | flops 786432 | bytes 4194305 | tf_op jit(solution)/shard_map/while/body/eval_jaxpr/add | solution.py:66
  234.8 11.0 %collective-permute-done.1 = bf16[16,128,128]{2,0,1:T(8,128)(2,1)} collective-permute-done((bf16[16,128,128]{2,0,1:T(8,128)(2,1)}, bf16[16,128,128]{2,0,1:T(8,128)(2,1)}, u32[]{:S(2)}, u32[]{:S(2)}) %collective-permute-start.1) | collective-permute-done | bytes 524320 | tf_op jit(solution)/shard_map/while/body/eval_jaxpr/ppermute | solution.py:18
  252.4 6.3 %collective-permute-done.6 = bf16[16]{0:T(256)(128)(2,1)S(1)} collective-permute-done((bf16[16]{0:T(256)(128)(2,1)S(1)}, bf16[16]{0:T(256)(128)(2,1)S(1)}, u32[]{:S(2)}, u32[]{:S(2)}) %collective-permute-start.6) | collective-permute-done | bytes 64 | tf_op jit(solution)/shard_map/ppermute | solution.py:18
  (295 shorter events, 133.3 us)
Async XLA Ops:
  4.4 19.9 %collective-permute-start = (bf16[16,128,128]{2,0,1:T(8,128)(2,1)}, bf16[16,128,128]{2,0,1:T(8,128)(2,1)}, u32[]{:S(2)}, u32[]{:S(2)}) collective-permute-start(bf16[16,128,128]{2,0,1:T(8,128)(2,1)} %get-tuple-element.443), channel_id=1, source_target_pairs={{16,0},{32,16},{48,32},{64,48},{80,64},{96,80},{112,96},{128,112},... | collective-permute-start | bytes 1572872 | tf_op jit(solution)/shard_map/while/body/eval_jaxpr/ppermute | solution.py:18
  5.2 18.6 %collective-permute-start.2 = (bf16[16]{0:T(256)(128)(2,1)S(1)}, bf16[16]{0:T(256)(128)(2,1)S(1)}, u32[]{:S(2)}, u32[]{:S(2)}) collective-permute-start(bf16[16]{0:T(256)(128)(2,1)S(1)} %get-tuple-element.444), channel_id=1, source_target_pairs={{16,0},{32,16},{48,32},{64,48},{80,64},{96,80},{112,96},{128,112},... | collective-permute-start | bytes 104 | tf_op jit(solution)/shard_map/while/body/eval_jaxpr/ppermute | solution.py:18
  7.5 24.9 %collective-permute-start.4 = (bf16[2,8,128,128]{3,1,2,0:T(8,128)(2,1)}, bf16[2,8,128,128]{3,1,2,0:T(8,128)(2,1)}, u32[]{:S(2)}, u32[]{:S(2)}) collective-permute-start(bf16[2,8,128,128]{3,1,2,0:T(8,128)(2,1)} %copy.169), channel_id=1, source_target_pairs={{2,0},{4,2},{6,4},{8,6},{10,8},{12,10},{14,12},{0,14},{3,1},{5,3},... | collective-permute-start | bytes 1572872 | tf_op jit(solution)/shard_map/while/body/eval_jaxpr/ppermute | solution.py:18
  13.4 19.1 %collective-permute-start.5 = (bf16[2,8]{1,0:T(2,128)(2,1)S(1)}, bf16[2,8]{1,0:T(2,128)(2,1)S(1)}, u32[]{:S(2)}, u32[]{:S(2)}) collective-permute-start(bf16[2,8]{1,0:T(2,128)(2,1)S(1)} %copy.170), channel_id=1, source_target_pairs={{2,0},{4,2},{6,4},{8,6},{10,8},{12,10},{14,12},{0,14},{3,1},{5,3},... | collective-permute-start | bytes 104 | tf_op jit(solution)/shard_map/while/body/eval_jaxpr/ppermute | solution.py:18
  42.3 16.3 %collective-permute-start = (bf16[16,128,128]{2,0,1:T(8,128)(2,1)}, bf16[16,128,128]{2,0,1:T(8,128)(2,1)}, u32[]{:S(2)}, u32[]{:S(2)}) collective-permute-start(bf16[16,128,128]{2,0,1:T(8,128)(2,1)} %get-tuple-element.443), channel_id=1, source_target_pairs={{16,0},{32,16},{48,32},{64,48},{80,64},{96,80},{112,96},{128,112},... | collective-permute-start | bytes 1572872 | tf_op jit(solution)/shard_map/while/body/eval_jaxpr/ppermute | solution.py:18
  42.3 16.1 %collective-permute-start.2 = (bf16[16]{0:T(256)(128)(2,1)S(1)}, bf16[16]{0:T(256)(128)(2,1)S(1)}, u32[]{:S(2)}, u32[]{:S(2)}) collective-permute-start(bf16[16]{0:T(256)(128)(2,1)S(1)} %get-tuple-element.444), channel_id=1, source_target_pairs={{16,0},{32,16},{48,32},{64,48},{80,64},{96,80},{112,96},{128,112},... | collective-permute-start | bytes 104 | tf_op jit(solution)/shard_map/while/body/eval_jaxpr/ppermute | solution.py:18
  44.9 22.2 %collective-permute-start.4 = (bf16[2,8,128,128]{3,1,2,0:T(8,128)(2,1)}, bf16[2,8,128,128]{3,1,2,0:T(8,128)(2,1)}, u32[]{:S(2)}, u32[]{:S(2)}) collective-permute-start(bf16[2,8,128,128]{3,1,2,0:T(8,128)(2,1)} %copy.169), channel_id=1, source_target_pairs={{2,0},{4,2},{6,4},{8,6},{10,8},{12,10},{14,12},{0,14},{3,1},{5,3},... | collective-permute-start | bytes 1572872 | tf_op jit(solution)/shard_map/while/body/eval_jaxpr/ppermute | solution.py:18
  48.0 19.1 %collective-permute-start.5 = (bf16[2,8]{1,0:T(2,128)(2,1)S(1)}, bf16[2,8]{1,0:T(2,128)(2,1)S(1)}, u32[]{:S(2)}, u32[]{:S(2)}) collective-permute-start(bf16[2,8]{1,0:T(2,128)(2,1)S(1)} %copy.170), channel_id=1, source_target_pairs={{2,0},{4,2},{6,4},{8,6},{10,8},{12,10},{14,12},{0,14},{3,1},{5,3},... | collective-permute-start | bytes 104 | tf_op jit(solution)/shard_map/while/body/eval_jaxpr/ppermute | solution.py:18
  77.5 20.2 %collective-permute-start.4 = (bf16[2,8,128,128]{3,1,2,0:T(8,128)(2,1)}, bf16[2,8,128,128]{3,1,2,0:T(8,128)(2,1)}, u32[]{:S(2)}, u32[]{:S(2)}) collective-permute-start(bf16[2,8,128,128]{3,1,2,0:T(8,128)(2,1)} %copy.169), channel_id=1, source_target_pairs={{2,0},{4,2},{6,4},{8,6},{10,8},{12,10},{14,12},{0,14},{3,1},{5,3},... | collective-permute-start | bytes 1572872 | tf_op jit(solution)/shard_map/while/body/eval_jaxpr/ppermute | solution.py:18
  80.3 17.2 %collective-permute-start.5 = (bf16[2,8]{1,0:T(2,128)(2,1)S(1)}, bf16[2,8]{1,0:T(2,128)(2,1)S(1)}, u32[]{:S(2)}, u32[]{:S(2)}) collective-permute-start(bf16[2,8]{1,0:T(2,128)(2,1)S(1)} %copy.170), channel_id=1, source_target_pairs={{2,0},{4,2},{6,4},{8,6},{10,8},{12,10},{14,12},{0,14},{3,1},{5,3},... | collective-permute-start | bytes 104 | tf_op jit(solution)/shard_map/while/body/eval_jaxpr/ppermute | solution.py:18
  111.2 18.9 %collective-permute-start.4 = (bf16[2,8,128,128]{3,1,2,0:T(8,128)(2,1)}, bf16[2,8,128,128]{3,1,2,0:T(8,128)(2,1)}, u32[]{:S(2)}, u32[]{:S(2)}) collective-permute-start(bf16[2,8,128,128]{3,1,2,0:T(8,128)(2,1)} %copy.169), channel_id=1, source_target_pairs={{2,0},{4,2},{6,4},{8,6},{10,8},{12,10},{14,12},{0,14},{3,1},{5,3},... | collective-permute-start | bytes 1572872 | tf_op jit(solution)/shard_map/while/body/eval_jaxpr/ppermute | solution.py:18
  111.2 18.8 %collective-permute-start.5 = (bf16[2,8]{1,0:T(2,128)(2,1)S(1)}, bf16[2,8]{1,0:T(2,128)(2,1)S(1)}, u32[]{:S(2)}, u32[]{:S(2)}) collective-permute-start(bf16[2,8]{1,0:T(2,128)(2,1)S(1)} %copy.170), channel_id=1, source_target_pairs={{2,0},{4,2},{6,4},{8,6},{10,8},{12,10},{14,12},{0,14},{3,1},{5,3},... | collective-permute-start | bytes 104 | tf_op jit(solution)/shard_map/while/body/eval_jaxpr/ppermute | solution.py:18
  138.6 19.0 %collective-permute-start = (bf16[16,128,128]{2,0,1:T(8,128)(2,1)}, bf16[16,128,128]{2,0,1:T(8,128)(2,1)}, u32[]{:S(2)}, u32[]{:S(2)}) collective-permute-start(bf16[16,128,128]{2,0,1:T(8,128)(2,1)} %get-tuple-element.443), channel_id=1, source_target_pairs={{16,0},{32,16},{48,32},{64,48},{80,64},{96,80},{112,96},{128,112},... | collective-permute-start | bytes 1572872 | tf_op jit(solution)/shard_map/while/body/eval_jaxpr/ppermute | solution.py:18
  141.1 16.4 %collective-permute-start.2 = (bf16[16]{0:T(256)(128)(2,1)S(1)}, bf16[16]{0:T(256)(128)(2,1)S(1)}, u32[]{:S(2)}, u32[]{:S(2)}) collective-permute-start(bf16[16]{0:T(256)(128)(2,1)S(1)} %get-tuple-element.444), channel_id=1, source_target_pairs={{16,0},{32,16},{48,32},{64,48},{80,64},{96,80},{112,96},{128,112},... | collective-permute-start | bytes 104 | tf_op jit(solution)/shard_map/while/body/eval_jaxpr/ppermute | solution.py:18
  143.0 21.6 %collective-permute-start.4 = (bf16[2,8,128,128]{3,1,2,0:T(8,128)(2,1)}, bf16[2,8,128,128]{3,1,2,0:T(8,128)(2,1)}, u32[]{:S(2)}, u32[]{:S(2)}) collective-permute-start(bf16[2,8,128,128]{3,1,2,0:T(8,128)(2,1)} %copy.169), channel_id=1, source_target_pairs={{2,0},{4,2},{6,4},{8,6},{10,8},{12,10},{14,12},{0,14},{3,1},{5,3},... | collective-permute-start | bytes 1572872 | tf_op jit(solution)/shard_map/while/body/eval_jaxpr/ppermute | solution.py:18
  147.1 16.6 %collective-permute-start.5 = (bf16[2,8]{1,0:T(2,128)(2,1)S(1)}, bf16[2,8]{1,0:T(2,128)(2,1)S(1)}, u32[]{:S(2)}, u32[]{:S(2)}) collective-permute-start(bf16[2,8]{1,0:T(2,128)(2,1)S(1)} %copy.170), channel_id=1, source_target_pairs={{2,0},{4,2},{6,4},{8,6},{10,8},{12,10},{14,12},{0,14},{3,1},{5,3},... | collective-permute-start | bytes 104 | tf_op jit(solution)/shard_map/while/body/eval_jaxpr/ppermute | solution.py:18
  174.3 19.0 %collective-permute-start = (bf16[16,128,128]{2,0,1:T(8,128)(2,1)}, bf16[16,128,128]{2,0,1:T(8,128)(2,1)}, u32[]{:S(2)}, u32[]{:S(2)}) collective-permute-start(bf16[16,128,128]{2,0,1:T(8,128)(2,1)} %get-tuple-element.443), channel_id=1, source_target_pairs={{16,0},{32,16},{48,32},{64,48},{80,64},{96,80},{112,96},{128,112},... | collective-permute-start | bytes 1572872 | tf_op jit(solution)/shard_map/while/body/eval_jaxpr/ppermute | solution.py:18
  174.3 18.9 %collective-permute-start.2 = (bf16[16]{0:T(256)(128)(2,1)S(1)}, bf16[16]{0:T(256)(128)(2,1)S(1)}, u32[]{:S(2)}, u32[]{:S(2)}) collective-permute-start(bf16[16]{0:T(256)(128)(2,1)S(1)} %get-tuple-element.444), channel_id=1, source_target_pairs={{16,0},{32,16},{48,32},{64,48},{80,64},{96,80},{112,96},{128,112},... | collective-permute-start | bytes 104 | tf_op jit(solution)/shard_map/while/body/eval_jaxpr/ppermute | solution.py:18
  176.2 24.1 %collective-permute-start.4 = (bf16[2,8,128,128]{3,1,2,0:T(8,128)(2,1)}, bf16[2,8,128,128]{3,1,2,0:T(8,128)(2,1)}, u32[]{:S(2)}, u32[]{:S(2)}) collective-permute-start(bf16[2,8,128,128]{3,1,2,0:T(8,128)(2,1)} %copy.169), channel_id=1, source_target_pairs={{2,0},{4,2},{6,4},{8,6},{10,8},{12,10},{14,12},{0,14},{3,1},{5,3},... | collective-permute-start | bytes 1572872 | tf_op jit(solution)/shard_map/while/body/eval_jaxpr/ppermute | solution.py:18
  182.8 16.6 %collective-permute-start.5 = (bf16[2,8]{1,0:T(2,128)(2,1)S(1)}, bf16[2,8]{1,0:T(2,128)(2,1)S(1)}, u32[]{:S(2)}, u32[]{:S(2)}) collective-permute-start(bf16[2,8]{1,0:T(2,128)(2,1)S(1)} %copy.170), channel_id=1, source_target_pairs={{2,0},{4,2},{6,4},{8,6},{10,8},{12,10},{14,12},{0,14},{3,1},{5,3},... | collective-permute-start | bytes 104 | tf_op jit(solution)/shard_map/while/body/eval_jaxpr/ppermute | solution.py:18
  210.1 17.9 %collective-permute-start = (bf16[16,128,128]{2,0,1:T(8,128)(2,1)}, bf16[16,128,128]{2,0,1:T(8,128)(2,1)}, u32[]{:S(2)}, u32[]{:S(2)}) collective-permute-start(bf16[16,128,128]{2,0,1:T(8,128)(2,1)} %get-tuple-element.443), channel_id=1, source_target_pairs={{16,0},{32,16},{48,32},{64,48},{80,64},{96,80},{112,96},{128,112},... | collective-permute-start | bytes 1572872 | tf_op jit(solution)/shard_map/while/body/eval_jaxpr/ppermute | solution.py:18
  210.1 17.7 %collective-permute-start.2 = (bf16[16]{0:T(256)(128)(2,1)S(1)}, bf16[16]{0:T(256)(128)(2,1)S(1)}, u32[]{:S(2)}, u32[]{:S(2)}) collective-permute-start(bf16[16]{0:T(256)(128)(2,1)S(1)} %get-tuple-element.444), channel_id=1, source_target_pairs={{16,0},{32,16},{48,32},{64,48},{80,64},{96,80},{112,96},{128,112},... | collective-permute-start | bytes 104 | tf_op jit(solution)/shard_map/while/body/eval_jaxpr/ppermute | solution.py:18
  211.9 22.8 %collective-permute-start.4 = (bf16[2,8,128,128]{3,1,2,0:T(8,128)(2,1)}, bf16[2,8,128,128]{3,1,2,0:T(8,128)(2,1)}, u32[]{:S(2)}, u32[]{:S(2)}) collective-permute-start(bf16[2,8,128,128]{3,1,2,0:T(8,128)(2,1)} %copy.169), channel_id=1, source_target_pairs={{2,0},{4,2},{6,4},{8,6},{10,8},{12,10},{14,12},{0,14},{3,1},{5,3},... | collective-permute-start | bytes 1572872 | tf_op jit(solution)/shard_map/while/body/eval_jaxpr/ppermute | solution.py:18
  217.4 16.6 %collective-permute-start.5 = (bf16[2,8]{1,0:T(2,128)(2,1)S(1)}, bf16[2,8]{1,0:T(2,128)(2,1)S(1)}, u32[]{:S(2)}, u32[]{:S(2)}) collective-permute-start(bf16[2,8]{1,0:T(2,128)(2,1)S(1)} %copy.170), channel_id=1, source_target_pairs={{2,0},{4,2},{6,4},{8,6},{10,8},{12,10},{14,12},{0,14},{3,1},{5,3},... | collective-permute-start | bytes 104 | tf_op jit(solution)/shard_map/while/body/eval_jaxpr/ppermute | solution.py:18
  (27 other events, 263.9 us)
where the time goes:
time: 267 us; the launch traced here: 265 us
  waiting for transfers between devices  74.8 us (28%)
  matrix products  62.5 us (23%)
  starting transfers between devices  53 us (20%)
  local copies, waits for them, and re-layouts  48.9 us (18%)
  other arithmetic  19.9 us (7%)
  loops' own time  5.47 us (2%)
    ppermute x44, waiting for transfers between devices, from_behind(): return lax.ppermute(block, axis, route)  74.8 us
    ppermute x44, starting transfers between devices, from_behind(): return lax.ppermute(block, axis, route)  53 us
    dot_general x32, matrix products, dense_panel(): jnp.einsum('sp,sxy->pxy', picker, blocks, preferred_element_type=jnp.floa...  43.9 us
    dot_general x16, matrix products, advance(): jnp.dot(left_dense, right_dense, preferred_element_type=jnp.float32)  18.6 us
    add x7, other arithmetic, advance(): running = running + product.reshape(RB * block_edge, col_span * block_edge)  18.4 us
    dot_general x32, local copies, waits for them, and re-layouts, advance(): jnp.dot(left_dense, right_dense, preferred_element_type=jnp.float32)  14.2 us
    while x28, local copies, waits for them, and re-layouts  13.6 us
    mul x16, local copies, waits for them, and re-layouts, advance(): product.reshape(RB, block_edge, col_span, block_edge)  6.29 us
  transfers between devices with their start and end apart: 44, of which 12 were waited for; matrix products, arithmetic and copies ran while one was open for 46% of the time, Pallas kernels for 0%

commit v1 on v0

v1 whole, which is shorter than its diff:
```python
import jax
import jax.numpy as jnp
from jax import lax
from jax.experimental import pallas as pl
from jax.experimental.pallas import tpu as pltpu
from jax.sharding import PartitionSpec as P

BLK = 128
RB = 8
CB = 4
KP = 4
SIDE = 4
META = 16
HALF = 8
ROWS = HALF * BLK + META
BZERO = 16 * ROWS
STEPS = (1, -1, 2)


def with_meta(blocks, position):
    lanes = jnp.pad(position.astype(jnp.bfloat16), (0, BLK - position.shape[0]))
    meta = jnp.broadcast_to(lanes[None, :], (META, BLK))
    return jnp.concatenate([blocks.reshape(HALF * BLK, BLK), meta], axis=0)


def move_a(value, distance, phase):
    pairs = []
    for x in range(SIDE):
        for y in range(SIDE):
            for core in range(2):
                along_y = (core == 0) == (phase == 0)
                tx = x if along_y else (x + distance) % SIDE
                ty = (y + distance) % SIDE if along_y else y
                pairs.append(((x * SIDE + y) * 2 + core, (tx * SIDE + ty) * 2 + core))
    return lax.ppermute(value, ("row", "layer"), pairs)


def move_b(value, depth):
    pairs = []
    for z in range(depth):
        pairs.append((z * 2, ((z + 1) % depth) * 2))
        pairs.append((z * 2 + 1, ((z - 1) % depth) * 2 + 1))
    return lax.ppermute(value, ("col", "layer"), pairs)


def swap(value):
    return lax.ppermute(value, "layer", [(0, 1), (1, 0)])


def delta(index):
    return jnp.where(index == 0, 0, jnp.where(index == 1, SIDE - 1, index - 1))


def multiply(place, keep, *refs):
    a_refs, b_refs = refs[:4], refs[4:13]
    send, own, av, bv, acc, meta_v, meta_s, table, sem, meta_sem = refs[13:]
    x, y, z, core = place[0], place[1], place[2], place[3]
    copies = []
    for g in range(4):
        for m in range(4):
            p = 4 * g + m
            copies.append(
                pltpu.make_async_copy(a_refs[g].at[m], av.at[pl.ds(p * ROWS, ROWS)], sem.at[p])
            )
    copies.append(pltpu.make_async_copy(b_refs[0].at[0], bv.at[pl.ds(0, ROWS)], sem.at[16]))
    copies.append(pltpu.make_async_copy(b_refs[0].at[1], bv.at[pl.ds(ROWS, ROWS)], sem.at[17]))
    for t in range(1, 4):
        up = jnp.where(core == 0, 8 - t, t)
        down = jnp.where(core == 0, t, 8 - t)
        for i in range(2):
            copies.append(
                pltpu.make_async_copy(
                    b_refs[t].at[i],
                    bv.at[pl.ds(pl.multiple_of((up * 2 + i) * ROWS, META), ROWS)],
                    sem.at[16 + 4 * t - 2 + i],
                )
            )
            copies.append(
                pltpu.make_async_copy(
                    b_refs[3 + t].at[i],
                    bv.at[pl.ds(pl.multiple_of((down * 2 + i) * ROWS, META), ROWS)],
                    sem.at[16 + 4 * t + i],
                )
            )
    copies.append(
        pltpu.make_async_copy(
            b_refs[7].at[0], bv.at[pl.ds(pl.multiple_of((8 + core) * ROWS, META), ROWS)], sem.at[30]
        )
    )
    copies.append(
        pltpu.make_async_copy(
            b_refs[8].at[0], bv.at[pl.ds(pl.multiple_of((9 - core) * ROWS, META), ROWS)], sem.at[31]
        )
    )
    for copy in copies:
        copy.start()
    acc[...] = jnp.zeros_like(acc)
    bv[BZERO : BZERO + BLK, :] = jnp.zeros((BLK, BLK), jnp.bfloat16)
    for copy in copies:
        copy.wait()
    for p in range(16):
        for held, at in ((av, p), (bv, 16 + p)):
            tile = held[p * ROWS + HALF * BLK : (p + 1) * ROWS, :]
            meta_v[at : at + 1, :] = tile.astype(jnp.float32)[0:1, :].astype(jnp.int32)
    to_scalars = pltpu.make_async_copy(meta_v, meta_s, meta_sem)
    to_scalars.start()
    to_scalars.wait()

    def panel(p, carry):
        g, m = p // 4, p % 4
        first, second = delta(g), delta(m)
        px = (x + jnp.where(core == 0, first, second)) % SIDE
        py = (y + jnp.where(core == 0, second, first)) % SIDE
        k = (px * SIDE + py + 2 * z) % 16
        q = (k - (x * SIDE + y) + 16) % 16
        where_b = ((q // 2 - z + 8) % 8) * 2 + q % 2
        for i in range(KP * CB):
            table[i] = BZERO
        for t in range(HALF):
            table[meta_s[16 + where_b, t]] = where_b * ROWS + t * BLK
        for s in range(HALF):
            number = meta_s[p, s]
            live = number < RB * KP
            number = jnp.where(live, number, 0)
            r, c = number // KP, number % KP
            left = av[pl.ds(pl.multiple_of(p * ROWS + s * BLK, META), BLK), :]
            right = jnp.concatenate(
                [
                    bv[pl.ds(pl.multiple_of(table[c * CB + n], META), BLK), :]
                    for n in range(CB)
                ],
                axis=1,
            )
            product = jnp.dot(left, right, preferred_element_type=jnp.float32)
            for n in range(CB):
                kept = jnp.where(live, keep[r, k * CB + n], 0).astype(jnp.float32)
                cols = slice(n * BLK, (n + 1) * BLK)
                acc[r, :, cols] += product[:, cols] * kept
        return carry

    lax.fori_loop(0, 16, panel, 0)

    @pl.when(core == 0)
    def _():
        own[...] = acc[:, :, : 2 * BLK]
        send[...] = acc[:, :, 2 * BLK :]

    @pl.when(core != 0)
    def _():
        own[...] = acc[:, :, 2 * BLK :]
        send[...] = acc[:, :, : 2 * BLK]


def partial_sums(place, keep, a_parts, b_parts):
    vmem = pl.BlockSpec(memory_space=pltpu.VMEM)
    smem = pl.BlockSpec(memory_space=pltpu.SMEM)
    anywhere = pl.BlockSpec(memory_space=pl.ANY)
    half = jax.ShapeDtypeStruct((RB, BLK, 2 * BLK), jnp.float32)
    return pl.pallas_call(
        multiply,
        out_shape=(half, half),
        in_specs=[smem, smem] + [anywhere] * 13,
        out_specs=(vmem, vmem),
        scratch_shapes=[
            pltpu.VMEM((16 * ROWS, BLK), jnp.bfloat16),
            pltpu.VMEM((16 * ROWS + BLK, BLK), jnp.bfloat16),
            pltpu.VMEM((RB, BLK, CB * BLK), jnp.float32),
            pltpu.VMEM((32, BLK), jnp.int32),
            pltpu.SMEM((32, BLK), jnp.int32),
            pltpu.SMEM((32,), jnp.int32),
            pltpu.SemaphoreType.DMA((32,)),
            pltpu.SemaphoreType.DMA,
        ],
        compiler_params=pltpu.CompilerParams(vmem_limit_bytes=32 * 1024 * 1024),
    )(place, keep, *a_parts, *b_parts)


def body(a_blocks, a_rows, a_cols, b_blocks, b_rows, b_cols, prod_keep, res_keep):
    depth = lax.axis_size("col")
    row = lax.axis_index("row")
    z = lax.axis_index("col")
    core = lax.axis_index("layer")
    place = jnp.stack([row // SIDE, row % SIDE, z, core]).astype(jnp.int32)

    a_half = lax.dynamic_index_in_dim(
        a_blocks[0, 0].reshape(HALF, 2, BLK, BLK), core, 1, keepdims=False
    )
    a_number = (a_rows[0, 0] * KP + a_cols[0, 0]).reshape(HALF, 2)
    a_number = lax.dynamic_index_in_dim(a_number, core, 1, keepdims=False)
    a_mine = with_meta(a_half, a_number)
    b_number = b_rows[:, 0] * CB + b_cols[:, 0]
    b_mine = jnp.stack([with_meta(b_blocks[i, 0], b_number[i]) for i in range(2)])

    b_from = [b_mine]
    for _ in range(3):
        b_from.append(move_b(b_from[-1], depth))
    last = move_b(lax.dynamic_slice_in_dim(b_from[3], core, 1, 0), depth)
    b_theirs = [swap(part) for part in b_from[1:]]
    last_theirs = swap(last)

    a_own = jnp.stack([a_mine] + [move_a(a_mine, d, 0) for d in STEPS])
    a_parts = [a_own] + [move_a(a_own, d, 1) for d in STEPS]

    send, own = partial_sums(
        place,
        prod_keep.reshape(RB, 16 * CB),
        a_parts,
        b_from + b_theirs + [last, last_theirs],
    )
    total = own + swap(send)
    total = total.reshape(RB, BLK, 2, BLK) * res_keep.astype(jnp.float32)[:, None, :, None]
    return total.reshape(RB * BLK, 2 * BLK).astype(jnp.bfloat16)


def solution(mesh):
    return jax.shard_map(
        body,
        mesh=mesh,
        in_specs=(
            P("col", "row", None, None, None),
            P("col", "row", None),
            P("col", "row", None),
            P("col", "row", None, None, None),
            P("col", "row", None),
            P("col", "row", None),
            P("col", None, "row"),
            P("col", ("row", "layer")),
        ),
        out_specs=P("col", ("row", "layer")),
        check_vma=False,
    )
```

time: 267 us -> 76.5 us (0.29)
  the two profiles are of different devices: /device:TPU:30 before, /device:TPU:1 now
where the time goes in v1:
time: 76.5 us; the launch traced here: 75.7 us
  starting transfers between devices  31.2 us (41%)
  waiting for transfers between devices  20.7 us (27%)
  Pallas kernels  13.1 us (17%)
  local copies, waits for them, and re-layouts  6.93 us (9%)
  other arithmetic  3.56 us (5%)
    ppermute x4, starting transfers between devices, move_b(): return lax.ppermute(value, ('col', 'layer'), pairs)  13.3 us
    pallas_call x1, Pallas kernels, partial_sums(): pl.pallas_call(multiply, out_shape=(half, half), in_specs=[smem, smem] +...  13.1 us
    ppermute x6, starting transfers between devices, move_a(): return lax.ppermute(value, ('row', 'layer'), pairs)  12.1 us
    ppermute x4, waiting for transfers between devices, move_b(): return lax.ppermute(value, ('col', 'layer'), pairs)  10.4 us
    ppermute x6, waiting for transfers between devices, move_a(): return lax.ppermute(value, ('row', 'layer'), pairs)  7.69 us
    ppermute x5, starting transfers between devices, swap(): return lax.ppermute(value, 'layer', [(0, 1), (1, 0)])  5.84 us
    unnamed x21, local copies, waits for them, and re-layouts  5.17 us
    ppermute x5, waiting for transfers between devices, swap(): return lax.ppermute(value, 'layer', [(0, 1), (1, 0)])  2.62 us
  transfers between devices with their start and end apart: 15, of which 8 were waited for; matrix products, arithmetic and copies ran while one was open for 1% of the time, Pallas kernels for 0%

profile of v1, /device:TPU:1, one launch (start us, length us, event | category | flops | bytes accessed | tf_op | source)
XLA Modules:
  0.0 75.7 jit_solution(3305677724981821839)
XLA Ops:
  0.0 1.1 %fusion.3 = (bf16[1,1,8,128,128]{4,3,2,1,0:T(8,128)(2,1)S(1)}, bf16[1,1,8,128,128]{4,3,2,1,0:T(8,128)(2,1)S(1)}) fusion(bf16[2,1,8,128,128]{4,3,2,1,0:T(8,128)(2,1)} %param.11), kind=kLoop, calls=%fused_computation.17 | loop fusion | bytes 1048576 | tf_op jit(solution)/shard_map/slice | solution.py:192
  2.0 6.5 %collective-permute-start.6 = (bf16[2,1040,128]{2,1,0:T(8,128)(2,1)S(1)}, bf16[2,1040,128]{2,1,0:T(8,128)(2,1)S(1)}, u32[]{:S(2)}, u32[]{:S(2)}) collective-permute-start(bf16[2,1040,128]{2,1,0:T(8,128)(2,1)S(1)} %pad_maximum_fusion.1.refs_4_), channel_id=1, source_target_pairs={{0,2},{1,15},{2,4},{3,1},{4,6},{5,3},{6,8},{7,5},{8,10},{9,7},{10,... | collective-permute-start | bytes 1597448 | tf_op jit(solution)/shard_map/ppermute | solution.py:43
  8.9 2.8 %collective-permute-start.2 = (bf16[1040,128]{1,0:T(8,128)(2,1)S(1)}, bf16[1040,128]{1,0:T(8,128)(2,1)S(1)}, u32[]{:S(2)}, u32[]{:S(2)}) collective-permute-start(bf16[1040,128]{1,0:T(8,128)(2,1)S(1)} %get-tuple-element.12), channel_id=1, source_target_pairs={{0,32},{1,129},{16,48},{17,145},{32,0},{33,161},{48,16},{49,177},{... | collective-permute-start | bytes 798728 | tf_op jit(solution)/shard_map/ppermute | solution.py:35
  12.1 2.4 %collective-permute-start.1 = (bf16[1040,128]{1,0:T(8,128)(2,1)S(1)}, bf16[1040,128]{1,0:T(8,128)(2,1)S(1)}, u32[]{:S(2)}, u32[]{:S(2)}) collective-permute-start(bf16[1040,128]{1,0:T(8,128)(2,1)S(1)} %get-tuple-element.12), channel_id=1, source_target_pairs={{0,48},{1,193},{16,0},{17,209},{32,16},{33,225},{48,32},{49,241},{... | collective-permute-start | bytes 798728 | tf_op jit(solution)/shard_map/ppermute | solution.py:35
  14.7 3.4 %collective-permute-start.7 = (bf16[2,1040,128]{2,1,0:T(8,128)(2,1)S(1)}, bf16[2,1040,128]{2,1,0:T(8,128)(2,1)}, u32[]{:S(2)}, u32[]{:S(2)}) collective-permute-start(bf16[2,1040,128]{2,1,0:T(8,128)(2,1)S(1)} %collective-permute-done.6.refs_5_), channel_id=1, source_target_pairs={{0,2},{1,15},{2,4},{3,1},{4,6},{5,3},{6,8},{7,5},{8,10},{9,7},{10,... | collective-permute-start | bytes 1597448 | tf_op jit(solution)/shard_map/ppermute | solution.py:43
  18.8 1.4 %collective-permute-start.3 = (bf16[4,1040,128]{2,1,0:T(8,128)(2,1)S(1)}, bf16[4,1040,128]{2,1,0:T(8,128)(2,1)S(1)}, u32[]{:S(2)}, u32[]{:S(2)}) collective-permute-start(bf16[4,1040,128]{2,1,0:T(8,128)(2,1)S(1)} %pad_maximum_fusion.refs_0_), channel_id=1, source_target_pairs={{0,64},{1,17},{16,80},{17,33},{32,96},{33,49},{48,112},{49,1},{64,... | collective-permute-start | bytes 3194888 | tf_op jit(solution)/shard_map/ppermute | solution.py:35
  20.2 4.1 %collective-permute-done.7.refs_6_ = bf16[2,1040,128]{2,1,0:T(8,128)(2,1)} collective-permute-done((bf16[2,1040,128]{2,1,0:T(8,128)(2,1)S(1)}, bf16[2,1040,128]{2,1,0:T(8,128)(2,1)}, u32[]{:S(2)}, u32[]{:S(2)}) %collective-permute-start.7) | collective-permute-done | bytes 532512 | tf_op jit(solution)/shard_map/ppermute | solution.py:43
  24.3 3.4 %collective-permute-start.8 = (bf16[2,1040,128]{2,1,0:T(8,128)(2,1)}, bf16[2,1040,128]{2,1,0:T(8,128)(2,1)S(1)}, u32[]{:S(2)}, u32[]{:S(2)}) collective-permute-start(bf16[2,1040,128]{2,1,0:T(8,128)(2,1)} %collective-permute-done.7.refs_6_), channel_id=1, source_target_pairs={{0,2},{1,15},{2,4},{3,1},{4,6},{5,3},{6,8},{7,5},{8,10},{9,7},{10,... | collective-permute-start | bytes 1597448 | tf_op jit(solution)/shard_map/ppermute | solution.py:43
  27.8 2.7 %collective-permute-start.4 = (bf16[4,1040,128]{2,1,0:T(8,128)(2,1)S(1)}, bf16[4,1040,128]{2,1,0:T(8,128)(2,1)}, u32[]{:S(2)}, u32[]{:S(2)}) collective-permute-start(bf16[4,1040,128]{2,1,0:T(8,128)(2,1)S(1)} %pad_maximum_fusion.refs_0_), channel_id=1, source_target_pairs={{0,192},{1,49},{16,208},{17,1},{32,224},{33,17},{48,240},{49,33},{... | collective-permute-start | bytes 3194888 | tf_op jit(solution)/shard_map/ppermute | solution.py:35
  30.5 2.5 %collective-permute-start.5 = (bf16[4,1040,128]{2,1,0:T(8,128)(2,1)S(1)}, bf16[4,1040,128]{2,1,0:T(8,128)(2,1)}, u32[]{:S(2)}, u32[]{:S(2)}) collective-permute-start(bf16[4,1040,128]{2,1,0:T(8,128)(2,1)S(1)} %pad_maximum_fusion.refs_0_), channel_id=1, source_target_pairs={{0,128},{1,33},{16,144},{17,49},{32,160},{33,1},{48,176},{49,17},{... | collective-permute-start | bytes 3194888 | tf_op jit(solution)/shard_map/ppermute | solution.py:35
  33.0 1.3 %collective-permute-done.8.refs_7_ = bf16[2,1040,128]{2,1,0:T(8,128)(2,1)S(1)} collective-permute-done((bf16[2,1040,128]{2,1,0:T(8,128)(2,1)}, bf16[2,1040,128]{2,1,0:T(8,128)(2,1)S(1)}, u32[]{:S(2)}, u32[]{:S(2)}) %collective-permute-start.8) | collective-permute-done | bytes 532512 | tf_op jit(solution)/shard_map/ppermute | solution.py:43
  34.3 3.7 %collective-permute-start.10 = (bf16[2,1040,128]{2,1,0:T(8,128)(2,1)}, bf16[2,1040,128]{2,1,0:T(8,128)(2,1)}, u32[]{:S(2)}, u32[]{:S(2)}) collective-permute-start(bf16[2,1040,128]{2,1,0:T(8,128)(2,1)} %collective-permute-done.7.refs_6_), channel_id=1, source_target_pairs={{0,1},{1,0},{2,3},{3,2},{4,5},{5,4},{6,7},{7,6},{8,9},{9,8},{10,11... | collective-permute-start | bytes 1597448 | tf_op jit(solution)/shard_map/ppermute | solution.py:47
  38.0 0.8 %copy-done.4 = bf16[2,1040,128]{2,1,0:T(8,128)(2,1)} copy-done((bf16[2,1040,128]{2,1,0:T(8,128)(2,1)}, bf16[2,1040,128]{2,1,0:T(8,128)(2,1)S(1)}, u32[]{:S(2)}) %copy-start.4) | copy-done | bytes 532504
  38.9 1.0 %copy-done.1 = bf16[4,1040,128]{2,1,0:T(8,128)(2,1)} copy-done((bf16[4,1040,128]{2,1,0:T(8,128)(2,1)}, bf16[4,1040,128]{2,1,0:T(8,128)(2,1)S(1)}, u32[]{:S(2)}) %copy-start.1) | copy-done | bytes 1064984
  39.9 4.7 %collective-permute-done.12.refs_11_ = bf16[1,1040,128]{2,1,0:T(8,128)(2,1)S(1)} collective-permute-done((bf16[1,1040,128]{2,1,0:T(8,128)(2,1)S(1)}, bf16[1,1040,128]{2,1,0:T(8,128)(2,1)S(1)}, u32[]{:S(2)}, u32[]{:S(2)}) %collective-permute-start.12) | collective-permute-done | bytes 266272 | tf_op jit(solution)/shard_map/ppermute | solution.py:43
  44.5 2.0 %collective-permute-start.13 = (bf16[1,1040,128]{2,1,0:T(8,128)(2,1)S(1)}, bf16[1,1040,128]{2,1,0:T(8,128)(2,1)}, u32[]{:S(2)}, u32[]{:S(2)}) collective-permute-start(bf16[1,1040,128]{2,1,0:T(8,128)(2,1)S(1)} %collective-permute-done.12.refs_11_), channel_id=1, source_target_pairs={{0,1},{1,0},{2,3},{3,2},{4,5},{5,4},{6,7},{7,6},{8,9},{9,8},{10,11... | collective-permute-start | bytes 798728 | tf_op jit(solution)/shard_map/ppermute | solution.py:47
  46.7 7.1 %collective-permute-done.4.refs_2_ = bf16[4,1040,128]{2,1,0:T(8,128)(2,1)} collective-permute-done((bf16[4,1040,128]{2,1,0:T(8,128)(2,1)S(1)}, bf16[4,1040,128]{2,1,0:T(8,128)(2,1)}, u32[]{:S(2)}, u32[]{:S(2)}) %collective-permute-start.4) | collective-permute-done | bytes 1064992 | tf_op jit(solution)/shard_map/ppermute | solution.py:35
  53.9 1.2 %copy-done.2 = bf16[4,1040,128]{2,1,0:T(8,128)(2,1)S(1)} copy-done((bf16[4,1040,128]{2,1,0:T(8,128)(2,1)S(1)}, bf16[4,1040,128]{2,1,0:T(8,128)(2,1)}, u32[]{:S(2)}) %copy-start.2) | copy-done | bytes 1064984
  55.1 1.0 %copy-done.5 = bf16[2,1040,128]{2,1,0:T(8,128)(2,1)S(1)} copy-done((bf16[2,1040,128]{2,1,0:T(8,128)(2,1)S(1)}, bf16[2,1040,128]{2,1,0:T(8,128)(2,1)}, u32[]{:S(2)}) %copy-start.5) | copy-done | bytes 532504
  56.1 13.1 %shard_map.82 = (f32[8,128,256]{2,1,0:T(8,128)}, f32[8,128,256]{2,1,0:T(8,128)S(1)}) custom-call(s32[4]{0:T(128)S(1)} %pad_add_fusion.place, s32[8,64]{1,0:T(8,128)S(1)} %copy.14.keep, bf16[4,1040,128]{2,1,0:T(8,128)(2,1)S(1)} %pad_maximum_fusion.refs_0_, bf16[4,1040,128]{2,1,0:T(8,128)(2,1)S(1)} %copy-done.2, ...), custom_call_target="tpu_custom_call" | custom-call | tf_op jit(solution)/shard_map/pallas_call | solution.py:159
  69.2 1.0 %copy-done.3 = f32[8,128,256]{2,1,0:T(8,128)} copy-done((f32[8,128,256]{2,1,0:T(8,128)}, f32[8,128,256]{2,1,0:T(8,128)S(1)}, u32[]{:S(2)}) %copy-start.3) | copy-done | bytes 1048600
  70.5 2.6 %collective-permute-done.14 = f32[8,128,256]{2,1,0:T(8,128)S(1)} collective-permute-done((f32[8,128,256]{2,1,0:T(8,128)}, f32[8,128,256]{2,1,0:T(8,128)S(1)}, u32[]{:S(2)}, u32[]{:S(2)}) %collective-permute-start.14) | collective-permute-done | bytes 1048608 | tf_op jit(solution)/shard_map/ppermute | solution.py:47
  73.1 1.4 %add.37 = f32[8,128,256]{2,1,0:T(8,128)S(1)} add(f32[8,128,256]{2,1,0:T(8,128)} %copy-done.3, f32[8,128,256]{2,1,0:T(8,128)S(1)} %collective-permute-done.14) | non-fusion elementwise | flops 262144 | bytes 3145728 | tf_op jit(solution)/shard_map/add | solution.py:210
  74.8 0.9 %fusion = bf16[1024,256]{1,0:T(8,128)(2,1)} fusion(f32[128,8,2,128]{3,2,1,0:T(2,128)S(1)} %bitcast.33, f32[8,128,256]{2,1,0:T(8,128)S(1)} %add.37), kind=kLoop, calls=%fused_computation.2 | loop fusion | flops 524288 | bytes 2621440 | tf_op jit(solution)/shard_map/convert_element_type | solution.py:212
  (53 shorter events, 3.4 us)
Async XLA Ops:
  0.0 8.5 %copy-start = (bf16[1,1,16,128,128]{4,3,2,1,0:T(8,128)(2,1)S(1)}, bf16[1,1,16,128,128]{4,3,2,1,0:T(8,128)(2,1)}, u32[]{:S(2)}) copy-start(bf16[1,1,16,128,128]{4,3,2,1,0:T(8,128)(2,1)} %param.8) | copy-start | bytes 1572868
  1.9 6.6 %copy-start.8 = (s32[1,1,16]{2,1,0:T(1,128)S(1)}, s32[1,1,16]{2,1,0:T(1,128)}, u32[]{:S(2)}) copy-start(s32[1,1,16]{2,1,0:T(1,128)} %param.10) | copy-start | bytes 196
  2.0 6.6 %copy-start.9 = (s32[1,1,16]{2,1,0:T(1,128)S(1)}, s32[1,1,16]{2,1,0:T(1,128)}, u32[]{:S(2)}) copy-start(s32[1,1,16]{2,1,0:T(1,128)} %param.9) | copy-start | bytes 196
  2.0 12.7 %collective-permute-start.6 = (bf16[2,1040,128]{2,1,0:T(8,128)(2,1)S(1)}, bf16[2,1040,128]{2,1,0:T(8,128)(2,1)S(1)}, u32[]{:S(2)}, u32[]{:S(2)}) collective-permute-start(bf16[2,1040,128]{2,1,0:T(8,128)(2,1)S(1)} %pad_maximum_fusion.1.refs_4_), channel_id=1, source_target_pairs={{0,2},{1,15},{2,4},{3,1},{4,6},{5,3},{6,8},{7,5},{8,10},{9,7},{10,... | collective-permute-start | bytes 1597448 | tf_op jit(solution)/shard_map/ppermute | solution.py:43
  8.9 9.2 %collective-permute-start.2 = (bf16[1040,128]{1,0:T(8,128)(2,1)S(1)}, bf16[1040,128]{1,0:T(8,128)(2,1)S(1)}, u32[]{:S(2)}, u32[]{:S(2)}) collective-permute-start(bf16[1040,128]{1,0:T(8,128)(2,1)S(1)} %get-tuple-element.12), channel_id=1, source_target_pairs={{0,32},{1,129},{16,48},{17,145},{32,0},{33,161},{48,16},{49,177},{... | collective-permute-start | bytes 798728 | tf_op jit(solution)/shard_map/ppermute | solution.py:35
  11.7 6.9 %collective-permute-start = (bf16[1040,128]{1,0:T(8,128)(2,1)S(1)}, bf16[1040,128]{1,0:T(8,128)(2,1)S(1)}, u32[]{:S(2)}, u32[]{:S(2)}) collective-permute-start(bf16[1040,128]{1,0:T(8,128)(2,1)S(1)} %get-tuple-element.12), channel_id=1, source_target_pairs={{0,16},{1,65},{16,32},{17,81},{32,48},{33,97},{48,0},{49,113},{64,... | collective-permute-start | bytes 798728 | tf_op jit(solution)/shard_map/ppermute | solution.py:35
  12.1 6.7 %collective-permute-start.1 = (bf16[1040,128]{1,0:T(8,128)(2,1)S(1)}, bf16[1040,128]{1,0:T(8,128)(2,1)S(1)}, u32[]{:S(2)}, u32[]{:S(2)}) collective-permute-start(bf16[1040,128]{1,0:T(8,128)(2,1)S(1)} %get-tuple-element.12), channel_id=1, source_target_pairs={{0,48},{1,193},{16,0},{17,209},{32,16},{33,225},{48,32},{49,241},{... | collective-permute-start | bytes 798728 | tf_op jit(solution)/shard_map/ppermute | solution.py:35
  14.7 9.6 %collective-permute-start.7 = (bf16[2,1040,128]{2,1,0:T(8,128)(2,1)S(1)}, bf16[2,1040,128]{2,1,0:T(8,128)(2,1)}, u32[]{:S(2)}, u32[]{:S(2)}) collective-permute-start(bf16[2,1040,128]{2,1,0:T(8,128)(2,1)S(1)} %collective-permute-done.6.refs_5_), channel_id=1, source_target_pairs={{0,2},{1,15},{2,4},{3,1},{4,6},{5,3},{6,8},{7,5},{8,10},{9,7},{10,... | collective-permute-start | bytes 1597448 | tf_op jit(solution)/shard_map/ppermute | solution.py:43
  18.7 27.8 %copy-start.6 = (s32[8,16,4]{1,2,0:T(4,128)S(1)}, s32[8,16,4]{1,2,0:T(4,128)}, u32[]{:S(2)}) copy-start(s32[8,16,4]{1,2,0:T(4,128)} %param.14) | copy-start | bytes 6148
  18.8 20.0 %collective-permute-start.3 = (bf16[4,1040,128]{2,1,0:T(8,128)(2,1)S(1)}, bf16[4,1040,128]{2,1,0:T(8,128)(2,1)S(1)}, u32[]{:S(2)}, u32[]{:S(2)}) collective-permute-start(bf16[4,1040,128]{2,1,0:T(8,128)(2,1)S(1)} %pad_maximum_fusion.refs_0_), channel_id=1, source_target_pairs={{0,64},{1,17},{16,80},{17,33},{32,96},{33,49},{48,112},{49,1},{64,... | collective-permute-start | bytes 3194888 | tf_op jit(solution)/shard_map/ppermute | solution.py:35
  24.3 9.9 %collective-permute-start.8 = (bf16[2,1040,128]{2,1,0:T(8,128)(2,1)}, bf16[2,1040,128]{2,1,0:T(8,128)(2,1)S(1)}, u32[]{:S(2)}, u32[]{:S(2)}) collective-permute-start(bf16[2,1040,128]{2,1,0:T(8,128)(2,1)} %collective-permute-done.7.refs_6_), channel_id=1, source_target_pairs={{0,2},{1,15},{2,4},{3,1},{4,6},{5,3},{6,8},{7,5},{8,10},{9,7},{10,... | collective-permute-start | bytes 1597448 | tf_op jit(solution)/shard_map/ppermute | solution.py:43
  27.8 26.1 %collective-permute-start.4 = (bf16[4,1040,128]{2,1,0:T(8,128)(2,1)S(1)}, bf16[4,1040,128]{2,1,0:T(8,128)(2,1)}, u32[]{:S(2)}, u32[]{:S(2)}) collective-permute-start(bf16[4,1040,128]{2,1,0:T(8,128)(2,1)S(1)} %pad_maximum_fusion.refs_0_), channel_id=1, source_target_pairs={{0,192},{1,49},{16,208},{17,1},{32,224},{33,17},{48,240},{49,33},{... | collective-permute-start | bytes 3194888 | tf_op jit(solution)/shard_map/ppermute | solution.py:35
  30.5 7.5 %collective-permute-start.9 = (bf16[2,1040,128]{2,1,0:T(8,128)(2,1)S(1)}, bf16[2,1040,128]{2,1,0:T(8,128)(2,1)S(1)}, u32[]{:S(2)}, u32[]{:S(2)}) collective-permute-start(bf16[2,1040,128]{2,1,0:T(8,128)(2,1)S(1)} %collective-permute-done.6.refs_5_), channel_id=1, source_target_pairs={{0,1},{1,0},{2,3},{3,2},{4,5},{5,4},{6,7},{7,6},{8,9},{9,8},{10,11... | collective-permute-start | bytes 1597448 | tf_op jit(solution)/shard_map/ppermute | solution.py:47
  30.5 23.3 %collective-permute-start.5 = (bf16[4,1040,128]{2,1,0:T(8,128)(2,1)S(1)}, bf16[4,1040,128]{2,1,0:T(8,128)(2,1)}, u32[]{:S(2)}, u32[]{:S(2)}) collective-permute-start(bf16[4,1040,128]{2,1,0:T(8,128)(2,1)S(1)} %pad_maximum_fusion.refs_0_), channel_id=1, source_target_pairs={{0,128},{1,33},{16,144},{17,49},{32,160},{33,1},{48,176},{49,17},{... | collective-permute-start | bytes 3194888 | tf_op jit(solution)/shard_map/ppermute | solution.py:35
  34.3 19.5 %collective-permute-start.10 = (bf16[2,1040,128]{2,1,0:T(8,128)(2,1)}, bf16[2,1040,128]{2,1,0:T(8,128)(2,1)}, u32[]{:S(2)}, u32[]{:S(2)}) collective-permute-start(bf16[2,1040,128]{2,1,0:T(8,128)(2,1)} %collective-permute-done.7.refs_6_), channel_id=1, source_target_pairs={{0,1},{1,0},{2,3},{3,2},{4,5},{5,4},{6,7},{7,6},{8,9},{9,8},{10,11... | collective-permute-start | bytes 1597448 | tf_op jit(solution)/shard_map/ppermute | solution.py:47
  38.8 5.7 %collective-permute-start.12 = (bf16[1,1040,128]{2,1,0:T(8,128)(2,1)S(1)}, bf16[1,1040,128]{2,1,0:T(8,128)(2,1)S(1)}, u32[]{:S(2)}, u32[]{:S(2)}) collective-permute-start(bf16[1,1040,128]{2,1,0:T(8,128)(2,1)S(1)} %constant_dynamic-slice_fusion), channel_id=1, source_target_pairs={{0,2},{1,15},{2,4},{3,1},{4,6},{5,3},{6,8},{7,5},{8,10},{9,7},{10,... | collective-permute-start | bytes 798728 | tf_op jit(solution)/shard_map/ppermute | solution.py:43
  38.9 1.0 %copy-start.1 = (bf16[4,1040,128]{2,1,0:T(8,128)(2,1)}, bf16[4,1040,128]{2,1,0:T(8,128)(2,1)S(1)}, u32[]{:S(2)}) copy-start(bf16[4,1040,128]{2,1,0:T(8,128)(2,1)S(1)} %collective-permute-done.3.refs_1_) | copy-start | bytes 3194884
  39.9 14.0 %collective-permute-start.11 = (bf16[2,1040,128]{2,1,0:T(8,128)(2,1)S(1)}, bf16[2,1040,128]{2,1,0:T(8,128)(2,1)}, u32[]{:S(2)}, u32[]{:S(2)}) collective-permute-start(bf16[2,1040,128]{2,1,0:T(8,128)(2,1)S(1)} %collective-permute-done.8.refs_7_), channel_id=1, source_target_pairs={{0,1},{1,0},{2,3},{3,2},{4,5},{5,4},{6,7},{7,6},{8,9},{9,8},{10,11... | collective-permute-start | bytes 1597448 | tf_op jit(solution)/shard_map/ppermute | solution.py:47
  44.5 9.3 %collective-permute-start.13 = (bf16[1,1040,128]{2,1,0:T(8,128)(2,1)S(1)}, bf16[1,1040,128]{2,1,0:T(8,128)(2,1)}, u32[]{:S(2)}, u32[]{:S(2)}) collective-permute-start(bf16[1,1040,128]{2,1,0:T(8,128)(2,1)S(1)} %collective-permute-done.12.refs_11_), channel_id=1, source_target_pairs={{0,1},{1,0},{2,3},{3,2},{4,5},{5,4},{6,7},{7,6},{8,9},{9,8},{10,11... | collective-permute-start | bytes 798728 | tf_op jit(solution)/shard_map/ppermute | solution.py:47
  46.6 23.8 %copy-start.7 = (s32[8,2]{0,1:T(2,128)S(1)}, s32[8,2]{0,1:T(2,128)}, u32[]{:S(2)}) copy-start(s32[8,2]{0,1:T(2,128)} %param.15) | copy-start | bytes 196
  53.8 1.2 %copy-start.2 = (bf16[4,1040,128]{2,1,0:T(8,128)(2,1)S(1)}, bf16[4,1040,128]{2,1,0:T(8,128)(2,1)}, u32[]{:S(2)}) copy-start(bf16[4,1040,128]{2,1,0:T(8,128)(2,1)} %copy-done.1) | copy-start | bytes 3194884
  55.1 1.0 %copy-start.5 = (bf16[2,1040,128]{2,1,0:T(8,128)(2,1)S(1)}, bf16[2,1040,128]{2,1,0:T(8,128)(2,1)}, u32[]{:S(2)}) copy-start(bf16[2,1040,128]{2,1,0:T(8,128)(2,1)} %copy-done.4) | copy-start | bytes 1597444
  69.2 1.0 %copy-start.3 = (f32[8,128,256]{2,1,0:T(8,128)}, f32[8,128,256]{2,1,0:T(8,128)S(1)}, u32[]{:S(2)}) copy-start(f32[8,128,256]{2,1,0:T(8,128)S(1)} %get-tuple-element.7) | copy-start | bytes 3145732
  70.2 2.9 %collective-permute-start.14 = (f32[8,128,256]{2,1,0:T(8,128)}, f32[8,128,256]{2,1,0:T(8,128)S(1)}, u32[]{:S(2)}, u32[]{:S(2)}) collective-permute-start(f32[8,128,256]{2,1,0:T(8,128)} %get-tuple-element.8), channel_id=1, source_target_pairs={{0,1},{1,0},{2,3},{3,2},{4,5},{5,4},{6,7},{7,6},{8,9},{9,8},{10,11... | collective-permute-start | bytes 3145736 | tf_op jit(solution)/shard_map/ppermute | solution.py:47
  (1 other events, 0.8 us)

commit v2 on v1

v2 whole, which is shorter than its diff:
```python
import jax
import jax.numpy as jnp
from jax import lax
from jax.experimental import pallas as pl
from jax.experimental.pallas import tpu as pltpu
from jax.sharding import PartitionSpec as P

BLK = 128
RB = 8
CB = 4
KP = 4
SIDE = 4
META = 16
HALF = 8
DATA = HALF * BLK
ROWS = DATA + META
STEPS = (1, -1, 2)
ITEMS = 6
MOST = 64
LISTS = 8
NONE = 128 * 128


def with_meta(blocks, first, second):
    numbers = jnp.concatenate([first, second]).astype(jnp.bfloat16)
    meta = jnp.broadcast_to(numbers[:, None], (META, BLK))
    return jnp.concatenate([blocks.reshape(DATA, BLK), meta], axis=0)


def move_a(value, distance, phase):
    pairs = []
    for x in range(SIDE):
        for y in range(SIDE):
            for core in range(2):
                along_y = (core == 0) == (phase == 0)
                tx = x if along_y else (x + distance) % SIDE
                ty = (y + distance) % SIDE if along_y else y
                pairs.append(((x * SIDE + y) * 2 + core, (tx * SIDE + ty) * 2 + core))
    return lax.ppermute(value, ("row", "layer"), pairs)


def move_b(value, depth):
    pairs = []
    for z in range(depth):
        pairs.append((z * 2, ((z + 1) % depth) * 2))
        pairs.append((z * 2 + 1, ((z - 1) % depth) * 2 + 1))
    return lax.ppermute(value, ("col", "layer"), pairs)


def swap(value):
    return lax.ppermute(value, "layer", [(0, 1), (1, 0)])


def delta(index):
    return (0, SIDE - 1, 1, 2)[index]


def multiply(place, keep, *refs):
    a_refs, b_refs = refs[:4], refs[4:13]
    send, own, av, bv, am, bm, keys, list_v, lists, data_sem, meta_sem, list_sem = refs[13:]
    x, y, z, core = place[0], place[1], place[2], place[3]
    spots = [(b_refs[0], 0, 2)]
    for t in range(1, 4):
        spots.append((b_refs[t], 2 * jnp.where(core == 0, 8 - t, t), 2))
        spots.append((b_refs[3 + t], 2 * jnp.where(core == 0, t, 8 - t), 2))
    spots.append((b_refs[7], 8 + core, 1))
    spots.append((b_refs[8], 9 - core, 1))
    copies, metas = [], []
    for held, meta, group in (
        (av, am, [(a_refs[g], 4 * g, 4) for g in range(4)]),
        (bv, bm, spots),
    ):
        for ref, at, count in group:
            n = len(copies)
            copies.append(
                pltpu.make_async_copy(
                    ref.at[:, pl.ds(0, DATA), :], held.at[pl.ds(at, count)], data_sem.at[n]
                )
            )
            metas.append(
                pltpu.make_async_copy(
                    ref.at[:, pl.ds(DATA, META), :], meta.at[pl.ds(at, count)], meta_sem.at[n]
                )
            )
    for copy in metas:
        copy.start()
    for copy in copies:
        copy.start()
    av[16, 0:BLK, :] = jnp.zeros((BLK, BLK), jnp.bfloat16)
    lane = lax.broadcasted_iota(jnp.int32, (HALF, BLK), 1)
    slot = lax.broadcasted_iota(jnp.int32, (HALF, BLK), 0).astype(jnp.float32)
    bucket_row = (lane // CB).astype(jnp.float32)
    bucket_col = (lane % CB).astype(jnp.float32)
    for copy in metas:
        copy.wait()
    count = jnp.zeros((HALF, BLK), jnp.float32)
    for p in range(16):
        first, second = delta(p // 4), delta(p % 4)
        px = (x + jnp.where(core == 0, first, second)) % SIDE
        py = (y + jnp.where(core == 0, second, first)) % SIDE
        k = (px * SIDE + py + 2 * z) % 16
        q = (k - (x * SIDE + y) + 16) % 16
        spot = ((q // 2 - z + 8) % 8) * 2 + q % 2
        numbers = am[p].astype(jnp.float32)
        wanted = numbers[HALF:, :] + bucket_col
        b_numbers = bm[spot].astype(jnp.float32)
        found = jnp.zeros((HALF, BLK), jnp.float32)
        for t in range(HALF):
            found = jnp.where(b_numbers[t : t + 1, :] == wanted, t + 1.0, found)
        kept = keep[pl.ds(k, 1), :].astype(jnp.float32)
        valid = jnp.where(numbers[:HALF, :] == bucket_row, kept, 0.0)
        valid = (valid != 0.0) & (found != 0.0)
        base = (p * HALF * 128 - 1 + spot * HALF).astype(jnp.float32)
        keys[p] = jnp.where(valid, base + slot * 128.0 + found, float(NONE))
        count = count + jnp.where(valid, 1.0, 0.0)
    count = jnp.sum(count, axis=0, keepdims=True)
    list_v[0:1, :] = count.astype(jnp.int32)
    largest = jnp.max(count).astype(jnp.int32)

    def pick(j):
        least = keys[0]
        for p in range(1, 16):
            least = jnp.minimum(least, keys[p])
        least = jnp.min(least, axis=0, keepdims=True)
        list_v[pl.ds(1 + j, 1), :] = least.astype(jnp.int32)
        for p in range(16):
            keys[p] = jnp.where(keys[p] == least, float(NONE), keys[p])

    for j in range(ITEMS):
        pick(j)
    near = pltpu.make_async_copy(
        list_v.at[pl.ds(0, LISTS)], lists.at[pl.ds(0, LISTS)], list_sem.at[0]
    )
    near.start()
    near.wait()
    for copy in copies:
        copy.wait()

    def product(b, start, length):
        left, right = [], []
        for j in range(length):
            code = lists[1 + start + j, b]
            ia, ib = code // 128, code % 128
            left.append(av[ia // HALF, pl.ds(pl.multiple_of((ia % HALF) * BLK, BLK), BLK), :])
            right.append(bv[ib // HALF, pl.ds(pl.multiple_of((ib % HALF) * BLK, BLK), BLK), :])
        return jnp.dot(
            jnp.concatenate(left, axis=1),
            jnp.concatenate(right, axis=0),
            preferred_element_type=jnp.float32,
        )

    outs = ((send, 2 * (1 - core)), (own, 2 * core))

    def block_row(r, carry):
        for ref, base in outs:
            for n in range(2):
                ref[r, :, n * BLK : (n + 1) * BLK] = product(r * CB + base + n, 0, ITEMS)
        return carry

    lax.fori_loop(0, RB, block_row, 0)

    @pl.when(largest > ITEMS)
    def _():
        def more(j, carry):
            pick(j)
            return carry

        lax.fori_loop(ITEMS, largest, more, 0)
        far = pltpu.make_async_copy(list_v, lists, list_sem.at[1])
        far.start()
        far.wait()

        def rest_of_row(r, carry):
            for ref, base in outs:
                for n in range(2):
                    b = r * CB + base + n

                    def one(j, inner):
                        ref[r, :, n * BLK : (n + 1) * BLK] += product(b, j, 1)
                        return inner

                    lax.fori_loop(ITEMS, jnp.maximum(lists[0, b], ITEMS), one, 0)
            return carry

        lax.fori_loop(0, RB, rest_of_row, 0)


def partial_sums(place, keep, a_parts, b_parts):
    vmem = pl.BlockSpec(memory_space=pltpu.VMEM)
    smem = pl.BlockSpec(memory_space=pltpu.SMEM)
    anywhere = pl.BlockSpec(memory_space=pl.ANY)
    half = jax.ShapeDtypeStruct((RB, BLK, 2 * BLK), jnp.float32)
    return pl.pallas_call(
        multiply,
        out_shape=(half, half),
        in_specs=[smem, vmem] + [anywhere] * 13,
        out_specs=(vmem, vmem),
        scratch_shapes=[
            pltpu.VMEM((17, DATA, BLK), jnp.bfloat16),
            pltpu.VMEM((16, DATA, BLK), jnp.bfloat16),
            pltpu.VMEM((16, META, BLK), jnp.bfloat16),
            pltpu.VMEM((16, META, BLK), jnp.bfloat16),
            pltpu.VMEM((16, HALF, BLK), jnp.float32),
            pltpu.VMEM((LISTS + MOST, BLK), jnp.int32),
            pltpu.SMEM((LISTS + MOST, BLK), jnp.int32),
            pltpu.SemaphoreType.DMA((13,)),
            pltpu.SemaphoreType.DMA((13,)),
            pltpu.SemaphoreType.DMA((2,)),
        ],
        compiler_params=pltpu.CompilerParams(vmem_limit_bytes=32 * 1024 * 1024),
    )(place, keep, *a_parts, *b_parts)


def finish(keep, own, other, out):
    for r in range(RB):
        for n in range(2):
            cols = slice(n * BLK, (n + 1) * BLK)
            total = own[r, :, cols] + other[r, :, cols]
            total = total * keep[r, n].astype(jnp.float32)
            out[r * BLK : (r + 1) * BLK, cols] = total.astype(jnp.bfloat16)


def filtered(keep, own, other):
    vmem = pl.BlockSpec(memory_space=pltpu.VMEM)
    return pl.pallas_call(
        finish,
        out_shape=jax.ShapeDtypeStruct((RB * BLK, 2 * BLK), jnp.bfloat16),
        in_specs=[pl.BlockSpec(memory_space=pltpu.SMEM), vmem, vmem],
        out_specs=vmem,
    )(keep, own, other)


def body(a_blocks, a_rows, a_cols, b_blocks, b_rows, b_cols, prod_keep, res_keep):
    depth = lax.axis_size("col")
    row = lax.axis_index("row")
    z = lax.axis_index("col")
    core = lax.axis_index("layer")
    place = jnp.stack([row // SIDE, row % SIDE, z, core]).astype(jnp.int32)

    def my_half(array):
        halves = array.reshape((HALF, 2) + array.shape[1:])
        return lax.dynamic_index_in_dim(halves, core, 1, keepdims=False)

    a_mine = with_meta(my_half(a_blocks[0, 0]), my_half(a_rows[0, 0]), my_half(a_cols[0, 0]) * CB)
    b_number = b_rows[:, 0] * CB + b_cols[:, 0]
    b_mine = jnp.stack([with_meta(b_blocks[i, 0], b_number[i], b_number[i]) for i in range(2)])

    b_from = [b_mine]
    for _ in range(3):
        b_from.append(move_b(b_from[-1], depth))
    last = move_b(lax.dynamic_slice_in_dim(b_from[3], core, 1, 0), depth)
    b_theirs = [swap(part) for part in b_from[1:]]
    last_theirs = swap(last)

    a_own = jnp.stack([a_mine] + [move_a(a_mine, d, 0) for d in STEPS])
    a_parts = [a_own] + [move_a(a_own, d, 1) for d in STEPS]

    keep = prod_keep.transpose(1, 0, 2).reshape(16, RB * CB)
    keep = jnp.pad(keep, ((0, 0), (0, BLK - RB * CB)))
    send, own = partial_sums(place, keep, a_parts, b_from + b_theirs + [last, last_theirs])
    return filtered(res_keep, own, swap(send))


def solution(mesh):
    return jax.shard_map(
        body,
        mesh=mesh,
        in_specs=(
            P("col", "row", None, None, None),
            P("col", "row", None),
            P("col", "row", None),
            P("col", "row", None, None, None),
            P("col", "row", None),
            P("col", "row", None),
            P("col", None, "row"),
            P("col", ("row", "layer")),
        ),
        out_specs=P("col", ("row", "layer")),
        check_vma=False,
    )
```

time: 76.5 us -> 78.3 us (1.024)
  the two profiles are of different devices: /device:TPU:1 before, /device:TPU:133 now
where the time goes in v2:
time: 78.3 us; the launch traced here: 77.9 us
  starting transfers between devices  37.1 us (47%)
  waiting for transfers between devices  17.3 us (22%)
  Pallas kernels  11.6 us (15%)
  local copies, waits for them, and re-layouts  8.55 us (11%)
  other arithmetic  3.18 us (4%)
    ppermute x5, starting transfers between devices, swap(): return lax.ppermute(value, 'layer', [(0, 1), (1, 0)])  23.4 us
    ppermute x4, waiting for transfers between devices, move_b(): return lax.ppermute(value, ('col', 'layer'), pairs)  11 us
    ppermute x6, starting transfers between devices, move_a(): return lax.ppermute(value, ('row', 'layer'), pairs)  9.62 us
    pallas_call x1, Pallas kernels, partial_sums(): pl.pallas_call(multiply, out_shape=(half, half), in_specs=[smem, vmem] +...  9.16 us
    unnamed x24, local copies, waits for them, and re-layouts  7.22 us
    ppermute x4, starting transfers between devices, move_b(): return lax.ppermute(value, ('col', 'layer'), pairs)  4.11 us
    ppermute x6, waiting for transfers between devices, move_a(): return lax.ppermute(value, ('row', 'layer'), pairs)  3.33 us
    ppermute x5, waiting for transfers between devices, swap(): return lax.ppermute(value, 'layer', [(0, 1), (1, 0)])  2.95 us
  transfers between devices with their start and end apart: 15, of which 8 were waited for; matrix products, arithmetic and copies ran while one was open for 4% of the time, Pallas kernels for 0%

profile of v2, /device:TPU:133, one launch (start us, length us, event | category | flops | bytes accessed | tf_op | source)
XLA Modules:
  0.0 77.9 jit_solution(16984223892073043730)
XLA Ops:
  0.8 1.1 %fusion.5 = (bf16[1,1,8,128,128]{4,3,2,1,0:T(8,128)(2,1)S(1)}, bf16[1,1,8,128,128]{4,3,2,1,0:T(8,128)(2,1)S(1)}) fusion(bf16[2,1,8,128,128]{4,3,2,1,0:T(8,128)(2,1)} %param.11), kind=kLoop, calls=%fused_computation.21 | loop fusion | bytes 1048576 | tf_op jit(solution)/shard_map/slice | solution.py:246
  5.2 2.5 %collective-permute-start.2 = (bf16[1040,128]{1,0:T(8,128)(2,1)S(1)}, bf16[1040,128]{1,0:T(8,128)(2,1)S(1)}, u32[]{:S(2)}, u32[]{:S(2)}) collective-permute-start(bf16[1040,128]{1,0:T(8,128)(2,1)S(1)} %get-tuple-element.12), channel_id=1, source_target_pairs={{0,32},{1,129},{16,48},{17,145},{32,0},{33,161},{48,16},{49,177},{... | collective-permute-start | bytes 798728 | tf_op jit(solution)/shard_map/ppermute | solution.py:39
  7.7 3.2 %collective-permute-done.6.refs_5_ = bf16[2,1040,128]{2,1,0:T(8,128)(2,1)S(1)} collective-permute-done((bf16[2,1040,128]{2,1,0:T(8,128)(2,1)S(1)}, bf16[2,1040,128]{2,1,0:T(8,128)(2,1)S(1)}, u32[]{:S(2)}, u32[]{:S(2)}) %collective-permute-start.6) | collective-permute-done | bytes 532512 | tf_op jit(solution)/shard_map/ppermute | solution.py:47
  10.9 0.9 %collective-permute-start.7 = (bf16[2,1040,128]{2,1,0:T(8,128)(2,1)S(1)}, bf16[2,1040,128]{2,1,0:T(8,128)(2,1)}, u32[]{:S(2)}, u32[]{:S(2)}) collective-permute-start(bf16[2,1040,128]{2,1,0:T(8,128)(2,1)S(1)} %collective-permute-done.6.refs_5_), channel_id=1, source_target_pairs={{0,2},{1,15},{2,4},{3,1},{4,6},{5,3},{6,8},{7,5},{8,10},{9,7},{10,... | collective-permute-start | bytes 1597448 | tf_op jit(solution)/shard_map/ppermute | solution.py:47
  12.3 2.8 %collective-permute-done = bf16[1040,128]{1,0:T(8,128)(2,1)S(1)} collective-permute-done((bf16[1040,128]{1,0:T(8,128)(2,1)S(1)}, bf16[1040,128]{1,0:T(8,128)(2,1)S(1)}, u32[]{:S(2)}, u32[]{:S(2)}) %collective-permute-start) | collective-permute-done | bytes 266272 | tf_op jit(solution)/shard_map/ppermute | solution.py:39
  15.3 1.4 %collective-permute-start.3 = (bf16[4,1040,128]{2,1,0:T(8,128)(2,1)S(1)}, bf16[4,1040,128]{2,1,0:T(8,128)(2,1)S(1)}, u32[]{:S(2)}, u32[]{:S(2)}) collective-permute-start(bf16[4,1040,128]{2,1,0:T(8,128)(2,1)S(1)} %pad_maximum_fusion.refs_0_), channel_id=1, source_target_pairs={{0,64},{1,17},{16,80},{17,33},{32,96},{33,49},{48,112},{49,1},{64,... | collective-permute-start | bytes 3194888 | tf_op jit(solution)/shard_map/ppermute | solution.py:39
  16.7 2.8 %collective-permute-done.7.refs_6_ = bf16[2,1040,128]{2,1,0:T(8,128)(2,1)} collective-permute-done((bf16[2,1040,128]{2,1,0:T(8,128)(2,1)S(1)}, bf16[2,1040,128]{2,1,0:T(8,128)(2,1)}, u32[]{:S(2)}, u32[]{:S(2)}) %collective-permute-start.7) | collective-permute-done | bytes 532512 | tf_op jit(solution)/shard_map/ppermute | solution.py:47
  19.4 2.0 %collective-permute-start.8 = (bf16[2,1040,128]{2,1,0:T(8,128)(2,1)}, bf16[2,1040,128]{2,1,0:T(8,128)(2,1)S(1)}, u32[]{:S(2)}, u32[]{:S(2)}) collective-permute-start(bf16[2,1040,128]{2,1,0:T(8,128)(2,1)} %collective-permute-done.7.refs_6_), channel_id=1, source_target_pairs={{0,2},{1,15},{2,4},{3,1},{4,6},{5,3},{6,8},{7,5},{8,10},{9,7},{10,... | collective-permute-start | bytes 1597448 | tf_op jit(solution)/shard_map/ppermute | solution.py:47
  21.4 2.5 %collective-permute-start.4 = (bf16[4,1040,128]{2,1,0:T(8,128)(2,1)S(1)}, bf16[4,1040,128]{2,1,0:T(8,128)(2,1)}, u32[]{:S(2)}, u32[]{:S(2)}) collective-permute-start(bf16[4,1040,128]{2,1,0:T(8,128)(2,1)S(1)} %pad_maximum_fusion.refs_0_), channel_id=1, source_target_pairs={{0,192},{1,49},{16,208},{17,1},{32,224},{33,17},{48,240},{49,33},{... | collective-permute-start | bytes 3194888 | tf_op jit(solution)/shard_map/ppermute | solution.py:39
  24.8 2.9 %collective-permute-start.5 = (bf16[4,1040,128]{2,1,0:T(8,128)(2,1)S(1)}, bf16[4,1040,128]{2,1,0:T(8,128)(2,1)}, u32[]{:S(2)}, u32[]{:S(2)}) collective-permute-start(bf16[4,1040,128]{2,1,0:T(8,128)(2,1)S(1)} %pad_maximum_fusion.refs_0_), channel_id=1, source_target_pairs={{0,128},{1,33},{16,144},{17,49},{32,160},{33,1},{48,176},{49,17},{... | collective-permute-start | bytes 3194888 | tf_op jit(solution)/shard_map/ppermute | solution.py:39
  28.1 6.8 %collective-permute-start.10 = (bf16[2,1040,128]{2,1,0:T(8,128)(2,1)}, bf16[2,1040,128]{2,1,0:T(8,128)(2,1)}, u32[]{:S(2)}, u32[]{:S(2)}) collective-permute-start(bf16[2,1040,128]{2,1,0:T(8,128)(2,1)} %collective-permute-done.7.refs_6_), channel_id=1, source_target_pairs={{0,1},{1,0},{2,3},{3,2},{4,5},{5,4},{6,7},{7,6},{8,9},{9,8},{10,11... | collective-permute-start | bytes 1597448 | tf_op jit(solution)/shard_map/ppermute | solution.py:51
  35.8 1.0 %copy-done.1 = bf16[4,1040,128]{2,1,0:T(8,128)(2,1)} copy-done((bf16[4,1040,128]{2,1,0:T(8,128)(2,1)}, bf16[4,1040,128]{2,1,0:T(8,128)(2,1)S(1)}, u32[]{:S(2)}) %copy-start.1) | copy-done | bytes 1064984
  36.7 1.1 %collective-permute-start.12 = (bf16[1,1040,128]{2,1,0:T(8,128)(2,1)S(1)}, bf16[1,1040,128]{2,1,0:T(8,128)(2,1)S(1)}, u32[]{:S(2)}, u32[]{:S(2)}) collective-permute-start(bf16[1,1040,128]{2,1,0:T(8,128)(2,1)S(1)} %constant_dynamic-slice_fusion), channel_id=1, source_target_pairs={{0,2},{1,15},{2,4},{3,1},{4,6},{5,3},{6,8},{7,5},{8,10},{9,7},{10,... | collective-permute-start | bytes 798728 | tf_op jit(solution)/shard_map/ppermute | solution.py:47
  37.8 4.6 %collective-permute-done.12.refs_11_ = bf16[1,1040,128]{2,1,0:T(8,128)(2,1)S(1)} collective-permute-done((bf16[1,1040,128]{2,1,0:T(8,128)(2,1)S(1)}, bf16[1,1040,128]{2,1,0:T(8,128)(2,1)S(1)}, u32[]{:S(2)}, u32[]{:S(2)}) %collective-permute-start.12) | collective-permute-done | bytes 266272 | tf_op jit(solution)/shard_map/ppermute | solution.py:47
  42.4 13.9 %collective-permute-start.13 = (bf16[1,1040,128]{2,1,0:T(8,128)(2,1)S(1)}, bf16[1,1040,128]{2,1,0:T(8,128)(2,1)}, u32[]{:S(2)}, u32[]{:S(2)}) collective-permute-start(bf16[1,1040,128]{2,1,0:T(8,128)(2,1)S(1)} %collective-permute-done.12.refs_11_), channel_id=1, source_target_pairs={{0,1},{1,0},{2,3},{3,2},{4,5},{5,4},{6,7},{7,6},{8,9},{9,8},{10,11... | collective-permute-start | bytes 798728 | tf_op jit(solution)/shard_map/ppermute | solution.py:51
  56.4 1.1 %collective-permute-done.13.refs_12_ = bf16[1,1040,128]{2,1,0:T(8,128)(2,1)} collective-permute-done((bf16[1,1040,128]{2,1,0:T(8,128)(2,1)S(1)}, bf16[1,1040,128]{2,1,0:T(8,128)(2,1)}, u32[]{:S(2)}, u32[]{:S(2)}) %collective-permute-start.13) | collective-permute-done | bytes 266272 | tf_op jit(solution)/shard_map/ppermute | solution.py:51
  57.6 1.2 %copy-done.2 = bf16[4,1040,128]{2,1,0:T(8,128)(2,1)S(1)} copy-done((bf16[4,1040,128]{2,1,0:T(8,128)(2,1)S(1)}, bf16[4,1040,128]{2,1,0:T(8,128)(2,1)}, u32[]{:S(2)}) %copy-start.2) | copy-done | bytes 1064984
  58.8 1.0 %copy-done.5 = bf16[2,1040,128]{2,1,0:T(8,128)(2,1)S(1)} copy-done((bf16[2,1040,128]{2,1,0:T(8,128)(2,1)S(1)}, bf16[2,1040,128]{2,1,0:T(8,128)(2,1)}, u32[]{:S(2)}) %copy-start.5) | copy-done | bytes 532504
  59.8 9.2 %shard_map.82 = (f32[8,128,256]{2,1,0:T(8,128)}, f32[8,128,256]{2,1,0:T(8,128)S(1)}) custom-call(s32[4]{0:T(128)S(1)} %pad_add_fusion.place, s32[16,128]{1,0:T(8,128)S(1)} %pad.4.keep, bf16[4,1040,128]{2,1,0:T(8,128)(2,1)S(1)} %pad_maximum_fusion.refs_0_, bf16[4,1040,128]{2,1,0:T(8,128)(2,1)S(1)} %copy-done.2, ...), custom_call_target="tpu_custom_call" | custom-call | tf_op jit(solution)/shard_map/pallas_call | solution.py:193
  69.0 1.0 %copy-done.3 = f32[8,128,256]{2,1,0:T(8,128)} copy-done((f32[8,128,256]{2,1,0:T(8,128)}, f32[8,128,256]{2,1,0:T(8,128)S(1)}, u32[]{:S(2)}) %copy-start.3) | copy-done | bytes 1048600
  70.0 2.0 %collective-permute-start.14 = (f32[8,128,256]{2,1,0:T(8,128)}, f32[8,128,256]{2,1,0:T(8,128)S(1)}, u32[]{:S(2)}, u32[]{:S(2)}) collective-permute-start(f32[8,128,256]{2,1,0:T(8,128)} %get-tuple-element.8), channel_id=1, source_target_pairs={{0,1},{1,0},{2,3},{3,2},{4,5},{5,4},{6,7},{7,6},{8,9},{9,8},{10,11... | collective-permute-start | bytes 3145736 | tf_op jit(solution)/shard_map/ppermute | solution.py:51
  72.7 1.8 %collective-permute-done.14.other = f32[8,128,256]{2,1,0:T(8,128)S(1)} collective-permute-done((f32[8,128,256]{2,1,0:T(8,128)}, f32[8,128,256]{2,1,0:T(8,128)S(1)}, u32[]{:S(2)}, u32[]{:S(2)}) %collective-permute-start.14) | collective-permute-done | bytes 1048608 | tf_op jit(solution)/shard_map/ppermute | solution.py:51
  74.5 1.0 %copy-done.6 = f32[8,128,256]{2,1,0:T(8,128)} copy-done((f32[8,128,256]{2,1,0:T(8,128)}, f32[8,128,256]{2,1,0:T(8,128)S(1)}, u32[]{:S(2)}) %copy-start.6) | copy-done | bytes 1048600
  75.5 2.5 %shard_map.83 = bf16[1024,256]{1,0:T(8,128)(2,1)} custom-call(s32[8,2]{1,0:T(8,128)} %copy.14.keep, f32[8,128,256]{2,1,0:T(8,128)} %copy-done.3, f32[8,128,256]{2,1,0:T(8,128)} %copy-done.6), custom_call_target="tpu_custom_call" | custom-call | tf_op jit(solution)/shard_map/pallas_call | solution.py:225
  (52 shorter events, 7.7 us)
Async XLA Ops:
  0.0 4.3 %copy-start = (bf16[1,1,16,128,128]{4,3,2,1,0:T(8,128)(2,1)S(1)}, bf16[1,1,16,128,128]{4,3,2,1,0:T(8,128)(2,1)}, u32[]{:S(2)}) copy-start(bf16[1,1,16,128,128]{4,3,2,1,0:T(8,128)(2,1)} %param.8) | copy-start | bytes 1572868
  1.9 1.1 %copy-start.9 = (s32[1,1,16]{2,1,0:T(1,128)S(1)}, s32[1,1,16]{2,1,0:T(1,128)}, u32[]{:S(2)}) copy-start(s32[1,1,16]{2,1,0:T(1,128)} %param.9) | copy-start | bytes 196
  1.9 1.8 %copy-start.10 = (s32[1,1,16]{2,1,0:T(1,128)S(1)}, s32[1,1,16]{2,1,0:T(1,128)}, u32[]{:S(2)}) copy-start(s32[1,1,16]{2,1,0:T(1,128)} %param.10) | copy-start | bytes 196
  2.4 8.5 %collective-permute-start.6 = (bf16[2,1040,128]{2,1,0:T(8,128)(2,1)S(1)}, bf16[2,1040,128]{2,1,0:T(8,128)(2,1)S(1)}, u32[]{:S(2)}, u32[]{:S(2)}) collective-permute-start(bf16[2,1040,128]{2,1,0:T(8,128)(2,1)S(1)} %pad_maximum_fusion.1.refs_4_), channel_id=1, source_target_pairs={{0,2},{1,15},{2,4},{3,1},{4,6},{5,3},{6,8},{7,5},{8,10},{9,7},{10,... | collective-permute-start | bytes 1597448 | tf_op jit(solution)/shard_map/ppermute | solution.py:47
  4.9 6.9 %collective-permute-start.1 = (bf16[1040,128]{1,0:T(8,128)(2,1)S(1)}, bf16[1040,128]{1,0:T(8,128)(2,1)S(1)}, u32[]{:S(2)}, u32[]{:S(2)}) collective-permute-start(bf16[1040,128]{1,0:T(8,128)(2,1)S(1)} %get-tuple-element.12), channel_id=1, source_target_pairs={{0,48},{1,193},{16,0},{17,209},{32,16},{33,225},{48,32},{49,241},{... | collective-permute-start | bytes 798728 | tf_op jit(solution)/shard_map/ppermute | solution.py:39
  5.2 7.1 %collective-permute-start.2 = (bf16[1040,128]{1,0:T(8,128)(2,1)S(1)}, bf16[1040,128]{1,0:T(8,128)(2,1)S(1)}, u32[]{:S(2)}, u32[]{:S(2)}) collective-permute-start(bf16[1040,128]{1,0:T(8,128)(2,1)S(1)} %get-tuple-element.12), channel_id=1, source_target_pairs={{0,32},{1,129},{16,48},{17,145},{32,0},{33,161},{48,16},{49,177},{... | collective-permute-start | bytes 798728 | tf_op jit(solution)/shard_map/ppermute | solution.py:39
  7.7 7.5 %collective-permute-start = (bf16[1040,128]{1,0:T(8,128)(2,1)S(1)}, bf16[1040,128]{1,0:T(8,128)(2,1)S(1)}, u32[]{:S(2)}, u32[]{:S(2)}) collective-permute-start(bf16[1040,128]{1,0:T(8,128)(2,1)S(1)} %get-tuple-element.12), channel_id=1, source_target_pairs={{0,16},{1,65},{16,32},{17,81},{32,48},{33,97},{48,0},{49,113},{64,... | collective-permute-start | bytes 798728 | tf_op jit(solution)/shard_map/ppermute | solution.py:39
  10.9 8.5 %collective-permute-start.7 = (bf16[2,1040,128]{2,1,0:T(8,128)(2,1)S(1)}, bf16[2,1040,128]{2,1,0:T(8,128)(2,1)}, u32[]{:S(2)}, u32[]{:S(2)}) collective-permute-start(bf16[2,1040,128]{2,1,0:T(8,128)(2,1)S(1)} %collective-permute-done.6.refs_5_), channel_id=1, source_target_pairs={{0,2},{1,15},{2,4},{3,1},{4,6},{5,3},{6,8},{7,5},{8,10},{9,7},{10,... | collective-permute-start | bytes 1597448 | tf_op jit(solution)/shard_map/ppermute | solution.py:47
  15.1 41.1 %copy-start.7 = (s32[8,16,4]{1,2,0:T(4,128)S(1)}, s32[8,16,4]{1,2,0:T(4,128)}, u32[]{:S(2)}) copy-start(s32[8,16,4]{1,2,0:T(4,128)} %param.14) | copy-start | bytes 6148
  15.3 20.5 %collective-permute-start.3 = (bf16[4,1040,128]{2,1,0:T(8,128)(2,1)S(1)}, bf16[4,1040,128]{2,1,0:T(8,128)(2,1)S(1)}, u32[]{:S(2)}, u32[]{:S(2)}) collective-permute-start(bf16[4,1040,128]{2,1,0:T(8,128)(2,1)S(1)} %pad_maximum_fusion.refs_0_), channel_id=1, source_target_pairs={{0,64},{1,17},{16,80},{17,33},{32,96},{33,49},{48,112},{49,1},{64,... | collective-permute-start | bytes 3194888 | tf_op jit(solution)/shard_map/ppermute | solution.py:39
  19.4 8.7 %collective-permute-start.8 = (bf16[2,1040,128]{2,1,0:T(8,128)(2,1)}, bf16[2,1040,128]{2,1,0:T(8,128)(2,1)S(1)}, u32[]{:S(2)}, u32[]{:S(2)}) collective-permute-start(bf16[2,1040,128]{2,1,0:T(8,128)(2,1)} %collective-permute-done.7.refs_6_), channel_id=1, source_target_pairs={{0,2},{1,15},{2,4},{3,1},{4,6},{5,3},{6,8},{7,5},{8,10},{9,7},{10,... | collective-permute-start | bytes 1597448 | tf_op jit(solution)/shard_map/ppermute | solution.py:47
  21.4 35.0 %collective-permute-start.4 = (bf16[4,1040,128]{2,1,0:T(8,128)(2,1)S(1)}, bf16[4,1040,128]{2,1,0:T(8,128)(2,1)}, u32[]{:S(2)}, u32[]{:S(2)}) collective-permute-start(bf16[4,1040,128]{2,1,0:T(8,128)(2,1)S(1)} %pad_maximum_fusion.refs_0_), channel_id=1, source_target_pairs={{0,192},{1,49},{16,208},{17,1},{32,224},{33,17},{48,240},{49,33},{... | collective-permute-start | bytes 3194888 | tf_op jit(solution)/shard_map/ppermute | solution.py:39
  24.0 10.9 %collective-permute-start.9 = (bf16[2,1040,128]{2,1,0:T(8,128)(2,1)S(1)}, bf16[2,1040,128]{2,1,0:T(8,128)(2,1)S(1)}, u32[]{:S(2)}, u32[]{:S(2)}) collective-permute-start(bf16[2,1040,128]{2,1,0:T(8,128)(2,1)S(1)} %collective-permute-done.6.refs_5_), channel_id=1, source_target_pairs={{0,1},{1,0},{2,3},{3,2},{4,5},{5,4},{6,7},{7,6},{8,9},{9,8},{10,11... | collective-permute-start | bytes 1597448 | tf_op jit(solution)/shard_map/ppermute | solution.py:51
  24.8 31.7 %collective-permute-start.5 = (bf16[4,1040,128]{2,1,0:T(8,128)(2,1)S(1)}, bf16[4,1040,128]{2,1,0:T(8,128)(2,1)}, u32[]{:S(2)}, u32[]{:S(2)}) collective-permute-start(bf16[4,1040,128]{2,1,0:T(8,128)(2,1)S(1)} %pad_maximum_fusion.refs_0_), channel_id=1, source_target_pairs={{0,128},{1,33},{16,144},{17,49},{32,160},{33,1},{48,176},{49,17},{... | collective-permute-start | bytes 3194888 | tf_op jit(solution)/shard_map/ppermute | solution.py:39
  28.1 28.3 %collective-permute-start.10 = (bf16[2,1040,128]{2,1,0:T(8,128)(2,1)}, bf16[2,1040,128]{2,1,0:T(8,128)(2,1)}, u32[]{:S(2)}, u32[]{:S(2)}) collective-permute-start(bf16[2,1040,128]{2,1,0:T(8,128)(2,1)} %collective-permute-done.7.refs_6_), channel_id=1, source_target_pairs={{0,1},{1,0},{2,3},{3,2},{4,5},{5,4},{6,7},{7,6},{8,9},{9,8},{10,11... | collective-permute-start | bytes 1597448 | tf_op jit(solution)/shard_map/ppermute | solution.py:51
  35.7 20.7 %collective-permute-start.11 = (bf16[2,1040,128]{2,1,0:T(8,128)(2,1)S(1)}, bf16[2,1040,128]{2,1,0:T(8,128)(2,1)}, u32[]{:S(2)}, u32[]{:S(2)}) collective-permute-start(bf16[2,1040,128]{2,1,0:T(8,128)(2,1)S(1)} %collective-permute-done.8.refs_7_), channel_id=1, source_target_pairs={{0,1},{1,0},{2,3},{3,2},{4,5},{5,4},{6,7},{7,6},{8,9},{9,8},{10,11... | collective-permute-start | bytes 1597448 | tf_op jit(solution)/shard_map/ppermute | solution.py:51
  35.8 1.0 %copy-start.1 = (bf16[4,1040,128]{2,1,0:T(8,128)(2,1)}, bf16[4,1040,128]{2,1,0:T(8,128)(2,1)S(1)}, u32[]{:S(2)}) copy-start(bf16[4,1040,128]{2,1,0:T(8,128)(2,1)S(1)} %collective-permute-done.3.refs_1_) | copy-start | bytes 3194884
  36.7 5.7 %collective-permute-start.12 = (bf16[1,1040,128]{2,1,0:T(8,128)(2,1)S(1)}, bf16[1,1040,128]{2,1,0:T(8,128)(2,1)S(1)}, u32[]{:S(2)}, u32[]{:S(2)}) collective-permute-start(bf16[1,1040,128]{2,1,0:T(8,128)(2,1)S(1)} %constant_dynamic-slice_fusion), channel_id=1, source_target_pairs={{0,2},{1,15},{2,4},{3,1},{4,6},{5,3},{6,8},{7,5},{8,10},{9,7},{10,... | collective-permute-start | bytes 798728 | tf_op jit(solution)/shard_map/ppermute | solution.py:47
  42.4 15.2 %collective-permute-start.13 = (bf16[1,1040,128]{2,1,0:T(8,128)(2,1)S(1)}, bf16[1,1040,128]{2,1,0:T(8,128)(2,1)}, u32[]{:S(2)}, u32[]{:S(2)}) collective-permute-start(bf16[1,1040,128]{2,1,0:T(8,128)(2,1)S(1)} %collective-permute-done.12.refs_11_), channel_id=1, source_target_pairs={{0,1},{1,0},{2,3},{3,2},{4,5},{5,4},{6,7},{7,6},{8,9},{9,8},{10,11... | collective-permute-start | bytes 798728 | tf_op jit(solution)/shard_map/ppermute | solution.py:51
  56.3 15.7 %copy-start.8 = (s32[8,2]{0,1:T(2,128)S(1)}, s32[8,2]{0,1:T(2,128)}, u32[]{:S(2)}) copy-start(s32[8,2]{0,1:T(2,128)} %param.15) | copy-start | bytes 196
  57.6 1.2 %copy-start.2 = (bf16[4,1040,128]{2,1,0:T(8,128)(2,1)S(1)}, bf16[4,1040,128]{2,1,0:T(8,128)(2,1)}, u32[]{:S(2)}) copy-start(bf16[4,1040,128]{2,1,0:T(8,128)(2,1)} %copy-done.1) | copy-start | bytes 3194884
  58.8 1.0 %copy-start.5 = (bf16[2,1040,128]{2,1,0:T(8,128)(2,1)S(1)}, bf16[2,1040,128]{2,1,0:T(8,128)(2,1)}, u32[]{:S(2)}) copy-start(bf16[2,1040,128]{2,1,0:T(8,128)(2,1)} %copy-done.4) | copy-start | bytes 1597444
  69.0 1.0 %copy-start.3 = (f32[8,128,256]{2,1,0:T(8,128)}, f32[8,128,256]{2,1,0:T(8,128)S(1)}, u32[]{:S(2)}) copy-start(f32[8,128,256]{2,1,0:T(8,128)S(1)} %get-tuple-element.7.own) | copy-start | bytes 3145732
  70.0 4.5 %collective-permute-start.14 = (f32[8,128,256]{2,1,0:T(8,128)}, f32[8,128,256]{2,1,0:T(8,128)S(1)}, u32[]{:S(2)}, u32[]{:S(2)}) collective-permute-start(f32[8,128,256]{2,1,0:T(8,128)} %get-tuple-element.8), channel_id=1, source_target_pairs={{0,1},{1,0},{2,3},{3,2},{4,5},{5,4},{6,7},{7,6},{8,9},{9,8},{10,11... | collective-permute-start | bytes 3145736 | tf_op jit(solution)/shard_map/ppermute | solution.py:51
  (2 other events, 1.8 us)

commit v3 on v2

v3 whole, which is shorter than its diff:
```python
import functools

import jax
import jax.numpy as jnp
from jax import lax
from jax.experimental import pallas as pl
from jax.experimental.pallas import tpu as pltpu
from jax.sharding import PartitionSpec as P

BLK = 128
RB = 8
CB = 4
KP = 4
SIDE = 4
META = 16
HALF = 8
DATA = HALF * BLK
ROWS = DATA + META
MOST = 64
LISTS = 8
NONE = 128 * 128
DELTA = (0, SIDE - 1, 1, 2)
LIMIT = 60 * 1024 * 1024


def move_a(value, distance, phase):
    pairs = []
    for x in range(SIDE):
        for y in range(SIDE):
            for core in range(2):
                along_y = (core == 0) == (phase == 0)
                tx = x if along_y else (x + distance) % SIDE
                ty = (y + distance) % SIDE if along_y else y
                pairs.append(((x * SIDE + y) * 2 + core, (tx * SIDE + ty) * 2 + core))
    return lax.ppermute(value, ("row", "layer"), pairs)


def move_b(value, depth):
    pairs = []
    for z in range(depth):
        pairs.append((z * 2, ((z + 1) % depth) * 2))
        pairs.append((z * 2 + 1, ((z - 1) % depth) * 2 + 1))
    return lax.ppermute(value, ("col", "layer"), pairs)


def swap(value):
    return lax.ppermute(value, "layer", [(0, 1), (1, 0)])


def pack(a_rows, a_cols, b_rows, b_cols, a_blocks, b_blocks, a_out, b_first, b_second, sem):
    core = lax.axis_index("layer")
    copies = []
    for s in range(HALF):
        copies.append(
            pltpu.make_async_copy(
                a_blocks.at[0, 0, 2 * s + core], a_out.at[pl.ds(s * BLK, BLK)], sem.at[s]
            )
        )
    for i, out in enumerate((b_first, b_second)):
        for t in range(HALF):
            copies.append(
                pltpu.make_async_copy(
                    b_blocks.at[i, 0, t], out.at[pl.ds(t * BLK, BLK)], sem.at[8 + 8 * i + t]
                )
            )
    for copy in copies:
        copy.start()
    line = lax.broadcasted_iota(jnp.int32, (META, BLK), 0)
    numbers = jnp.zeros((META, BLK), jnp.int32)
    for s in range(HALF):
        numbers = jnp.where(line == s, a_rows[0, 0, 2 * s + core], numbers)
        numbers = jnp.where(line == HALF + s, a_cols[0, 0, 2 * s + core] * CB, numbers)
    a_out[DATA:ROWS, :] = numbers.astype(jnp.float32).astype(jnp.bfloat16)
    for i, out in enumerate((b_first, b_second)):
        numbers = jnp.zeros((META, BLK), jnp.int32)
        for t in range(HALF):
            numbers = jnp.where(line == t, b_rows[i, 0, t] * CB + b_cols[i, 0, t], numbers)
        out[DATA:ROWS, :] = numbers.astype(jnp.float32).astype(jnp.bfloat16)
    for copy in copies:
        copy.wait()


def packed(a_blocks, a_rows, a_cols, b_blocks, b_rows, b_cols):
    vmem = pl.BlockSpec(memory_space=pltpu.VMEM)
    smem = pl.BlockSpec(memory_space=pltpu.SMEM)
    anywhere = pl.BlockSpec(memory_space=pl.ANY)
    tile = jax.ShapeDtypeStruct((ROWS, BLK), jnp.bfloat16)
    return pl.pallas_call(
        pack,
        out_shape=(tile, tile, tile),
        in_specs=[smem] * 4 + [anywhere] * 2,
        out_specs=(vmem,) * 3,
        scratch_shapes=[pltpu.SemaphoreType.DMA((24,))],
        name="pack",
    )(a_rows, a_cols, b_rows, b_cols, a_blocks, b_blocks)


def multiply(groups, items, from_tiles, added, place, keep, *refs):
    x, y, z, core = place[0], place[1], place[2], place[3]
    panels = [(g, m) for g, ms in groups for m in ms]
    n_a = len(groups)
    a_refs, refs = refs[:n_a], refs[n_a:]
    n_b = 1 if from_tiles else 16
    b_refs, refs = refs[:n_b], refs[n_b:]
    if added:
        (send_in, own_in), refs = refs[:2], refs[2:]
    send, own = refs[:2]
    refs = refs[2:]
    if not from_tiles:
        tiles, refs = refs[0], refs[1:]
    av, bv, am, bm, keys, list_v, lists, data_sem, meta_sem, list_sem, add_sem = refs
    spots = []
    for p, (g, m) in enumerate(panels):
        px = (x + jnp.where(core == 0, DELTA[g], DELTA[m])) % SIDE
        py = (y + jnp.where(core == 0, DELTA[m], DELTA[g])) % SIDE
        k = (px * SIDE + py + 2 * z) % 16
        q = (k - (x * SIDE + y) + 16) % 16
        spots.append((k, ((q // 2 - z + 8) % 8) * 2 + q % 2))
    sources = []
    at = 0
    for (g, ms), ref in zip(groups, a_refs):
        sources.append((ref, av, am, at, len(ms)))
        at += len(ms)
    if from_tiles:
        for p, (k, spot) in enumerate(spots):
            sources.append((b_refs[0].at[pl.ds(spot, 1)], bv, bm, p, 1))
    else:
        sources.append((b_refs[0], bv, bm, 0, 1))
        sources.append((b_refs[1], bv, bm, 1, 1))
        for t in range(1, 4):
            for i in range(2):
                up = 2 * jnp.where(core == 0, 8 - t, t) + i
                down = 2 * jnp.where(core == 0, t, 8 - t) + i
                sources.append((b_refs[2 * t + i], bv, bm, up, 1))
                sources.append((b_refs[6 + 2 * t + i], bv, bm, down, 1))
        sources.append((b_refs[14], bv, bm, 8 + core, 1))
        sources.append((b_refs[15], bv, bm, 9 - core, 1))
    copies, metas = [], []
    for n, (ref, held, meta, at, count) in enumerate(sources):
        copies.append(
            pltpu.make_async_copy(
                ref.at[:, pl.ds(0, DATA), :], held.at[pl.ds(at, count)], data_sem.at[n]
            )
        )
        metas.append(
            pltpu.make_async_copy(
                ref.at[:, pl.ds(DATA, META), :], meta.at[pl.ds(at, count)], meta_sem.at[n]
            )
        )
    for copy in metas:
        copy.start()
    for copy in copies:
        copy.start()
    if added:
        adds = [
            pltpu.make_async_copy(send_in, send, add_sem.at[0]),
            pltpu.make_async_copy(own_in, own, add_sem.at[1]),
        ]
        for copy in adds:
            copy.start()
    none_a = len(panels)
    av[none_a, 0:BLK, :] = jnp.zeros((BLK, BLK), jnp.bfloat16)
    none = float(none_a * HALF * 128)
    lane = lax.broadcasted_iota(jnp.int32, (HALF, BLK), 1)
    slot = lax.broadcasted_iota(jnp.int32, (HALF, BLK), 0).astype(jnp.float32)
    bucket_row = (lane // CB).astype(jnp.float32)
    bucket_col = (lane % CB).astype(jnp.float32)
    for copy in metas:
        copy.wait()
    count = jnp.zeros((HALF, BLK), jnp.float32)
    for p, (k, spot) in enumerate(spots):
        if from_tiles:
            spot = jnp.int32(p)
        numbers = am[p].astype(jnp.float32)
        wanted = numbers[HALF:, :] + bucket_col
        b_numbers = bm[spot].astype(jnp.float32)
        found = jnp.zeros((HALF, BLK), jnp.float32)
        for t in range(HALF):
            found = jnp.where(b_numbers[t : t + 1, :] == wanted, t + 1.0, found)
        kept = keep[pl.ds(k, 1), :].astype(jnp.float32)
        valid = jnp.where(numbers[:HALF, :] == bucket_row, kept, 0.0)
        valid = (valid != 0.0) & (found != 0.0)
        base = (p * HALF * 128 - 1 + spot * HALF).astype(jnp.float32)
        keys[p] = jnp.where(valid, base + slot * 128.0 + found, none)
        count = count + jnp.where(valid, 1.0, 0.0)
    count = jnp.sum(count, axis=0, keepdims=True)
    list_v[0:1, :] = count.astype(jnp.int32)
    largest = jnp.max(count).astype(jnp.int32)

    def pick(j):
        least = keys[0]
        for p in range(1, len(panels)):
            least = jnp.minimum(least, keys[p])
        least = jnp.min(least, axis=0, keepdims=True)
        list_v[pl.ds(1 + j, 1), :] = least.astype(jnp.int32)
        for p in range(len(panels)):
            keys[p] = jnp.where(keys[p] == least, none, keys[p])

    for j in range(items):
        pick(j)
    near = pltpu.make_async_copy(
        list_v.at[pl.ds(0, LISTS)], lists.at[pl.ds(0, LISTS)], list_sem.at[0]
    )
    near.start()
    near.wait()
    for copy in copies:
        copy.wait()
    if added:
        for copy in adds:
            copy.wait()
    else:
        keeping = pltpu.make_async_copy(bv, tiles.at[:, pl.ds(0, DATA), :], add_sem.at[0])
        keeping.start()
        keeping_meta = pltpu.make_async_copy(bm, tiles.at[:, pl.ds(DATA, META), :], add_sem.at[1])
        keeping_meta.start()

    def product(b, start, length):
        left, right = [], []
        for j in range(length):
            code = lists[1 + start + j, b]
            ia, ib = code // 128, code % 128
            left.append(av[ia // HALF, pl.ds(pl.multiple_of((ia % HALF) * BLK, BLK), BLK), :])
            right.append(bv[ib // HALF, pl.ds(pl.multiple_of((ib % HALF) * BLK, BLK), BLK), :])
        return jnp.dot(
            jnp.concatenate(left, axis=1),
            jnp.concatenate(right, axis=0),
            preferred_element_type=jnp.float32,
        )

    outs = ((send, 2 * (1 - core)), (own, 2 * core))
    for r in range(RB):
        for ref, base in outs:
            for n in range(2):
                cols = slice(n * BLK, (n + 1) * BLK)
                result = product(r * CB + base + n, 0, items)
                ref[r, :, cols] = ref[r, :, cols] + result if added else result

    @pl.when(largest > items)
    def _():
        def more(j, carry):
            pick(j)
            return carry

        lax.fori_loop(items, largest, more, 0)
        far = pltpu.make_async_copy(list_v, lists, list_sem.at[1])
        far.start()
        far.wait()

        def rest_of_row(r, carry):
            for ref, base in outs:
                for n in range(2):
                    b = r * CB + base + n

                    def one(j, inner):
                        ref[r, :, n * BLK : (n + 1) * BLK] += product(b, j, 1)
                        return inner

                    lax.fori_loop(items, jnp.maximum(lists[0, b], items), one, 0)
            return carry

        lax.fori_loop(0, RB, rest_of_row, 0)

    if not added:
        keeping.wait()
        keeping_meta.wait()


def partial_sums(place, keep, groups, items, a_parts, b_parts, before=None):
    vmem = pl.BlockSpec(memory_space=pltpu.VMEM)
    smem = pl.BlockSpec(memory_space=pltpu.SMEM)
    anywhere = pl.BlockSpec(memory_space=pl.ANY)
    n_panels = sum(len(ms) for _, ms in groups)
    added = before is not None
    n_b = n_panels if added else 16
    half = jax.ShapeDtypeStruct((RB, BLK, 2 * BLK), jnp.float32)
    out_shape, out_specs = [half, half], [vmem, vmem]
    if not added:
        out_shape.append(jax.ShapeDtypeStruct((16, ROWS, BLK), jnp.bfloat16))
        out_specs.append(anywhere)
    extra = list(before) if added else []
    n_sources = len(a_parts) + (n_panels if added else 16)
    return pl.pallas_call(
        functools.partial(multiply, groups, items, added, added),
        out_shape=out_shape,
        in_specs=[smem, vmem] + [anywhere] * (len(a_parts) + len(b_parts) + len(extra)),
        out_specs=out_specs,
        scratch_shapes=[
            pltpu.VMEM((n_panels + 1, DATA, BLK), jnp.bfloat16),
            pltpu.VMEM((n_b, DATA, BLK), jnp.bfloat16),
            pltpu.VMEM((n_panels, META, BLK), jnp.bfloat16),
            pltpu.VMEM((n_b, META, BLK), jnp.bfloat16),
            pltpu.VMEM((n_panels, HALF, BLK), jnp.float32),
            pltpu.VMEM((LISTS + MOST, BLK), jnp.int32),
            pltpu.SMEM((LISTS + MOST, BLK), jnp.int32),
            pltpu.SemaphoreType.DMA((n_sources,)),
            pltpu.SemaphoreType.DMA((n_sources,)),
            pltpu.SemaphoreType.DMA((2,)),
            pltpu.SemaphoreType.DMA((2,)),
        ],
        compiler_params=pltpu.CompilerParams(vmem_limit_bytes=LIMIT),
        name="late" if added else "early",
    )(place, keep, *a_parts, *b_parts, *extra)


def finish(keep, own, other, out):
    for r in range(RB):
        for n in range(2):
            cols = slice(n * BLK, (n + 1) * BLK)
            total = own[r, :, cols] + other[r, :, cols]
            total = total * keep[r, n].astype(jnp.float32)
            out[r * BLK : (r + 1) * BLK, cols] = total.astype(jnp.bfloat16)


def filtered(keep, own, other):
    vmem = pl.BlockSpec(memory_space=pltpu.VMEM)
    return pl.pallas_call(
        finish,
        out_shape=jax.ShapeDtypeStruct((RB * BLK, 2 * BLK), jnp.bfloat16),
        in_specs=[pl.BlockSpec(memory_space=pltpu.SMEM), vmem, vmem],
        out_specs=vmem,
        compiler_params=pltpu.CompilerParams(vmem_limit_bytes=LIMIT),
        name="finish",
    )(keep, own, other)


def body(a_blocks, a_rows, a_cols, b_blocks, b_rows, b_cols, prod_keep, res_keep):
    depth = lax.axis_size("col")
    row = lax.axis_index("row")
    z = lax.axis_index("col")
    core = lax.axis_index("layer")
    place = jnp.stack([row // SIDE, row % SIDE, z, core]).astype(jnp.int32)
    keep = prod_keep.transpose(1, 0, 2).reshape(16, RB * CB)
    keep = jnp.pad(keep, ((0, 0), (0, BLK - RB * CB)))

    a_mine, b_first, b_second = packed(a_blocks, a_rows, a_cols, b_blocks, b_rows, b_cols)

    mine = [[b_first[None], b_second[None]]]
    for _ in range(3):
        mine.append([move_b(part, depth) for part in mine[-1]])
    last = move_b(jnp.where(core == 0, mine[3][0], mine[3][1]), depth)
    theirs = [[swap(part) for part in pair] for pair in mine[1:]]
    b_parts = [part for pair in mine + theirs for part in pair] + [last, swap(last)]

    a_own = jnp.stack([a_mine] + [move_a(a_mine, d, 0) for d in (1, -1, 2)])
    a_up, a_down = move_a(a_own, 1, 1), move_a(a_own, -1, 1)
    a_far = [move_a(a_up[:2], 1, 1), move_a(a_down[2:], -1, 1)]

    whole = (0, 1, 2, 3)
    send, own, tiles = partial_sums(
        place, keep, ((0, whole), (1, whole), (2, whole)), 4, [a_own, a_up, a_down], b_parts
    )
    send, own = partial_sums(
        place, keep, ((3, (0, 1)), (3, (2, 3))), 2, a_far, [tiles], (send, own)
    )
    return filtered(res_keep, own, swap(send))


def solution(mesh):
    return jax.shard_map(
        body,
        mesh=mesh,
        in_specs=(
            P("col", "row", None, None, None),
            P("col", "row", None),
            P("col", "row", None),
            P("col", "row", None, None, None),
            P("col", "row", None),
            P("col", "row", None),
            P("col", None, "row"),
            P("col", ("row", "layer")),
        ),
        out_specs=P("col", ("row", "layer")),
        check_vma=False,
    )
```

time: 78.3 us -> 80.3 us (1.026)
  the two profiles are of different devices: /device:TPU:133 before, /device:TPU:1 now
where the time goes in v3:
time: 80.3 us; the launch traced here: 79.8 us
  starting transfers between devices  41.1 us (51%)
  Pallas kernels  24 us (30%)
  waiting for transfers between devices  6.6 us (8%)
  local copies, waits for them, and re-layouts  5.21 us (6%)
  other arithmetic  2.66 us (3%)
    ppermute x7, starting transfers between devices, move_b(): return lax.ppermute(value, ('col', 'layer'), pairs)  19.4 us
    pallas_call x2, Pallas kernels, partial_sums(): pl.pallas_call(functools.partial(multiply, groups, items, added, added),...  18.7 us
    ppermute x7, starting transfers between devices, move_a(): return lax.ppermute(value, ('row', 'layer'), pairs)  10.9 us
    ppermute x8, starting transfers between devices, swap(): return lax.ppermute(value, 'layer', [(0, 1), (1, 0)])  10.8 us
    ppermute x7, waiting for transfers between devices, move_b(): return lax.ppermute(value, ('col', 'layer'), pairs)  3.87 us
    pallas_call x1, Pallas kernels, packed(): pl.pallas_call(pack, out_shape=(tile, tile, tile), in_specs=[smem] * 4 +...  2.89 us
    unnamed x31, local copies, waits for them, and re-layouts  2.69 us
    pallas_call x1, Pallas kernels, filtered(): pl.pallas_call(finish, out_shape=jax.ShapeDtypeStruct((RB * BLK, 2 * BLK)...  2.46 us
  transfers between devices with their start and end apart: 22, of which 6 were waited for; matrix products, arithmetic and copies ran while one was open for 7% of the time, Pallas kernels for 13%

profile of v3, /device:TPU:1, one launch (start us, length us, event | category | flops | bytes accessed | tf_op | source)
XLA Modules:
  0.0 79.8 jit_solution(15463096318291022008)
XLA Ops:
  0.0 2.9 %pack.1 = (bf16[1040,128]{1,0:T(8,128)(2,1)}, bf16[1040,128]{1,0:T(8,128)(2,1)}, bf16[1040,128]{1,0:T(8,128)(2,1)}) custom-call(s32[1,1,16]{2,1,0:T(1,128)} %a_rows.1, s32[1,1,16]{2,1,0:T(1,128)} %a_cols.1, s32[2,1,8]{2,1,0:T(1,128)} %b_rows.1, s32[2,1,8]{2,1,0:T(1,128)} %b_cols.1, bf16[1,1,16,128,128]{4,3,2,1,0:T(8,128)(2,1)} %a_blocks.1, ...), custom_call_target="tpu_custom_call" | custom-call | tf_op jit(solution)/shard_map/pack/pallas_call | solution.py:88
  2.9 2.1 %collective-permute-start = (bf16[1040,128]{1,0:T(8,128)(2,1)}, bf16[1040,128]{1,0:T(8,128)(2,1)S(1)}, u32[]{:S(2)}, u32[]{:S(2)}) collective-permute-start(bf16[1040,128]{1,0:T(8,128)(2,1)} %get-tuple-element.13), channel_id=1, source_target_pairs={{0,16},{1,65},{16,32},{17,81},{32,48},{33,97},{48,0},{49,113},{64,... | collective-permute-start | bytes 798728 | tf_op jit(solution)/shard_map/ppermute | solution.py:35
  5.0 1.4 %collective-permute-start.1 = (bf16[1040,128]{1,0:T(8,128)(2,1)}, bf16[1040,128]{1,0:T(8,128)(2,1)S(1)}, u32[]{:S(2)}, u32[]{:S(2)}) collective-permute-start(bf16[1040,128]{1,0:T(8,128)(2,1)} %get-tuple-element.13), channel_id=1, source_target_pairs={{0,48},{1,193},{16,0},{17,209},{32,16},{33,225},{48,32},{49,241},{... | collective-permute-start | bytes 798728 | tf_op jit(solution)/shard_map/ppermute | solution.py:35
  6.4 1.6 %collective-permute-start.2 = (bf16[1040,128]{1,0:T(8,128)(2,1)}, bf16[1040,128]{1,0:T(8,128)(2,1)S(1)}, u32[]{:S(2)}, u32[]{:S(2)}) collective-permute-start(bf16[1040,128]{1,0:T(8,128)(2,1)} %get-tuple-element.13), channel_id=1, source_target_pairs={{0,32},{1,129},{16,48},{17,145},{32,0},{33,161},{48,16},{49,177},{... | collective-permute-start | bytes 798728 | tf_op jit(solution)/shard_map/ppermute | solution.py:35
  8.0 5.6 %collective-permute-start.7 = (bf16[1,1040,128]{2,1,0:T(8,128)(2,1)}, bf16[1,1040,128]{2,1,0:T(8,128)(2,1)S(1)}, u32[]{:S(2)}, u32[]{:S(2)}) collective-permute-start(bf16[1,1040,128]{2,1,0:T(8,128)(2,1)} %bitcast.13), channel_id=1, source_target_pairs={{0,2},{1,15},{2,4},{3,1},{4,6},{5,3},{6,8},{7,5},{8,10},{9,7},{10,... | collective-permute-start | bytes 798728 | tf_op jit(solution)/shard_map/ppermute | solution.py:43
  14.6 1.1 %pad_maximum_fusion.refs_0_ = bf16[4,1040,128]{2,1,0:T(8,128)(2,1)S(1)} fusion(bf16[1,1040,128]{2,1,0:T(8,128)(2,1)S(1)} %bitcast.20, bf16[1,1040,128]{2,1,0:T(8,128)(2,1)S(1)} %bitcast.19, bf16[1,1040,128]{2,1,0:T(8,128)(2,1)S(1)} %bitcast.18, bf16[1,1040,128]{2,1,0:T(8,128)(2,1)} %bitcast.17), kind=kLoop, calls=%fused_computation | loop fusion | flops 1597440 | bytes 2129920 | tf_op jit(solution)/shard_map/stack | solution.py:344
  15.7 1.1 %collective-permute-start.3 = (bf16[4,1040,128]{2,1,0:T(8,128)(2,1)S(1)}, bf16[4,1040,128]{2,1,0:T(8,128)(2,1)S(1)}, u32[]{:S(2)}, u32[]{:S(2)}) collective-permute-start(bf16[4,1040,128]{2,1,0:T(8,128)(2,1)S(1)} %pad_maximum_fusion.refs_0_), channel_id=1, source_target_pairs={{0,64},{1,17},{16,80},{17,33},{32,96},{33,49},{48,112},{49,1},{64,... | collective-permute-start | bytes 3194888 | tf_op jit(solution)/shard_map/ppermute | solution.py:35
  16.8 1.8 %collective-permute-start.5 = (bf16[4,1040,128]{2,1,0:T(8,128)(2,1)S(1)}, bf16[4,1040,128]{2,1,0:T(8,128)(2,1)S(1)}, u32[]{:S(2)}, u32[]{:S(2)}) collective-permute-start(bf16[4,1040,128]{2,1,0:T(8,128)(2,1)S(1)} %pad_maximum_fusion.refs_0_), channel_id=1, source_target_pairs={{0,192},{1,49},{16,208},{17,1},{32,224},{33,17},{48,240},{49,33},{... | collective-permute-start | bytes 3194888 | tf_op jit(solution)/shard_map/ppermute | solution.py:35
  18.6 5.6 %collective-permute-start.9 = (bf16[1,1040,128]{2,1,0:T(8,128)(2,1)S(1)}, bf16[1,1040,128]{2,1,0:T(8,128)(2,1)}, u32[]{:S(2)}, u32[]{:S(2)}) collective-permute-start(bf16[1,1040,128]{2,1,0:T(8,128)(2,1)S(1)} %collective-permute-done.7.refs_5_), channel_id=1, source_target_pairs={{0,2},{1,15},{2,4},{3,1},{4,6},{5,3},{6,8},{7,5},{8,10},{9,7},{10,... | collective-permute-start | bytes 798728 | tf_op jit(solution)/shard_map/ppermute | solution.py:43
  24.9 2.6 %collective-permute-done.9.refs_7_ = bf16[1,1040,128]{2,1,0:T(8,128)(2,1)} collective-permute-done((bf16[1,1040,128]{2,1,0:T(8,128)(2,1)S(1)}, bf16[1,1040,128]{2,1,0:T(8,128)(2,1)}, u32[]{:S(2)}, u32[]{:S(2)}) %collective-permute-start.9) | collective-permute-done | bytes 266272 | tf_op jit(solution)/shard_map/ppermute | solution.py:43
  27.6 3.4 %collective-permute-start.11 = (bf16[1,1040,128]{2,1,0:T(8,128)(2,1)}, bf16[1,1040,128]{2,1,0:T(8,128)(2,1)S(1)}, u32[]{:S(2)}, u32[]{:S(2)}) collective-permute-start(bf16[1,1040,128]{2,1,0:T(8,128)(2,1)} %collective-permute-done.9.refs_7_), channel_id=1, source_target_pairs={{0,2},{1,15},{2,4},{3,1},{4,6},{5,3},{6,8},{7,5},{8,10},{9,7},{10,... | collective-permute-start | bytes 798728 | tf_op jit(solution)/shard_map/ppermute | solution.py:43
  31.0 2.8 %collective-permute-start.12 = (bf16[1,1040,128]{2,1,0:T(8,128)(2,1)}, bf16[1,1040,128]{2,1,0:T(8,128)(2,1)}, u32[]{:S(2)}, u32[]{:S(2)}) collective-permute-start(bf16[1,1040,128]{2,1,0:T(8,128)(2,1)} %collective-permute-done.10.refs_8_), channel_id=1, source_target_pairs={{0,2},{1,15},{2,4},{3,1},{4,6},{5,3},{6,8},{7,5},{8,10},{9,7},{10,... | collective-permute-start | bytes 798728 | tf_op jit(solution)/shard_map/ppermute | solution.py:43
  34.7 4.4 %collective-permute-start.14 = (bf16[1,1040,128]{2,1,0:T(8,128)(2,1)}, bf16[1,1040,128]{2,1,0:T(8,128)(2,1)S(1)}, u32[]{:S(2)}, u32[]{:S(2)}) collective-permute-start(bf16[1,1040,128]{2,1,0:T(8,128)(2,1)} %copy-done.8), channel_id=1, source_target_pairs={{0,1},{1,0},{2,3},{3,2},{4,5},{5,4},{6,7},{7,6},{8,9},{9,8},{10,11... | collective-permute-start | bytes 798728 | tf_op jit(solution)/shard_map/ppermute | solution.py:47
  39.0 3.0 %collective-permute-start.15 = (bf16[1,1040,128]{2,1,0:T(8,128)(2,1)}, bf16[1,1040,128]{2,1,0:T(8,128)(2,1)S(1)}, u32[]{:S(2)}, u32[]{:S(2)}) collective-permute-start(bf16[1,1040,128]{2,1,0:T(8,128)(2,1)} %collective-permute-done.9.refs_7_), channel_id=1, source_target_pairs={{0,1},{1,0},{2,3},{3,2},{4,5},{5,4},{6,7},{7,6},{8,9},{9,8},{10,11... | collective-permute-start | bytes 798728 | tf_op jit(solution)/shard_map/ppermute | solution.py:47
  42.0 1.0 %broadcast_select_fusion = bf16[1,1040,128]{2,1,0:T(8,128)(2,1)S(1)} fusion(bf16[1,1040,128]{2,1,0:T(8,128)(2,1)S(1)} %collective-permute-done.11.refs_9_, bf16[1,1040,128]{2,1,0:T(8,128)(2,1)} %collective-permute-done.12.refs_10_, pred[]{:T(512)S(6)} %eq.5), kind=kLoop, calls=%fused_computation.1 | loop fusion | flops 133120 | bytes 798721 | tf_op jit(solution)/shard_map/jit(_where)/select_n | solution.py:340
  43.1 1.0 %slice.8 = bf16[2,1040,128]{2,1,0:T(8,128)(2,1)} slice(bf16[4,1040,128]{2,1,0:T(8,128)(2,1)S(1)} %collective-permute-done.3.refs_1_), slice={[0:2], [0:1040], [0:128]} | slice | bytes 1064960 | tf_op jit(solution)/shard_map/slice | solution.py:346
  45.5 1.4 %collective-permute-start.4 = (bf16[2,1040,128]{2,1,0:T(8,128)(2,1)}, bf16[2,1040,128]{2,1,0:T(8,128)(2,1)S(1)}, u32[]{:S(2)}, u32[]{:S(2)}) collective-permute-start(bf16[2,1040,128]{2,1,0:T(8,128)(2,1)} %slice.8), channel_id=1, source_target_pairs={{0,64},{1,17},{16,80},{17,33},{32,96},{33,49},{48,112},{49,1},{64,... | collective-permute-start | bytes 1597448 | tf_op jit(solution)/shard_map/ppermute | solution.py:35
  46.9 1.5 %collective-permute-start.6 = (bf16[2,1040,128]{2,1,0:T(8,128)(2,1)}, bf16[2,1040,128]{2,1,0:T(8,128)(2,1)S(1)}, u32[]{:S(2)}, u32[]{:S(2)}) collective-permute-start(bf16[2,1040,128]{2,1,0:T(8,128)(2,1)} %slice.9), channel_id=1, source_target_pairs={{0,192},{1,49},{16,208},{17,1},{32,224},{33,17},{48,240},{49,33},{... | collective-permute-start | bytes 1597448 | tf_op jit(solution)/shard_map/ppermute | solution.py:35
  49.8 2.4 %collective-permute-start.20 = (bf16[1,1040,128]{2,1,0:T(8,128)(2,1)}, bf16[1,1040,128]{2,1,0:T(8,128)(2,1)}, u32[]{:S(2)}, u32[]{:S(2)}) collective-permute-start(bf16[1,1040,128]{2,1,0:T(8,128)(2,1)} %collective-permute-done.19.refs_17_), channel_id=1, source_target_pairs={{0,1},{1,0},{2,3},{3,2},{4,5},{5,4},{6,7},{7,6},{8,9},{9,8},{10,11... | collective-permute-start | bytes 798728 | tf_op jit(solution)/shard_map/ppermute | solution.py:47
  53.7 10.7 %early.1 = (f32[8,128,256]{2,1,0:T(8,128)}, f32[8,128,256]{2,1,0:T(8,128)}, bf16[16,1040,128]{2,1,0:T(8,128)(2,1)}) custom-call(s32[4]{0:T(128)} %pad_add_fusion.place, s32[16,128]{1,0:T(8,128)} %pad.4.keep, bf16[4,1040,128]{2,1,0:T(8,128)(2,1)} %copy-done, bf16[4,1040,128]{2,1,0:T(8,128)(2,1)} %copy-done.1, bf16[4,1040,128]{2,1,0:T(8,128)(2,1)} %copy-done.2, ...), custom_call_target="tpu_custom_call" | custom-call | tf_op jit(solution)/shard_map/early/pallas_call | solution.py:282
  65.4 8.0 %late.1 = (f32[8,128,256]{2,1,0:T(8,128)}, f32[8,128,256]{2,1,0:T(8,128)}) custom-call(s32[4]{0:T(128)} %pad_add_fusion.place, s32[16,128]{1,0:T(8,128)} %pad.4.keep, bf16[2,1040,128]{2,1,0:T(8,128)(2,1)} %copy-done.5, bf16[2,1040,128]{2,1,0:T(8,128)(2,1)} %copy-done.6, bf16[16,1040,128]{2,1,0:T(8,128)(2,1)} %get-tuple-element.16.refs_2_, ...), custom_call_target="tpu_custom_call" | custom-call | tf_op jit(solution)/shard_map/late/pallas_call | solution.py:282
  74.1 2.2 %collective-permute-done.21.other = f32[8,128,256]{2,1,0:T(8,128)S(1)} collective-permute-done((f32[8,128,256]{2,1,0:T(8,128)}, f32[8,128,256]{2,1,0:T(8,128)S(1)}, u32[]{:S(2)}, u32[]{:S(2)}) %collective-permute-start.21) | collective-permute-done | bytes 1048608 | tf_op jit(solution)/shard_map/ppermute | solution.py:47
  76.3 1.0 %copy-done.4 = f32[8,128,256]{2,1,0:T(8,128)} copy-done((f32[8,128,256]{2,1,0:T(8,128)}, f32[8,128,256]{2,1,0:T(8,128)S(1)}, u32[]{:S(2)}) %copy-start.4) | copy-done | bytes 1048600
  77.3 2.5 %finish.1 = bf16[1024,256]{1,0:T(8,128)(2,1)} custom-call(s32[8,2]{1,0:T(8,128)} %copy.12.keep, f32[8,128,256]{2,1,0:T(8,128)} %get-tuple-element.19.own, f32[8,128,256]{2,1,0:T(8,128)} %copy-done.4), custom_call_target="tpu_custom_call" | custom-call | tf_op jit(solution)/shard_map/finish/pallas_call | solution.py:316
  (62 shorter events, 8.7 us)
Async XLA Ops:
  2.9 11.4 %collective-permute-start = (bf16[1040,128]{1,0:T(8,128)(2,1)}, bf16[1040,128]{1,0:T(8,128)(2,1)S(1)}, u32[]{:S(2)}, u32[]{:S(2)}) collective-permute-start(bf16[1040,128]{1,0:T(8,128)(2,1)} %get-tuple-element.13), channel_id=1, source_target_pairs={{0,16},{1,65},{16,32},{17,81},{32,48},{33,97},{48,0},{49,113},{64,... | collective-permute-start | bytes 798728 | tf_op jit(solution)/shard_map/ppermute | solution.py:35
  5.0 9.3 %collective-permute-start.1 = (bf16[1040,128]{1,0:T(8,128)(2,1)}, bf16[1040,128]{1,0:T(8,128)(2,1)S(1)}, u32[]{:S(2)}, u32[]{:S(2)}) collective-permute-start(bf16[1040,128]{1,0:T(8,128)(2,1)} %get-tuple-element.13), channel_id=1, source_target_pairs={{0,48},{1,193},{16,0},{17,209},{32,16},{33,225},{48,32},{49,241},{... | collective-permute-start | bytes 798728 | tf_op jit(solution)/shard_map/ppermute | solution.py:35
  6.4 8.3 %collective-permute-start.2 = (bf16[1040,128]{1,0:T(8,128)(2,1)}, bf16[1040,128]{1,0:T(8,128)(2,1)S(1)}, u32[]{:S(2)}, u32[]{:S(2)}) collective-permute-start(bf16[1040,128]{1,0:T(8,128)(2,1)} %get-tuple-element.13), channel_id=1, source_target_pairs={{0,32},{1,129},{16,48},{17,145},{32,0},{33,161},{48,16},{49,177},{... | collective-permute-start | bytes 798728 | tf_op jit(solution)/shard_map/ppermute | solution.py:35
  8.0 10.6 %collective-permute-start.7 = (bf16[1,1040,128]{2,1,0:T(8,128)(2,1)}, bf16[1,1040,128]{2,1,0:T(8,128)(2,1)S(1)}, u32[]{:S(2)}, u32[]{:S(2)}) collective-permute-start(bf16[1,1040,128]{2,1,0:T(8,128)(2,1)} %bitcast.13), channel_id=1, source_target_pairs={{0,2},{1,15},{2,4},{3,1},{4,6},{5,3},{6,8},{7,5},{8,10},{9,7},{10,... | collective-permute-start | bytes 798728 | tf_op jit(solution)/shard_map/ppermute | solution.py:43
  13.6 10.6 %collective-permute-start.8 = (bf16[1,1040,128]{2,1,0:T(8,128)(2,1)}, bf16[1,1040,128]{2,1,0:T(8,128)(2,1)S(1)}, u32[]{:S(2)}, u32[]{:S(2)}) collective-permute-start(bf16[1,1040,128]{2,1,0:T(8,128)(2,1)} %bitcast.15), channel_id=1, source_target_pairs={{0,2},{1,15},{2,4},{3,1},{4,6},{5,3},{6,8},{7,5},{8,10},{9,7},{10,... | collective-permute-start | bytes 798728 | tf_op jit(solution)/shard_map/ppermute | solution.py:43
  15.7 29.8 %copy-start = (bf16[4,1040,128]{2,1,0:T(8,128)(2,1)}, bf16[4,1040,128]{2,1,0:T(8,128)(2,1)S(1)}, u32[]{:S(2)}) copy-start(bf16[4,1040,128]{2,1,0:T(8,128)(2,1)S(1)} %pad_maximum_fusion.refs_0_) | copy-start | bytes 3194884
  15.7 27.3 %collective-permute-start.3 = (bf16[4,1040,128]{2,1,0:T(8,128)(2,1)S(1)}, bf16[4,1040,128]{2,1,0:T(8,128)(2,1)S(1)}, u32[]{:S(2)}, u32[]{:S(2)}) collective-permute-start(bf16[4,1040,128]{2,1,0:T(8,128)(2,1)S(1)} %pad_maximum_fusion.refs_0_), channel_id=1, source_target_pairs={{0,64},{1,17},{16,80},{17,33},{32,96},{33,49},{48,112},{49,1},{64,... | collective-permute-start | bytes 3194888 | tf_op jit(solution)/shard_map/ppermute | solution.py:35
  16.8 27.3 %collective-permute-start.5 = (bf16[4,1040,128]{2,1,0:T(8,128)(2,1)S(1)}, bf16[4,1040,128]{2,1,0:T(8,128)(2,1)S(1)}, u32[]{:S(2)}, u32[]{:S(2)}) collective-permute-start(bf16[4,1040,128]{2,1,0:T(8,128)(2,1)S(1)} %pad_maximum_fusion.refs_0_), channel_id=1, source_target_pairs={{0,192},{1,49},{16,208},{17,1},{32,224},{33,17},{48,240},{49,33},{... | collective-permute-start | bytes 3194888 | tf_op jit(solution)/shard_map/ppermute | solution.py:35
  18.6 8.9 %collective-permute-start.9 = (bf16[1,1040,128]{2,1,0:T(8,128)(2,1)S(1)}, bf16[1,1040,128]{2,1,0:T(8,128)(2,1)}, u32[]{:S(2)}, u32[]{:S(2)}) collective-permute-start(bf16[1,1040,128]{2,1,0:T(8,128)(2,1)S(1)} %collective-permute-done.7.refs_5_), channel_id=1, source_target_pairs={{0,2},{1,15},{2,4},{3,1},{4,6},{5,3},{6,8},{7,5},{8,10},{9,7},{10,... | collective-permute-start | bytes 798728 | tf_op jit(solution)/shard_map/ppermute | solution.py:43
  24.2 6.8 %collective-permute-start.10 = (bf16[1,1040,128]{2,1,0:T(8,128)(2,1)S(1)}, bf16[1,1040,128]{2,1,0:T(8,128)(2,1)}, u32[]{:S(2)}, u32[]{:S(2)}) collective-permute-start(bf16[1,1040,128]{2,1,0:T(8,128)(2,1)S(1)} %collective-permute-done.8.refs_6_), channel_id=1, source_target_pairs={{0,2},{1,15},{2,4},{3,1},{4,6},{5,3},{6,8},{7,5},{8,10},{9,7},{10,... | collective-permute-start | bytes 798728 | tf_op jit(solution)/shard_map/ppermute | solution.py:43
  27.6 7.1 %collective-permute-start.11 = (bf16[1,1040,128]{2,1,0:T(8,128)(2,1)}, bf16[1,1040,128]{2,1,0:T(8,128)(2,1)S(1)}, u32[]{:S(2)}, u32[]{:S(2)}) collective-permute-start(bf16[1,1040,128]{2,1,0:T(8,128)(2,1)} %collective-permute-done.9.refs_7_), channel_id=1, source_target_pairs={{0,2},{1,15},{2,4},{3,1},{4,6},{5,3},{6,8},{7,5},{8,10},{9,7},{10,... | collective-permute-start | bytes 798728 | tf_op jit(solution)/shard_map/ppermute | solution.py:43
  31.0 8.0 %collective-permute-start.12 = (bf16[1,1040,128]{2,1,0:T(8,128)(2,1)}, bf16[1,1040,128]{2,1,0:T(8,128)(2,1)}, u32[]{:S(2)}, u32[]{:S(2)}) collective-permute-start(bf16[1,1040,128]{2,1,0:T(8,128)(2,1)} %collective-permute-done.10.refs_8_), channel_id=1, source_target_pairs={{0,2},{1,15},{2,4},{3,1},{4,6},{5,3},{6,8},{7,5},{8,10},{9,7},{10,... | collective-permute-start | bytes 798728 | tf_op jit(solution)/shard_map/ppermute | solution.py:43
  33.8 11.7 %collective-permute-start.13 = (bf16[1,1040,128]{2,1,0:T(8,128)(2,1)}, bf16[1,1040,128]{2,1,0:T(8,128)(2,1)S(1)}, u32[]{:S(2)}, u32[]{:S(2)}) collective-permute-start(bf16[1,1040,128]{2,1,0:T(8,128)(2,1)} %copy-done.7), channel_id=1, source_target_pairs={{0,1},{1,0},{2,3},{3,2},{4,5},{5,4},{6,7},{7,6},{8,9},{9,8},{10,11... | collective-permute-start | bytes 798728 | tf_op jit(solution)/shard_map/ppermute | solution.py:47
  34.7 13.8 %copy-start.3 = (bf16[1,1040,128]{2,1,0:T(8,128)(2,1)}, bf16[1,1040,128]{2,1,0:T(8,128)(2,1)S(1)}, u32[]{:S(2)}) copy-start(bf16[1,1040,128]{2,1,0:T(8,128)(2,1)S(1)} %collective-permute-done.11.refs_9_) | copy-start | bytes 798724
  34.7 12.2 %collective-permute-start.14 = (bf16[1,1040,128]{2,1,0:T(8,128)(2,1)}, bf16[1,1040,128]{2,1,0:T(8,128)(2,1)S(1)}, u32[]{:S(2)}, u32[]{:S(2)}) collective-permute-start(bf16[1,1040,128]{2,1,0:T(8,128)(2,1)} %copy-done.8), channel_id=1, source_target_pairs={{0,1},{1,0},{2,3},{3,2},{4,5},{5,4},{6,7},{7,6},{8,9},{9,8},{10,11... | collective-permute-start | bytes 798728 | tf_op jit(solution)/shard_map/ppermute | solution.py:47
  39.0 9.4 %collective-permute-start.15 = (bf16[1,1040,128]{2,1,0:T(8,128)(2,1)}, bf16[1,1040,128]{2,1,0:T(8,128)(2,1)S(1)}, u32[]{:S(2)}, u32[]{:S(2)}) collective-permute-start(bf16[1,1040,128]{2,1,0:T(8,128)(2,1)} %collective-permute-done.9.refs_7_), channel_id=1, source_target_pairs={{0,1},{1,0},{2,3},{3,2},{4,5},{5,4},{6,7},{7,6},{8,9},{9,8},{10,11... | collective-permute-start | bytes 798728 | tf_op jit(solution)/shard_map/ppermute | solution.py:47
  43.0 6.0 %collective-permute-start.16 = (bf16[1,1040,128]{2,1,0:T(8,128)(2,1)}, bf16[1,1040,128]{2,1,0:T(8,128)(2,1)S(1)}, u32[]{:S(2)}, u32[]{:S(2)}) collective-permute-start(bf16[1,1040,128]{2,1,0:T(8,128)(2,1)} %collective-permute-done.10.refs_8_), channel_id=1, source_target_pairs={{0,1},{1,0},{2,3},{3,2},{4,5},{5,4},{6,7},{7,6},{8,9},{9,8},{10,11... | collective-permute-start | bytes 798728 | tf_op jit(solution)/shard_map/ppermute | solution.py:47
  44.1 5.7 %collective-permute-start.19 = (bf16[1,1040,128]{2,1,0:T(8,128)(2,1)S(1)}, bf16[1,1040,128]{2,1,0:T(8,128)(2,1)}, u32[]{:S(2)}, u32[]{:S(2)}) collective-permute-start(bf16[1,1040,128]{2,1,0:T(8,128)(2,1)S(1)} %broadcast_select_fusion), channel_id=1, source_target_pairs={{0,2},{1,15},{2,4},{3,1},{4,6},{5,3},{6,8},{7,5},{8,10},{9,7},{10,... | collective-permute-start | bytes 798728 | tf_op jit(solution)/shard_map/ppermute | solution.py:43
  45.5 18.9 %collective-permute-start.4 = (bf16[2,1040,128]{2,1,0:T(8,128)(2,1)}, bf16[2,1040,128]{2,1,0:T(8,128)(2,1)S(1)}, u32[]{:S(2)}, u32[]{:S(2)}) collective-permute-start(bf16[2,1040,128]{2,1,0:T(8,128)(2,1)} %slice.8), channel_id=1, source_target_pairs={{0,64},{1,17},{16,80},{17,33},{32,96},{33,49},{48,112},{49,1},{64,... | collective-permute-start | bytes 1597448 | tf_op jit(solution)/shard_map/ppermute | solution.py:35
  46.9 17.5 %collective-permute-start.6 = (bf16[2,1040,128]{2,1,0:T(8,128)(2,1)}, bf16[2,1040,128]{2,1,0:T(8,128)(2,1)S(1)}, u32[]{:S(2)}, u32[]{:S(2)}) collective-permute-start(bf16[2,1040,128]{2,1,0:T(8,128)(2,1)} %slice.9), channel_id=1, source_target_pairs={{0,192},{1,49},{16,208},{17,1},{32,224},{33,17},{48,240},{49,33},{... | collective-permute-start | bytes 1597448 | tf_op jit(solution)/shard_map/ppermute | solution.py:35
  48.4 5.0 %collective-permute-start.17 = (bf16[1,1040,128]{2,1,0:T(8,128)(2,1)S(1)}, bf16[1,1040,128]{2,1,0:T(8,128)(2,1)}, u32[]{:S(2)}, u32[]{:S(2)}) collective-permute-start(bf16[1,1040,128]{2,1,0:T(8,128)(2,1)S(1)} %collective-permute-done.11.refs_9_), channel_id=1, source_target_pairs={{0,1},{1,0},{2,3},{3,2},{4,5},{5,4},{6,7},{7,6},{8,9},{9,8},{10,11... | collective-permute-start | bytes 798728 | tf_op jit(solution)/shard_map/ppermute | solution.py:47
  49.0 4.5 %collective-permute-start.18 = (bf16[1,1040,128]{2,1,0:T(8,128)(2,1)}, bf16[1,1040,128]{2,1,0:T(8,128)(2,1)}, u32[]{:S(2)}, u32[]{:S(2)}) collective-permute-start(bf16[1,1040,128]{2,1,0:T(8,128)(2,1)} %collective-permute-done.12.refs_10_), channel_id=1, source_target_pairs={{0,1},{1,0},{2,3},{3,2},{4,5},{5,4},{6,7},{7,6},{8,9},{9,8},{10,11... | collective-permute-start | bytes 798728 | tf_op jit(solution)/shard_map/ppermute | solution.py:47
  49.8 3.9 %collective-permute-start.20 = (bf16[1,1040,128]{2,1,0:T(8,128)(2,1)}, bf16[1,1040,128]{2,1,0:T(8,128)(2,1)}, u32[]{:S(2)}, u32[]{:S(2)}) collective-permute-start(bf16[1,1040,128]{2,1,0:T(8,128)(2,1)} %collective-permute-done.19.refs_17_), channel_id=1, source_target_pairs={{0,1},{1,0},{2,3},{3,2},{4,5},{5,4},{6,7},{7,6},{8,9},{9,8},{10,11... | collective-permute-start | bytes 798728 | tf_op jit(solution)/shard_map/ppermute | solution.py:47
  73.4 3.0 %collective-permute-start.21 = (f32[8,128,256]{2,1,0:T(8,128)}, f32[8,128,256]{2,1,0:T(8,128)S(1)}, u32[]{:S(2)}, u32[]{:S(2)}) collective-permute-start(f32[8,128,256]{2,1,0:T(8,128)} %get-tuple-element.20), channel_id=1, source_target_pairs={{0,1},{1,0},{2,3},{3,2},{4,5},{5,4},{6,7},{7,6},{8,9},{9,8},{10,11... | collective-permute-start | bytes 3145736 | tf_op jit(solution)/shard_map/ppermute | solution.py:47
  (13 other events, 55.5 us)

commit v4 on v2

v4 whole, which is shorter than its diff:
```python
import jax
import jax.numpy as jnp
from jax import lax
from jax.experimental import pallas as pl
from jax.experimental.pallas import tpu as pltpu
from jax.sharding import PartitionSpec as P

BLK = 128
RB = 8
CB = 4
KP = 4
SIDE = 4
META = 16
HALF = 8
DATA = HALF * BLK
ROWS = DATA + META
MOST = 64
PICKS = 8
NEAR = 16
LISTS = 80
STEP = 8
BUCKETS = 32
NONE = 128
DELTA = (0, SIDE - 1, 1, 2)
STEPS = (1, -1, 2)


def move_a(value, distance, phase):
    pairs = []
    for x in range(SIDE):
        for y in range(SIDE):
            for core in range(2):
                along_y = (core == 0) == (phase == 0)
                tx = x if along_y else (x + distance) % SIDE
                ty = (y + distance) % SIDE if along_y else y
                pairs.append(((x * SIDE + y) * 2 + core, (tx * SIDE + ty) * 2 + core))
    return lax.ppermute(value, ("row", "layer"), pairs)


def move_b(value, distance, depth):
    pairs = []
    for z in range(depth):
        pairs.append((z * 2, ((z + distance) % depth) * 2))
        pairs.append((z * 2 + 1, ((z - distance) % depth) * 2 + 1))
    return lax.ppermute(value, ("col", "layer"), pairs)


def swap(value):
    return lax.ppermute(value, "layer", [(0, 1), (1, 0)])


def pack(
    a_rows, a_cols, b_rows, b_cols, a_blocks, b_blocks, a_out, b_out, ar, ac, br, bc, sem, num_sem
):
    core = lax.axis_index("layer")
    numbers = [
        pltpu.make_async_copy(source, held, num_sem.at[n])
        for n, (source, held) in enumerate(
            ((a_rows, ar), (a_cols, ac), (b_rows, br), (b_cols, bc))
        )
    ]
    for copy in numbers:
        copy.start()
    copies = []
    for i in range(2):
        for t in range(HALF):
            copies.append(
                pltpu.make_async_copy(
                    b_blocks.at[i, 0, t], b_out.at[i, pl.ds(t * BLK, BLK)], sem.at[8 * i + t]
                )
            )
    for s in range(HALF):
        copies.append(
            pltpu.make_async_copy(
                a_blocks.at[0, 0, 2 * s + core], a_out.at[pl.ds(s * BLK, BLK)], sem.at[16 + s]
            )
        )
    for copy in copies:
        copy.start()
    for copy in numbers:
        copy.wait()
    line = lax.broadcasted_iota(jnp.int32, (META, BLK), 0)
    tile = jnp.zeros((META, BLK), jnp.int32)
    for s in range(HALF):
        tile = jnp.where(line == s, ar[0, 0, 2 * s + core], tile)
        tile = jnp.where(line == HALF + s, ac[0, 0, 2 * s + core] * CB, tile)
    a_out[DATA:ROWS, :] = tile.astype(jnp.float32).astype(jnp.bfloat16)
    for i in range(2):
        tile = jnp.zeros((META, BLK), jnp.int32)
        for t in range(HALF):
            tile = jnp.where(line == t, br[i, 0, t] * CB + bc[i, 0, t], tile)
        b_out[i, DATA:ROWS, :] = tile.astype(jnp.float32).astype(jnp.bfloat16)
    for copy in copies:
        copy.wait()


def packed(a_blocks, a_rows, a_cols, b_blocks, b_rows, b_cols):
    vmem = pl.BlockSpec(memory_space=pltpu.VMEM)
    anywhere = pl.BlockSpec(memory_space=pl.ANY)
    return pl.pallas_call(
        pack,
        out_shape=(
            jax.ShapeDtypeStruct((ROWS, BLK), jnp.bfloat16),
            jax.ShapeDtypeStruct((2, ROWS, BLK), jnp.bfloat16),
        ),
        in_specs=[anywhere] * 6,
        out_specs=(vmem,) * 2,
        scratch_shapes=[
            pltpu.SMEM((1, 1, 16), jnp.int32),
            pltpu.SMEM((1, 1, 16), jnp.int32),
            pltpu.SMEM((2, 1, HALF), jnp.int32),
            pltpu.SMEM((2, 1, HALF), jnp.int32),
            pltpu.SemaphoreType.DMA((24,)),
            pltpu.SemaphoreType.DMA((4,)),
        ],
        compiler_params=pltpu.CompilerParams(vmem_limit_bytes=4 * 1024 * 1024),
        name="pack",
    )(
        *[
            pltpu.with_memory_space_constraint(part, pltpu.HBM)
            for part in (a_rows, a_cols, b_rows, b_cols, a_blocks, b_blocks)
        ]
    )


def read_numbers(*refs):
    out, sem = refs[3:]
    copies = [
        pltpu.make_async_copy(ref.at[:, pl.ds(DATA, META), :], out.at[pl.ds(4 * g, 4)], sem.at[g])
        for g, ref in enumerate(refs[:3])
    ]
    for copy in copies:
        copy.start()
    for copy in copies:
        copy.wait()


def numbers_of(parts):
    return pl.pallas_call(
        read_numbers,
        out_shape=jax.ShapeDtypeStruct((12, META, BLK), jnp.bfloat16),
        in_specs=[pl.BlockSpec(memory_space=pl.ANY)] * 3,
        out_specs=pl.BlockSpec(memory_space=pltpu.VMEM),
        scratch_shapes=[pltpu.SemaphoreType.DMA((3,))],
        cost_estimate=pl.CostEstimate(flops=10000000000, bytes_accessed=0, transcendentals=0),
        compiler_params=pltpu.CompilerParams(vmem_limit_bytes=4 * 1024 * 1024),
        name="numbers",
    )(*parts)


def multiply(keep, far_numbers, *refs):
    a_refs, b_refs = refs[:4], refs[4:13]
    send, own, av, bv, am, bm, acc, keys, list_v, lists, flat = refs[13:24]
    data_sem, meta_sem, list_sem = refs[24:]
    row, z, core = lax.axis_index("row"), lax.axis_index("col"), lax.axis_index("layer")
    x, y = row // SIDE, row % SIDE
    spots = [(b_refs[0], 0, 2)]
    for t in range(1, 4):
        spots.append((b_refs[t], 2 * jnp.where(core == 0, 8 - t, t), 2))
        spots.append((b_refs[3 + t], 2 * jnp.where(core == 0, t, 8 - t), 2))
    spots.append((b_refs[7], 8 + core, 1))
    spots.append((b_refs[8], 9 - core, 1))
    copies, metas = [], []
    for held, meta, group in (
        (av, am, [(a_refs[g], 4 * g, 4) for g in range(4)]),
        (bv, bm, spots),
    ):
        for ref, at, count in group:
            n = len(copies)
            whole = 1 <= n <= 3
            copies.append(
                pltpu.make_async_copy(
                    ref.at[:, pl.ds(0, DATA), :], held.at[pl.ds(at, count)], data_sem.at[n]
                )
            )
            if whole:
                continue
            metas.append(
                pltpu.make_async_copy(
                    ref.at[:, pl.ds(DATA, META), :], meta.at[pl.ds(at, count)], meta_sem.at[n]
                )
            )
    for copy in metas:
        copy.start()
    for copy in copies:
        copy.start()
    av[16, 0:BLK, :] = jnp.zeros((BLK, BLK), jnp.bfloat16)
    acc[...] = jnp.zeros_like(acc)
    none = float(NONE * 128)
    lane = lax.broadcasted_iota(jnp.int32, (HALF, BLK), 1)
    slot = lax.broadcasted_iota(jnp.int32, (HALF, BLK), 0).astype(jnp.float32)
    bucket_row = (lane // CB).astype(jnp.float32)
    bucket_col = (lane % CB).astype(jnp.float32)
    for copy in metas:
        copy.wait()
    count = jnp.zeros((HALF, BLK), jnp.float32)
    for p in range(16):
        first, second = DELTA[p // 4], DELTA[p % 4]
        px = (x + jnp.where(core == 0, first, second)) % SIDE
        py = (y + jnp.where(core == 0, second, first)) % SIDE
        k = (px * SIDE + py + 2 * z) % 16
        q = (k - row + 16) % 16
        spot = ((q // 2 - z + 8) % 8) * 2 + q % 2
        numbers = (am[p] if p < 4 else far_numbers[p - 4]).astype(jnp.float32)
        wanted = numbers[HALF:, :] + bucket_col
        b_numbers = bm[spot].astype(jnp.float32)
        found = jnp.zeros((HALF, BLK), jnp.float32)
        for t in range(HALF):
            found = jnp.where(b_numbers[t : t + 1, :] == wanted, t + 1.0, found)
        kept = keep[pl.ds(k, 1), :].astype(jnp.float32)
        valid = jnp.where(numbers[:HALF, :] == bucket_row, kept, 0.0)
        valid = (valid != 0.0) & (found != 0.0)
        base = (p * HALF * 128 - 1 + spot * HALF).astype(jnp.float32)
        keys[p] = jnp.where(valid, base + slot * 128.0 + found, none)
        count = count + jnp.where(valid, 1.0, 0.0)
    count = jnp.sum(count, axis=0, keepdims=True)
    list_v[0:1, :] = count.astype(jnp.int32)
    largest = jnp.max(count).astype(jnp.int32)

    def pick(j):
        least = keys[0]
        for p in range(1, 16):
            least = jnp.minimum(least, keys[p])
        least = jnp.min(least, axis=0, keepdims=True)
        list_v[pl.ds(1 + j, 1), :] = least.astype(jnp.int32)
        for p in range(16):
            keys[p] = jnp.where(keys[p] == least, none, keys[p])

    for j in range(PICKS):
        pick(j)
    first_part = pltpu.make_async_copy(
        list_v.at[pl.ds(0, NEAR)], lists.at[pl.ds(0, NEAR)], list_sem.at[0]
    )
    first_part.start()
    first_part.wait()

    @pl.when(largest > PICKS)
    def _():
        def more(j, carry):
            pick(j)
            return carry

        lax.fori_loop(PICKS, largest, more, 0)
        whole = pltpu.make_async_copy(list_v, lists, list_sem.at[1])
        whole.start()
        whole.wait()

    def bucket(b, n):
        length = lists[0, b]
        for j in range(4):
            flat[n + j] = lists[1 + j, b] * BUCKETS + b

        def item(j, carry):
            flat[n + j] = lists[1 + j, b] * BUCKETS + b
            return carry

        lax.fori_loop(4, jnp.maximum(length, 4), item, 0)
        return n + length

    total = lax.fori_loop(0, BUCKETS, bucket, 0, unroll=4)
    for j in range(STEP):
        flat[total + j] = NONE * 128 * BUCKETS
    for copy in copies:
        copy.wait()

    def step(i, carry):
        for j in range(STEP):
            code = flat[i * STEP + j]
            b, code = code % BUCKETS, code // BUCKETS
            ia, ib = code // 128, code % 128
            left = av[ia // HALF, pl.ds(pl.multiple_of((ia % HALF) * BLK, BLK), BLK), :]
            right = bv[ib // HALF, pl.ds(pl.multiple_of((ib % HALF) * BLK, BLK), BLK), :]
            acc[b] += jnp.dot(left, right, preferred_element_type=jnp.float32)
        return carry

    lax.fori_loop(0, (total + STEP - 1) // STEP, step, 0)
    for r in range(RB):
        for n in range(2):
            send[2 * r + n] = acc[r * CB + 2 * (1 - core) + n]
            own[2 * r + n] = acc[r * CB + 2 * core + n]


def partial_sums(keep, a_parts, b_parts):
    vmem = pl.BlockSpec(memory_space=pltpu.VMEM)
    anywhere = pl.BlockSpec(memory_space=pl.ANY)
    half = jax.ShapeDtypeStruct((2 * RB, BLK, BLK), jnp.float32)
    return pl.pallas_call(
        multiply,
        out_shape=(half, half),
        in_specs=[vmem, vmem] + [anywhere] * 13,
        out_specs=(vmem, vmem),
        scratch_shapes=[
            pltpu.VMEM((17, DATA, BLK), jnp.bfloat16),
            pltpu.VMEM((16, DATA, BLK), jnp.bfloat16),
            pltpu.VMEM((4, META, BLK), jnp.bfloat16),
            pltpu.VMEM((16, META, BLK), jnp.bfloat16),
            pltpu.VMEM((BUCKETS, BLK, BLK), jnp.float32),
            pltpu.VMEM((16, HALF, BLK), jnp.float32),
            pltpu.VMEM((LISTS, BLK), jnp.int32),
            pltpu.SMEM((LISTS, BLK), jnp.int32),
            pltpu.SMEM((BUCKETS * MOST + 2 * STEP,), jnp.int32),
            pltpu.SemaphoreType.DMA((13,)),
            pltpu.SemaphoreType.DMA((13,)),
            pltpu.SemaphoreType.DMA((2,)),
        ],
        compiler_params=pltpu.CompilerParams(vmem_limit_bytes=28 * 1024 * 1024),
        name="multiply",
    )(keep, numbers_of(a_parts[1:]), *a_parts, *b_parts)


def finish(keep, own, other, out):
    for r in range(RB):
        for n in range(2):
            total = (own[2 * r + n] + other[2 * r + n]) * keep[r, n].astype(jnp.float32)
            out[r * BLK : (r + 1) * BLK, n * BLK : (n + 1) * BLK] = total.astype(jnp.bfloat16)


def filtered(keep, own, other):
    vmem = pl.BlockSpec(memory_space=pltpu.VMEM)
    return pl.pallas_call(
        finish,
        out_shape=jax.ShapeDtypeStruct((RB * BLK, 2 * BLK), jnp.bfloat16),
        in_specs=[pl.BlockSpec(memory_space=pltpu.SMEM), vmem, vmem],
        out_specs=vmem,
        name="finish",
    )(keep, own, other)


def body(a_blocks, a_rows, a_cols, b_blocks, b_rows, b_cols, prod_keep, res_keep):
    depth = lax.axis_size("col")
    core = lax.axis_index("layer")
    keep = prod_keep.transpose(1, 0, 2).reshape(16, RB * CB)
    keep = jnp.pad(keep, ((0, 0), (0, BLK - RB * CB)))

    a_mine, b_mine = packed(a_blocks, a_rows, a_cols, b_blocks, b_rows, b_cols)

    b_from = [b_mine, move_b(b_mine, 1, depth), move_b(b_mine, 2, depth)]
    b_from.append(move_b(b_from[2], 1, depth))
    last = move_b(jnp.where(core == 0, b_from[2][:1], b_from[2][1:]), 2, depth)
    b_theirs = [swap(part) for part in b_from[1:]]

    a_own = jnp.stack([a_mine] + [move_a(a_mine, d, 0) for d in STEPS])
    a_parts = [a_own] + [move_a(a_own, d, 1) for d in STEPS]

    send, own = partial_sums(keep, a_parts, b_from + b_theirs + [last, swap(last)])
    return filtered(res_keep, own, swap(send))


def solution(mesh):
    return jax.shard_map(
        body,
        mesh=mesh,
        in_specs=(
            P("col", "row", None, None, None),
            P("col", "row", None),
            P("col", "row", None),
            P("col", "row", None, None, None),
            P("col", "row", None),
            P("col", "row", None),
            P("col", None, "row"),
            P("col", ("row", "layer")),
        ),
        out_specs=P("col", ("row", "layer")),
        check_vma=False,
    )
```

time: 78.3 us -> 65.4 us (0.84)
  the two profiles are of different devices: /device:TPU:133 before, /device:TPU:1 now
where the time goes in v4:
time: 65.4 us; the launch traced here: 64.9 us
  starting transfers between devices  30.7 us (47%)
  waiting for transfers between devices  18.1 us (28%)
  Pallas kernels  12.5 us (19%)
  local copies, waits for them, and re-layouts  2.72 us (4%)
  other arithmetic  0.87 us (1%)
    ppermute x4, starting transfers between devices, move_b(): return lax.ppermute(value, ('col', 'layer'), pairs)  16.5 us
    ppermute x4, waiting for transfers between devices, move_b(): return lax.ppermute(value, ('col', 'layer'), pairs)  13.2 us
    ppermute x6, starting transfers between devices, move_a(): return lax.ppermute(value, ('row', 'layer'), pairs)  9.28 us
    pallas_call x1, Pallas kernels, partial_sums(): pl.pallas_call(multiply, out_shape=(half, half), in_specs=[vmem, vmem] +...  7.94 us
    ppermute x5, starting transfers between devices, swap(): return lax.ppermute(value, 'layer', [(0, 1), (1, 0)])  4.97 us
    ppermute x5, waiting for transfers between devices, swap(): return lax.ppermute(value, 'layer', [(0, 1), (1, 0)])  4.45 us
    unnamed x9, local copies, waits for them, and re-layouts  2.65 us
    pallas_call x1, Pallas kernels, filtered(): pl.pallas_call(finish, out_shape=jax.ShapeDtypeStruct((RB * BLK, 2 * BLK)...  2.46 us
  transfers between devices with their start and end apart: 15, of which 7 were waited for; matrix products, arithmetic and copies ran while one was open for 2% of the time, Pallas kernels for 1%

profile of v4, /device:TPU:1, one launch (start us, length us, event | category | flops | bytes accessed | tf_op | source)
XLA Modules:
  0.0 64.9 jit_solution(11933050198691865084)
XLA Ops:
  0.0 1.3 %pack.1 = (bf16[1040,128]{1,0:T(8,128)(2,1)S(1)}, bf16[2,1040,128]{2,1,0:T(8,128)(2,1)S(1)}) custom-call(s32[1,1,16]{2,1,0:T(1,128)} %a_rows.1, s32[1,1,16]{2,1,0:T(1,128)} %a_cols.1, s32[2,1,8]{2,1,0:T(1,128)} %b_rows.1, s32[2,1,8]{2,1,0:T(1,128)} %b_cols.1, bf16[1,1,16,128,128]{4,3,2,1,0:T(8,128)(2,1)} %a_blocks.1, bf16[2,1,8,128,128]{4,3,2,1,0:T(8,128)(2,1)} %b_blocks.1), custom_call_target="tpu_custom_call" | custom-call | tf_op jit(solution)/shard_map/pack/pallas_call | solution.py:100
  1.3 2.1 %collective-permute-start = (bf16[1040,128]{1,0:T(8,128)(2,1)S(1)}, bf16[1040,128]{1,0:T(8,128)(2,1)S(1)}, u32[]{:S(2)}, u32[]{:S(2)}) collective-permute-start(bf16[1040,128]{1,0:T(8,128)(2,1)S(1)} %get-tuple-element.9), channel_id=1, source_target_pairs={{0,16},{1,65},{16,32},{17,81},{32,48},{33,97},{48,0},{49,113},{64,... | collective-permute-start | bytes 798728 | tf_op jit(solution)/shard_map/ppermute | solution.py:37
  3.5 1.4 %collective-permute-start.1 = (bf16[1040,128]{1,0:T(8,128)(2,1)S(1)}, bf16[1040,128]{1,0:T(8,128)(2,1)S(1)}, u32[]{:S(2)}, u32[]{:S(2)}) collective-permute-start(bf16[1040,128]{1,0:T(8,128)(2,1)S(1)} %get-tuple-element.9), channel_id=1, source_target_pairs={{0,48},{1,193},{16,0},{17,209},{32,16},{33,225},{48,32},{49,241},{... | collective-permute-start | bytes 798728 | tf_op jit(solution)/shard_map/ppermute | solution.py:37
  4.8 1.6 %collective-permute-start.2 = (bf16[1040,128]{1,0:T(8,128)(2,1)S(1)}, bf16[1040,128]{1,0:T(8,128)(2,1)S(1)}, u32[]{:S(2)}, u32[]{:S(2)}) collective-permute-start(bf16[1040,128]{1,0:T(8,128)(2,1)S(1)} %get-tuple-element.9), channel_id=1, source_target_pairs={{0,32},{1,129},{16,48},{17,145},{32,0},{33,161},{48,16},{49,177},{... | collective-permute-start | bytes 798728 | tf_op jit(solution)/shard_map/ppermute | solution.py:37
  6.5 6.0 %collective-permute-start.7 = (bf16[2,1040,128]{2,1,0:T(8,128)(2,1)S(1)}, bf16[2,1040,128]{2,1,0:T(8,128)(2,1)S(1)}, u32[]{:S(2)}, u32[]{:S(2)}) collective-permute-start(bf16[2,1040,128]{2,1,0:T(8,128)(2,1)S(1)} %get-tuple-element.10.refs_4_), channel_id=1, source_target_pairs={{0,4},{1,13},{2,6},{3,15},{4,8},{5,1},{6,10},{7,3},{8,12},{9,5},{1... | collective-permute-start | bytes 1597448 | tf_op jit(solution)/shard_map/ppermute | solution.py:45
  13.0 1.1 %collective-permute-start.3 = (bf16[4,1040,128]{2,1,0:T(8,128)(2,1)S(1)}, bf16[4,1040,128]{2,1,0:T(8,128)(2,1)S(1)}, u32[]{:S(2)}, u32[]{:S(2)}) collective-permute-start(bf16[4,1040,128]{2,1,0:T(8,128)(2,1)S(1)} %pad_maximum_fusion.refs_0_), channel_id=1, source_target_pairs={{0,64},{1,17},{16,80},{17,33},{32,96},{33,49},{48,112},{49,1},{64,... | collective-permute-start | bytes 3194888 | tf_op jit(solution)/shard_map/ppermute | solution.py:37
  14.1 1.8 %collective-permute-start.4 = (bf16[4,1040,128]{2,1,0:T(8,128)(2,1)S(1)}, bf16[4,1040,128]{2,1,0:T(8,128)(2,1)}, u32[]{:S(2)}, u32[]{:S(2)}) collective-permute-start(bf16[4,1040,128]{2,1,0:T(8,128)(2,1)S(1)} %pad_maximum_fusion.refs_0_), channel_id=1, source_target_pairs={{0,192},{1,49},{16,208},{17,1},{32,224},{33,17},{48,240},{49,33},{... | collective-permute-start | bytes 3194888 | tf_op jit(solution)/shard_map/ppermute | solution.py:37
  15.9 1.3 %collective-permute-start.5 = (bf16[4,1040,128]{2,1,0:T(8,128)(2,1)S(1)}, bf16[4,1040,128]{2,1,0:T(8,128)(2,1)}, u32[]{:S(2)}, u32[]{:S(2)}) collective-permute-start(bf16[4,1040,128]{2,1,0:T(8,128)(2,1)S(1)} %pad_maximum_fusion.refs_0_), channel_id=1, source_target_pairs={{0,128},{1,33},{16,144},{17,49},{32,160},{33,1},{48,176},{49,17},{... | collective-permute-start | bytes 3194888 | tf_op jit(solution)/shard_map/ppermute | solution.py:37
  17.2 5.6 %collective-permute-start.6 = (bf16[2,1040,128]{2,1,0:T(8,128)(2,1)S(1)}, bf16[2,1040,128]{2,1,0:T(8,128)(2,1)}, u32[]{:S(2)}, u32[]{:S(2)}) collective-permute-start(bf16[2,1040,128]{2,1,0:T(8,128)(2,1)S(1)} %get-tuple-element.10.refs_4_), channel_id=1, source_target_pairs={{0,2},{1,15},{2,4},{3,1},{4,6},{5,3},{6,8},{7,5},{8,10},{9,7},{10,... | collective-permute-start | bytes 1597448 | tf_op jit(solution)/shard_map/ppermute | solution.py:45
  22.7 1.7 %collective-permute-done.7.refs_6_ = bf16[2,1040,128]{2,1,0:T(8,128)(2,1)S(1)} collective-permute-done((bf16[2,1040,128]{2,1,0:T(8,128)(2,1)S(1)}, bf16[2,1040,128]{2,1,0:T(8,128)(2,1)S(1)}, u32[]{:S(2)}, u32[]{:S(2)}) %collective-permute-start.7) | collective-permute-done | bytes 532512 | tf_op jit(solution)/shard_map/ppermute | solution.py:45
  24.4 2.2 %collective-permute-start.8 = (bf16[2,1040,128]{2,1,0:T(8,128)(2,1)S(1)}, bf16[2,1040,128]{2,1,0:T(8,128)(2,1)}, u32[]{:S(2)}, u32[]{:S(2)}) collective-permute-start(bf16[2,1040,128]{2,1,0:T(8,128)(2,1)S(1)} %collective-permute-done.7.refs_6_), channel_id=1, source_target_pairs={{0,2},{1,15},{2,4},{3,1},{4,6},{5,3},{6,8},{7,5},{8,10},{9,7},{10,... | collective-permute-start | bytes 1597448 | tf_op jit(solution)/shard_map/ppermute | solution.py:45
  26.6 0.7 %slice_select_fusion = bf16[1,1040,128]{2,1,0:T(8,128)(2,1)} fusion(bf16[2,1040,128]{2,1,0:T(8,128)(2,1)S(1)} %collective-permute-done.7.refs_6_, pred[]{:T(512)S(6)} %eq.3), kind=kLoop, calls=%fused_computation.1 | loop fusion | flops 133120 | bytes 798721 | tf_op jit(solution)/shard_map/jit(_where)/select_n | solution.py:339
  27.3 2.9 %collective-permute-done.6.refs_5_ = bf16[2,1040,128]{2,1,0:T(8,128)(2,1)} collective-permute-done((bf16[2,1040,128]{2,1,0:T(8,128)(2,1)S(1)}, bf16[2,1040,128]{2,1,0:T(8,128)(2,1)}, u32[]{:S(2)}, u32[]{:S(2)}) %collective-permute-start.6) | collective-permute-done | bytes 532512 | tf_op jit(solution)/shard_map/ppermute | solution.py:45
  30.3 2.7 %collective-permute-start.12 = (bf16[1,1040,128]{2,1,0:T(8,128)(2,1)}, bf16[1,1040,128]{2,1,0:T(8,128)(2,1)S(1)}, u32[]{:S(2)}, u32[]{:S(2)}) collective-permute-start(bf16[1,1040,128]{2,1,0:T(8,128)(2,1)} %slice_select_fusion), channel_id=1, source_target_pairs={{0,4},{1,13},{2,6},{3,15},{4,8},{5,1},{6,10},{7,3},{8,12},{9,5},{1... | collective-permute-start | bytes 798728 | tf_op jit(solution)/shard_map/ppermute | solution.py:45
  33.0 8.6 %collective-permute-done.12.refs_11_ = bf16[1,1040,128]{2,1,0:T(8,128)(2,1)S(1)} collective-permute-done((bf16[1,1040,128]{2,1,0:T(8,128)(2,1)}, bf16[1,1040,128]{2,1,0:T(8,128)(2,1)S(1)}, u32[]{:S(2)}, u32[]{:S(2)}) %collective-permute-start.12) | collective-permute-done | bytes 266272 | tf_op jit(solution)/shard_map/ppermute | solution.py:45
  41.7 4.4 %collective-permute-start.10 = (bf16[2,1040,128]{2,1,0:T(8,128)(2,1)S(1)}, bf16[2,1040,128]{2,1,0:T(8,128)(2,1)S(1)}, u32[]{:S(2)}, u32[]{:S(2)}) collective-permute-start(bf16[2,1040,128]{2,1,0:T(8,128)(2,1)S(1)} %collective-permute-done.7.refs_6_), channel_id=1, source_target_pairs={{0,1},{1,0},{2,3},{3,2},{4,5},{5,4},{6,7},{7,6},{8,9},{9,8},{10,11... | collective-permute-start | bytes 1597448 | tf_op jit(solution)/shard_map/ppermute | solution.py:49
  46.6 0.8 %numbers.1.far_numbers = bf16[12,16,128]{2,1,0:T(8,128)(2,1)S(1)} custom-call(bf16[4,1040,128]{2,1,0:T(8,128)(2,1)S(1)} %collective-permute-done.3.refs_0_.refs_1_, bf16[4,1040,128]{2,1,0:T(8,128)(2,1)} %collective-permute-done.4.refs_1_.refs_2_, bf16[4,1040,128]{2,1,0:T(8,128)(2,1)} %collective-permute-done.5.refs_2_.refs_3_), custom_call_target="tpu_custom_call" | custom-call | flops 10000000000 | tf_op jit(solution)/shard_map/numbers/pallas_call | solution.py:139
  47.4 1.6 %collective-permute-done.13.refs_12_ = bf16[1,1040,128]{2,1,0:T(8,128)(2,1)S(1)} collective-permute-done((bf16[1,1040,128]{2,1,0:T(8,128)(2,1)S(1)}, bf16[1,1040,128]{2,1,0:T(8,128)(2,1)S(1)}, u32[]{:S(2)}, u32[]{:S(2)}) %collective-permute-start.13) | collective-permute-done | bytes 266272 | tf_op jit(solution)/shard_map/ppermute | solution.py:49
  49.7 7.9 %multiply.1 = (f32[16,128,128]{2,1,0:T(8,128)}, f32[16,128,128]{2,1,0:T(8,128)S(1)}) custom-call(s32[16,128]{1,0:T(8,128)S(1)} %pad.4.keep, bf16[12,16,128]{2,1,0:T(8,128)(2,1)S(1)} %numbers.1.far_numbers, bf16[4,1040,128]{2,1,0:T(8,128)(2,1)S(1)} %pad_maximum_fusion.refs_0_, bf16[4,1040,128]{2,1,0:T(8,128)(2,1)S(1)} %collective-permute-done.3.refs_0_.refs_1_, ...), custom_call_target="tpu_custom_call" | custom-call | tf_op jit(solution)/shard_map/multiply/pallas_call | solution.py:287
  57.6 1.0 %copy-done = f32[16,128,128]{2,1,0:T(8,128)} copy-done((f32[16,128,128]{2,1,0:T(8,128)}, f32[16,128,128]{2,1,0:T(8,128)S(1)}, u32[]{:S(2)}) %copy-start) | copy-done | bytes 1048600
  58.6 0.7 %copy.12.keep = s32[8,2]{1,0:T(8,128)} copy(s32[8,2]{0,1:T(2,128)S(1)} %copy-done.3) | data formatting | bytes 128 | tf_op args[7]
  59.3 2.2 %collective-permute-done.14.other = f32[16,128,128]{2,1,0:T(8,128)S(1)} collective-permute-done((f32[16,128,128]{2,1,0:T(8,128)}, f32[16,128,128]{2,1,0:T(8,128)S(1)}, u32[]{:S(2)}, u32[]{:S(2)}) %collective-permute-start.14) | collective-permute-done | bytes 1048608 | tf_op jit(solution)/shard_map/ppermute | solution.py:49
  61.5 1.0 %copy-done.1 = f32[16,128,128]{2,1,0:T(8,128)} copy-done((f32[16,128,128]{2,1,0:T(8,128)}, f32[16,128,128]{2,1,0:T(8,128)S(1)}, u32[]{:S(2)}) %copy-start.1) | copy-done | bytes 1048600
  62.5 2.5 %finish.1 = bf16[1024,256]{1,0:T(8,128)(2,1)} custom-call(s32[8,2]{1,0:T(8,128)} %copy.12.keep, f32[16,128,128]{2,1,0:T(8,128)} %copy-done, f32[16,128,128]{2,1,0:T(8,128)} %copy-done.1), custom_call_target="tpu_custom_call" | custom-call | tf_op jit(solution)/shard_map/finish/pallas_call | solution.py:320
  (23 shorter events, 1.9 us)
Async XLA Ops:
  1.3 11.1 %collective-permute-start = (bf16[1040,128]{1,0:T(8,128)(2,1)S(1)}, bf16[1040,128]{1,0:T(8,128)(2,1)S(1)}, u32[]{:S(2)}, u32[]{:S(2)}) collective-permute-start(bf16[1040,128]{1,0:T(8,128)(2,1)S(1)} %get-tuple-element.9), channel_id=1, source_target_pairs={{0,16},{1,65},{16,32},{17,81},{32,48},{33,97},{48,0},{49,113},{64,... | collective-permute-start | bytes 798728 | tf_op jit(solution)/shard_map/ppermute | solution.py:37
  3.5 9.0 %collective-permute-start.1 = (bf16[1040,128]{1,0:T(8,128)(2,1)S(1)}, bf16[1040,128]{1,0:T(8,128)(2,1)S(1)}, u32[]{:S(2)}, u32[]{:S(2)}) collective-permute-start(bf16[1040,128]{1,0:T(8,128)(2,1)S(1)} %get-tuple-element.9), channel_id=1, source_target_pairs={{0,48},{1,193},{16,0},{17,209},{32,16},{33,225},{48,32},{49,241},{... | collective-permute-start | bytes 798728 | tf_op jit(solution)/shard_map/ppermute | solution.py:37
  4.8 8.0 %collective-permute-start.2 = (bf16[1040,128]{1,0:T(8,128)(2,1)S(1)}, bf16[1040,128]{1,0:T(8,128)(2,1)S(1)}, u32[]{:S(2)}, u32[]{:S(2)}) collective-permute-start(bf16[1040,128]{1,0:T(8,128)(2,1)S(1)} %get-tuple-element.9), channel_id=1, source_target_pairs={{0,32},{1,129},{16,48},{17,145},{32,0},{33,161},{48,16},{49,177},{... | collective-permute-start | bytes 798728 | tf_op jit(solution)/shard_map/ppermute | solution.py:37
  6.5 17.9 %collective-permute-start.7 = (bf16[2,1040,128]{2,1,0:T(8,128)(2,1)S(1)}, bf16[2,1040,128]{2,1,0:T(8,128)(2,1)S(1)}, u32[]{:S(2)}, u32[]{:S(2)}) collective-permute-start(bf16[2,1040,128]{2,1,0:T(8,128)(2,1)S(1)} %get-tuple-element.10.refs_4_), channel_id=1, source_target_pairs={{0,4},{1,13},{2,6},{3,15},{4,8},{5,1},{6,10},{7,3},{8,12},{9,5},{1... | collective-permute-start | bytes 1597448 | tf_op jit(solution)/shard_map/ppermute | solution.py:45
  12.9 20.1 %copy-start.2 = (s32[8,16,4]{1,2,0:T(4,128)S(1)}, s32[8,16,4]{1,2,0:T(4,128)}, u32[]{:S(2)}) copy-start(s32[8,16,4]{1,2,0:T(4,128)} %param.14) | copy-start | bytes 6148
  13.0 33.0 %collective-permute-start.3 = (bf16[4,1040,128]{2,1,0:T(8,128)(2,1)S(1)}, bf16[4,1040,128]{2,1,0:T(8,128)(2,1)S(1)}, u32[]{:S(2)}, u32[]{:S(2)}) collective-permute-start(bf16[4,1040,128]{2,1,0:T(8,128)(2,1)S(1)} %pad_maximum_fusion.refs_0_), channel_id=1, source_target_pairs={{0,64},{1,17},{16,80},{17,33},{32,96},{33,49},{48,112},{49,1},{64,... | collective-permute-start | bytes 3194888 | tf_op jit(solution)/shard_map/ppermute | solution.py:37
  14.1 32.5 %collective-permute-start.4 = (bf16[4,1040,128]{2,1,0:T(8,128)(2,1)S(1)}, bf16[4,1040,128]{2,1,0:T(8,128)(2,1)}, u32[]{:S(2)}, u32[]{:S(2)}) collective-permute-start(bf16[4,1040,128]{2,1,0:T(8,128)(2,1)S(1)} %pad_maximum_fusion.refs_0_), channel_id=1, source_target_pairs={{0,192},{1,49},{16,208},{17,1},{32,224},{33,17},{48,240},{49,33},{... | collective-permute-start | bytes 3194888 | tf_op jit(solution)/shard_map/ppermute | solution.py:37
  15.9 30.7 %collective-permute-start.5 = (bf16[4,1040,128]{2,1,0:T(8,128)(2,1)S(1)}, bf16[4,1040,128]{2,1,0:T(8,128)(2,1)}, u32[]{:S(2)}, u32[]{:S(2)}) collective-permute-start(bf16[4,1040,128]{2,1,0:T(8,128)(2,1)S(1)} %pad_maximum_fusion.refs_0_), channel_id=1, source_target_pairs={{0,128},{1,33},{16,144},{17,49},{32,160},{33,1},{48,176},{49,17},{... | collective-permute-start | bytes 3194888 | tf_op jit(solution)/shard_map/ppermute | solution.py:37
  17.2 13.1 %collective-permute-start.6 = (bf16[2,1040,128]{2,1,0:T(8,128)(2,1)S(1)}, bf16[2,1040,128]{2,1,0:T(8,128)(2,1)}, u32[]{:S(2)}, u32[]{:S(2)}) collective-permute-start(bf16[2,1040,128]{2,1,0:T(8,128)(2,1)S(1)} %get-tuple-element.10.refs_4_), channel_id=1, source_target_pairs={{0,2},{1,15},{2,4},{3,1},{4,6},{5,3},{6,8},{7,5},{8,10},{9,7},{10,... | collective-permute-start | bytes 1597448 | tf_op jit(solution)/shard_map/ppermute | solution.py:45
  24.4 21.6 %collective-permute-start.8 = (bf16[2,1040,128]{2,1,0:T(8,128)(2,1)S(1)}, bf16[2,1040,128]{2,1,0:T(8,128)(2,1)}, u32[]{:S(2)}, u32[]{:S(2)}) collective-permute-start(bf16[2,1040,128]{2,1,0:T(8,128)(2,1)S(1)} %collective-permute-done.7.refs_6_), channel_id=1, source_target_pairs={{0,2},{1,15},{2,4},{3,1},{4,6},{5,3},{6,8},{7,5},{8,10},{9,7},{10,... | collective-permute-start | bytes 1597448 | tf_op jit(solution)/shard_map/ppermute | solution.py:45
  30.3 11.4 %collective-permute-start.12 = (bf16[1,1040,128]{2,1,0:T(8,128)(2,1)}, bf16[1,1040,128]{2,1,0:T(8,128)(2,1)S(1)}, u32[]{:S(2)}, u32[]{:S(2)}) collective-permute-start(bf16[1,1040,128]{2,1,0:T(8,128)(2,1)} %slice_select_fusion), channel_id=1, source_target_pairs={{0,4},{1,13},{2,6},{3,15},{4,8},{5,1},{6,10},{7,3},{8,12},{9,5},{1... | collective-permute-start | bytes 798728 | tf_op jit(solution)/shard_map/ppermute | solution.py:45
  41.7 7.4 %collective-permute-start.10 = (bf16[2,1040,128]{2,1,0:T(8,128)(2,1)S(1)}, bf16[2,1040,128]{2,1,0:T(8,128)(2,1)S(1)}, u32[]{:S(2)}, u32[]{:S(2)}) collective-permute-start(bf16[2,1040,128]{2,1,0:T(8,128)(2,1)S(1)} %collective-permute-done.7.refs_6_), channel_id=1, source_target_pairs={{0,1},{1,0},{2,3},{3,2},{4,5},{5,4},{6,7},{7,6},{8,9},{9,8},{10,11... | collective-permute-start | bytes 1597448 | tf_op jit(solution)/shard_map/ppermute | solution.py:49
  46.0 3.0 %collective-permute-start.9 = (bf16[2,1040,128]{2,1,0:T(8,128)(2,1)}, bf16[2,1040,128]{2,1,0:T(8,128)(2,1)S(1)}, u32[]{:S(2)}, u32[]{:S(2)}) collective-permute-start(bf16[2,1040,128]{2,1,0:T(8,128)(2,1)} %collective-permute-done.6.refs_5_), channel_id=1, source_target_pairs={{0,1},{1,0},{2,3},{3,2},{4,5},{5,4},{6,7},{7,6},{8,9},{9,8},{10,11... | collective-permute-start | bytes 1597448 | tf_op jit(solution)/shard_map/ppermute | solution.py:49
  46.0 3.0 %collective-permute-start.13 = (bf16[1,1040,128]{2,1,0:T(8,128)(2,1)S(1)}, bf16[1,1040,128]{2,1,0:T(8,128)(2,1)S(1)}, u32[]{:S(2)}, u32[]{:S(2)}) collective-permute-start(bf16[1,1040,128]{2,1,0:T(8,128)(2,1)S(1)} %collective-permute-done.12.refs_11_), channel_id=1, source_target_pairs={{0,1},{1,0},{2,3},{3,2},{4,5},{5,4},{6,7},{7,6},{8,9},{9,8},{10,11... | collective-permute-start | bytes 798728 | tf_op jit(solution)/shard_map/ppermute | solution.py:49
  46.5 3.1 %collective-permute-start.11 = (bf16[2,1040,128]{2,1,0:T(8,128)(2,1)}, bf16[2,1040,128]{2,1,0:T(8,128)(2,1)S(1)}, u32[]{:S(2)}, u32[]{:S(2)}) collective-permute-start(bf16[2,1040,128]{2,1,0:T(8,128)(2,1)} %collective-permute-done.8.refs_7_), channel_id=1, source_target_pairs={{0,1},{1,0},{2,3},{3,2},{4,5},{5,4},{6,7},{7,6},{8,9},{9,8},{10,11... | collective-permute-start | bytes 1597448 | tf_op jit(solution)/shard_map/ppermute | solution.py:49
  47.4 11.2 %copy-start.3 = (s32[8,2]{0,1:T(2,128)S(1)}, s32[8,2]{0,1:T(2,128)}, u32[]{:S(2)}) copy-start(s32[8,2]{0,1:T(2,128)} %param.15) | copy-start | bytes 196
  57.6 1.0 %copy-start = (f32[16,128,128]{2,1,0:T(8,128)}, f32[16,128,128]{2,1,0:T(8,128)S(1)}, u32[]{:S(2)}) copy-start(f32[16,128,128]{2,1,0:T(8,128)S(1)} %get-tuple-element.11.own) | copy-start | bytes 3145732
  58.6 2.9 %collective-permute-start.14 = (f32[16,128,128]{2,1,0:T(8,128)}, f32[16,128,128]{2,1,0:T(8,128)S(1)}, u32[]{:S(2)}, u32[]{:S(2)}) collective-permute-start(f32[16,128,128]{2,1,0:T(8,128)} %get-tuple-element.12), channel_id=1, source_target_pairs={{0,1},{1,0},{2,3},{3,2},{4,5},{5,4},{6,7},{7,6},{8,9},{9,8},{10,11... | collective-permute-start | bytes 3145736 | tf_op jit(solution)/shard_map/ppermute | solution.py:49
  61.5 1.0 %copy-start.1 = (f32[16,128,128]{2,1,0:T(8,128)}, f32[16,128,128]{2,1,0:T(8,128)S(1)}, u32[]{:S(2)}) copy-start(f32[16,128,128]{2,1,0:T(8,128)S(1)} %collective-permute-done.14.other) | copy-start | bytes 3145732

commit v5 on v4

--- a/solution.py
+++ b/solution.py
@@ -20,6 +20,7 @@
 LISTS = 80
 STEP = 8
 BUCKETS = 32
+ITEMS = 2
 NONE = 128
 DELTA = (0, SIDE - 1, 1, 2)
 STEPS = (1, -1, 2)
@@ -123,35 +124,28 @@
     )
 
 
-def read_numbers(*refs):
-    out, sem = refs[3:]
-    copies = [
-        pltpu.make_async_copy(ref.at[:, pl.ds(DATA, META), :], out.at[pl.ds(4 * g, 4)], sem.at[g])
-        for g, ref in enumerate(refs[:3])
-    ]
-    for copy in copies:
-        copy.start()
-    for copy in copies:
-        copy.wait()
-
-
-def numbers_of(parts):
+def mark(*refs):
+    refs[-1][...] = jnp.zeros_like(refs[-1])
+
+
+def marker(parts, microseconds):
     return pl.pallas_call(
-        read_numbers,
-        out_shape=jax.ShapeDtypeStruct((12, META, BLK), jnp.bfloat16),
-        in_specs=[pl.BlockSpec(memory_space=pl.ANY)] * 3,
+        mark,
+        out_shape=jax.ShapeDtypeStruct((8, BLK), jnp.float32),
+        in_specs=[pl.BlockSpec(memory_space=pl.ANY)] * len(parts),
         out_specs=pl.BlockSpec(memory_space=pltpu.VMEM),
-        scratch_shapes=[pltpu.SemaphoreType.DMA((3,))],
-        cost_estimate=pl.CostEstimate(flops=10000000000, bytes_accessed=0, transcendentals=0),
+        cost_estimate=pl.CostEstimate(
+            flops=int(microseconds * 1.15e9), bytes_accessed=0, transcendentals=0
+        ),
         compiler_params=pltpu.CompilerParams(vmem_limit_bytes=4 * 1024 * 1024),
-        name="numbers",
+        name="marker",
     )(*parts)
 
 
-def multiply(keep, far_numbers, *refs):
+def multiply(keep, marked, *refs):
     a_refs, b_refs = refs[:4], refs[4:13]
     send, own, av, bv, am, bm, acc, keys, list_v, lists, flat = refs[13:24]
-    data_sem, meta_sem, list_sem = refs[24:]
+    data_sem, meta_sem, list_sem, out_sem = refs[24:]
     row, z, core = lax.axis_index("row"), lax.axis_index("col"), lax.axis_index("layer")
     x, y = row // SIDE, row % SIDE
     spots = [(b_refs[0], 0, 2)]
@@ -167,14 +161,11 @@
     ):
         for ref, at, count in group:
             n = len(copies)
-            whole = 1 <= n <= 3
             copies.append(
                 pltpu.make_async_copy(
                     ref.at[:, pl.ds(0, DATA), :], held.at[pl.ds(at, count)], data_sem.at[n]
                 )
             )
-            if whole:
-                continue
             metas.append(
                 pltpu.make_async_copy(
                     ref.at[:, pl.ds(DATA, META), :], meta.at[pl.ds(at, count)], meta_sem.at[n]
@@ -185,7 +176,6 @@
     for copy in copies:
         copy.start()
     av[16, 0:BLK, :] = jnp.zeros((BLK, BLK), jnp.bfloat16)
-    acc[...] = jnp.zeros_like(acc)
     none = float(NONE * 128)
     lane = lax.broadcasted_iota(jnp.int32, (HALF, BLK), 1)
     slot = lax.broadcasted_iota(jnp.int32, (HALF, BLK), 0).astype(jnp.float32)
@@ -201,7 +191,7 @@
         k = (px * SIDE + py + 2 * z) % 16
         q = (k - row + 16) % 16
         spot = ((q // 2 - z + 8) % 8) * 2 + q % 2
-        numbers = (am[p] if p < 4 else far_numbers[p - 4]).astype(jnp.float32)
+        numbers = am[p].astype(jnp.float32)
         wanted = numbers[HALF:, :] + bucket_col
         b_numbers = bm[spot].astype(jnp.float32)
         found = jnp.zeros((HALF, BLK), jnp.float32)
@@ -247,15 +237,15 @@
 
     def bucket(b, n):
         length = lists[0, b]
-        for j in range(4):
-            flat[n + j] = lists[1 + j, b] * BUCKETS + b
+        for j in range(2):
+            flat[n + j] = lists[1 + ITEMS + j, b] * BUCKETS + b
 
         def item(j, carry):
-            flat[n + j] = lists[1 + j, b] * BUCKETS + b
+            flat[n + j - ITEMS] = lists[1 + j, b] * BUCKETS + b
             return carry
 
-        lax.fori_loop(4, jnp.maximum(length, 4), item, 0)
-        return n + length
+        lax.fori_loop(ITEMS + 2, jnp.maximum(length, ITEMS + 2), item, 0)
+        return n + jnp.maximum(length - ITEMS, 0)
 
     total = lax.fori_loop(0, BUCKETS, bucket, 0, unroll=4)
     for j in range(STEP):
@@ -263,21 +253,41 @@
     for copy in copies:
         copy.wait()
 
+    def blocks_of(code):
+        ia, ib = code // 128, code % 128
+        return (
+            av[ia // HALF, pl.ds(pl.multiple_of((ia % HALF) * BLK, BLK), BLK), :],
+            bv[ib // HALF, pl.ds(pl.multiple_of((ib % HALF) * BLK, BLK), BLK), :],
+        )
+
+    for b in range(BUCKETS):
+        pairs = [blocks_of(lists[1 + j, b]) for j in range(ITEMS)]
+        acc[b] = jnp.dot(
+            jnp.concatenate([left for left, _ in pairs], axis=1),
+            jnp.concatenate([right for _, right in pairs], axis=0),
+            preferred_element_type=jnp.float32,
+        )
+
     def step(i, carry):
         for j in range(STEP):
             code = flat[i * STEP + j]
-            b, code = code % BUCKETS, code // BUCKETS
-            ia, ib = code // 128, code % 128
-            left = av[ia // HALF, pl.ds(pl.multiple_of((ia % HALF) * BLK, BLK), BLK), :]
-            right = bv[ib // HALF, pl.ds(pl.multiple_of((ib % HALF) * BLK, BLK), BLK), :]
-            acc[b] += jnp.dot(left, right, preferred_element_type=jnp.float32)
+            left, right = blocks_of(code // BUCKETS)
+            acc[code % BUCKETS] += jnp.dot(left, right, preferred_element_type=jnp.float32)
         return carry
 
     lax.fori_loop(0, (total + STEP - 1) // STEP, step, 0)
-    for r in range(RB):
-        for n in range(2):
-            send[2 * r + n] = acc[r * CB + 2 * (1 - core) + n]
-            own[2 * r + n] = acc[r * CB + 2 * core + n]
+    keeping = []
+    for n, (out, base) in enumerate(((send, 2 * (1 - core)), (own, 2 * core))):
+        for r in range(RB):
+            keeping.append(
+                pltpu.make_async_copy(
+                    acc.at[pl.ds(r * CB + base, 2)], out.at[pl.ds(2 * r, 2)], out_sem.at[n, r]
+                )
+            )
+    for copy in keeping:
+        copy.start()
+    for copy in keeping:
+        copy.wait()
 
 
 def partial_sums(keep, a_parts, b_parts):
@@ -286,13 +296,13 @@
     half = jax.ShapeDtypeStruct((2 * RB, BLK, BLK), jnp.float32)
     return pl.pallas_call(
         multiply,
-        out_shape=(half, half),
+        out_shape=(half, pltpu.HBM(half.shape, half.dtype)),
         in_specs=[vmem, vmem] + [anywhere] * 13,
-        out_specs=(vmem, vmem),
+        out_specs=(anywhere, anywhere),
         scratch_shapes=[
             pltpu.VMEM((17, DATA, BLK), jnp.bfloat16),
             pltpu.VMEM((16, DATA, BLK), jnp.bfloat16),
-            pltpu.VMEM((4, META, BLK), jnp.bfloat16),
+            pltpu.VMEM((16, META, BLK), jnp.bfloat16),
             pltpu.VMEM((16, META, BLK), jnp.bfloat16),
             pltpu.VMEM((BUCKETS, BLK, BLK), jnp.float32),
             pltpu.VMEM((16, HALF, BLK), jnp.float32),
@@ -302,28 +312,59 @@
             pltpu.SemaphoreType.DMA((13,)),
             pltpu.SemaphoreType.DMA((13,)),
             pltpu.SemaphoreType.DMA((2,)),
+            pltpu.SemaphoreType.DMA((2, RB)),
         ],
         compiler_params=pltpu.CompilerParams(vmem_limit_bytes=28 * 1024 * 1024),
         name="multiply",
-    )(keep, numbers_of(a_parts[1:]), *a_parts, *b_parts)
-
-
-def finish(keep, own, other, out):
-    for r in range(RB):
-        for n in range(2):
-            total = (own[2 * r + n] + other[2 * r + n]) * keep[r, n].astype(jnp.float32)
-            out[r * BLK : (r + 1) * BLK, n * BLK : (n + 1) * BLK] = total.astype(jnp.bfloat16)
+    )(keep, marker(a_parts[1:], 10), *a_parts, *b_parts)
+
+
+def finish(keep_in, own, other, out, held, made, keep, sem, out_sem, keep_sem):
+    keeps = pltpu.make_async_copy(keep_in, keep, keep_sem)
+    keeps.start()
+    copies = [
+        pltpu.make_async_copy(
+            source.at[pl.ds(4 * r, 4)], held.at[i, pl.ds(4 * r, 4)], sem.at[i, r]
+        )
+        for r in range(RB // 2)
+        for i, source in enumerate((own, other))
+    ]
+    for copy in copies:
+        copy.start()
+    keeps.wait()
+    written = []
+    for r in range(RB // 2):
+        copies[2 * r].wait()
+        copies[2 * r + 1].wait()
+        for b in range(4 * r, 4 * r + 4):
+            total = (held[0, b] + held[1, b]) * keep[b // 2, b % 2].astype(jnp.float32)
+            cols = slice(b % 2 * BLK, (b % 2 + 1) * BLK)
+            made[b // 2 * BLK : (b // 2 + 1) * BLK, cols] = total.astype(jnp.bfloat16)
+        rows = pl.ds(2 * r * BLK, 2 * BLK)
+        written.append(pltpu.make_async_copy(made.at[rows], out.at[rows], out_sem.at[r]))
+        written[-1].start()
+    for copy in written:
+        copy.wait()
 
 
 def filtered(keep, own, other):
-    vmem = pl.BlockSpec(memory_space=pltpu.VMEM)
+    anywhere = pl.BlockSpec(memory_space=pl.ANY)
     return pl.pallas_call(
         finish,
         out_shape=jax.ShapeDtypeStruct((RB * BLK, 2 * BLK), jnp.bfloat16),
-        in_specs=[pl.BlockSpec(memory_space=pltpu.SMEM), vmem, vmem],
-        out_specs=vmem,
+        in_specs=[anywhere] * 3,
+        out_specs=anywhere,
+        scratch_shapes=[
+            pltpu.VMEM((2, 2 * RB, BLK, BLK), jnp.float32),
+            pltpu.VMEM((RB * BLK, 2 * BLK), jnp.bfloat16),
+            pltpu.SMEM((RB, 2), jnp.int32),
+            pltpu.SemaphoreType.DMA((2, RB // 2)),
+            pltpu.SemaphoreType.DMA((RB // 2,)),
+            pltpu.SemaphoreType.DMA,
+        ],
+        compiler_params=pltpu.CompilerParams(vmem_limit_bytes=8 * 1024 * 1024),
         name="finish",
-    )(keep, own, other)
+    )(keep, pltpu.with_memory_space_constraint(own, pltpu.HBM), other)
 
 
 def body(a_blocks, a_rows, a_cols, b_blocks, b_rows, b_cols, prod_keep, res_keep):
@@ -334,10 +375,14 @@
 
     a_mine, b_mine = packed(a_blocks, a_rows, a_cols, b_blocks, b_rows, b_cols)
 
-    b_from = [b_mine, move_b(b_mine, 1, depth), move_b(b_mine, 2, depth)]
-    b_from.append(move_b(b_from[2], 1, depth))
-    last = move_b(jnp.where(core == 0, b_from[2][:1], b_from[2][1:]), 2, depth)
-    b_theirs = [swap(part) for part in b_from[1:]]
+    b_one = move_b(b_mine, 1, depth)
+    b_two, b_one_back = lax.optimization_barrier((move_b(b_one, 1, depth), swap(b_one)))
+    b_three = move_b(b_two, 1, depth)
+    part = jnp.where(core == 0, b_two[:1], b_two[1:])
+    part, b_two_back = lax.optimization_barrier((part, swap(b_two)))
+    last = move_b(part, 2, depth)
+    b_from = [b_mine, b_one, b_two, b_three]
+    b_theirs = [b_one_back, b_two_back, swap(b_three)]
 
     a_own = jnp.stack([a_mine] + [move_a(a_mine, d, 0) for d in STEPS])
     a_parts = [a_own] + [move_a(a_own, d, 1) for d in STEPS]

time: 65.4 us -> 59.1 us (0.904)
  starting transfers between devices: 30.7 us -> 26.4 us
  Pallas kernels: 12.5 us -> 10.1 us
  waiting for transfers between devices: 18.1 us -> 19.9 us
  local copies, waits for them, and re-layouts: 2.72 us -> 0.97 us
    ppermute x4, starting transfers between devices: 16.5 us -> 11.4 us  [move_b(): return lax.ppermute(value, ('col', 'layer'), pairs)]
    ppermute x6, waiting for transfers between devices: 0.38 us -> 4.89 us  [move_a(): return lax.ppermute(value, ('row', 'layer'), pairs)]
    pallas_call x2, Pallas kernels: 8.7 us -> 6.79 us  [the longest x1 6.79 us: partial_sums(): pl.pallas_call(multiply, out_shape=(half, pltpu.HBM(half.shape, half.dtyp...]
    unnamed x9 -> x13, local copies, waits for them, and re-layouts: 2.65 us -> 0.9 us
    ppermute x5, waiting for transfers between devices: 4.45 us -> 2.8 us  [swap(): return lax.ppermute(value, 'layer', [(0, 1), (1, 0)])]
    ppermute x5, starting transfers between devices: 4.97 us -> 6.31 us  [swap(): return lax.ppermute(value, 'layer', [(0, 1), (1, 0)])]
    ppermute x4, waiting for transfers between devices: 13.2 us -> 12.2 us  [move_b(): return lax.ppermute(value, ('col', 'layer'), pairs)]
  transfers between devices with their start and end apart: 15 -> 15, of which waited for: 7 -> 9; matrix products, arithmetic and copies ran while one was open for 2% -> 2% of each run, Pallas kernels for 1% -> 0%
where the time goes in v5:
time: 59.1 us; the launch traced here: 58.5 us
  starting transfers between devices  26.4 us (45%)
  waiting for transfers between devices  19.9 us (34%)
  Pallas kernels  10.1 us (17%)
  local copies, waits for them, and re-layouts  0.97 us (2%)
  other arithmetic  0.87 us (1%)
    ppermute x4, waiting for transfers between devices, move_b(): return lax.ppermute(value, ('col', 'layer'), pairs)  12.2 us
    ppermute x4, starting transfers between devices, move_b(): return lax.ppermute(value, ('col', 'layer'), pairs)  11.4 us
    ppermute x6, starting transfers between devices, move_a(): return lax.ppermute(value, ('row', 'layer'), pairs)  8.67 us
    pallas_call x1, Pallas kernels, partial_sums(): pl.pallas_call(multiply, out_shape=(half, pltpu.HBM(half.shape, half.dtyp...  6.79 us
    ppermute x5, starting transfers between devices, swap(): return lax.ppermute(value, 'layer', [(0, 1), (1, 0)])  6.31 us
    ppermute x6, waiting for transfers between devices, move_a(): return lax.ppermute(value, ('row', 'layer'), pairs)  4.89 us
    ppermute x5, waiting for transfers between devices, swap(): return lax.ppermute(value, 'layer', [(0, 1), (1, 0)])  2.8 us
    pallas_call x1, Pallas kernels, filtered(): pl.pallas_call(finish, out_shape=jax.ShapeDtypeStruct((RB * BLK, 2 * BLK)...  2 us
  transfers between devices with their start and end apart: 15, of which 9 were waited for; matrix products, arithmetic and copies ran while one was open for 2% of the time, Pallas kernels for 0%

profile of v5, /device:TPU:1, one launch (start us, length us, event | category | flops | bytes accessed | tf_op | source)
XLA Modules:
  0.0 58.5 jit_solution(14215388133155227672)
XLA Ops:
  0.0 1.3 %pack.1 = (bf16[1040,128]{1,0:T(8,128)(2,1)S(1)}, bf16[2,1040,128]{2,1,0:T(8,128)(2,1)S(1)}) custom-call(s32[1,1,16]{2,1,0:T(1,128)} %a_rows.1, s32[1,1,16]{2,1,0:T(1,128)} %a_cols.1, s32[2,1,8]{2,1,0:T(1,128)} %b_rows.1, s32[2,1,8]{2,1,0:T(1,128)} %b_cols.1, bf16[1,1,16,128,128]{4,3,2,1,0:T(8,128)(2,1)} %a_blocks.1, bf16[2,1,8,128,128]{4,3,2,1,0:T(8,128)(2,1)} %b_blocks.1), custom_call_target="tpu_custom_call" | custom-call | tf_op jit(solution)/shard_map/pack/pallas_call | solution.py:101
  1.3 6.5 %collective-permute-start.6 = (bf16[2,1040,128]{2,1,0:T(8,128)(2,1)S(1)}, bf16[2,1040,128]{2,1,0:T(8,128)(2,1)S(1)}, u32[]{:S(2)}, u32[]{:S(2)}) collective-permute-start(bf16[2,1040,128]{2,1,0:T(8,128)(2,1)S(1)} %get-tuple-element.14.refs_4_), channel_id=1, source_target_pairs={{0,2},{1,15},{2,4},{3,1},{4,6},{5,3},{6,8},{7,5},{8,10},{9,7},{10,... | collective-permute-start | bytes 1597448 | tf_op jit(solution)/shard_map/ppermute | solution.py:46
  7.8 1.2 %collective-permute-start = (bf16[1040,128]{1,0:T(8,128)(2,1)S(1)}, bf16[1040,128]{1,0:T(8,128)(2,1)S(1)}, u32[]{:S(2)}, u32[]{:S(2)}) collective-permute-start(bf16[1040,128]{1,0:T(8,128)(2,1)S(1)} %get-tuple-element.13), channel_id=1, source_target_pairs={{0,16},{1,65},{16,32},{17,81},{32,48},{33,97},{48,0},{49,113},{64,... | collective-permute-start | bytes 798728 | tf_op jit(solution)/shard_map/ppermute | solution.py:38
  9.0 1.5 %collective-permute-start.1 = (bf16[1040,128]{1,0:T(8,128)(2,1)S(1)}, bf16[1040,128]{1,0:T(8,128)(2,1)S(1)}, u32[]{:S(2)}, u32[]{:S(2)}) collective-permute-start(bf16[1040,128]{1,0:T(8,128)(2,1)S(1)} %get-tuple-element.13), channel_id=1, source_target_pairs={{0,48},{1,193},{16,0},{17,209},{32,16},{33,225},{48,32},{49,241},{... | collective-permute-start | bytes 798728 | tf_op jit(solution)/shard_map/ppermute | solution.py:38
  10.5 1.5 %collective-permute-start.2 = (bf16[1040,128]{1,0:T(8,128)(2,1)S(1)}, bf16[1040,128]{1,0:T(8,128)(2,1)S(1)}, u32[]{:S(2)}, u32[]{:S(2)}) collective-permute-start(bf16[1040,128]{1,0:T(8,128)(2,1)S(1)} %get-tuple-element.13), channel_id=1, source_target_pairs={{0,32},{1,129},{16,48},{17,145},{32,0},{33,161},{48,16},{49,177},{... | collective-permute-start | bytes 798728 | tf_op jit(solution)/shard_map/ppermute | solution.py:38
  12.0 2.0 %collective-permute-done.6.refs_5_ = bf16[2,1040,128]{2,1,0:T(8,128)(2,1)S(1)} collective-permute-done((bf16[2,1040,128]{2,1,0:T(8,128)(2,1)S(1)}, bf16[2,1040,128]{2,1,0:T(8,128)(2,1)S(1)}, u32[]{:S(2)}, u32[]{:S(2)}) %collective-permute-start.6) | collective-permute-done | bytes 532512 | tf_op jit(solution)/shard_map/ppermute | solution.py:46
  14.0 3.4 %collective-permute-start.7 = (bf16[2,1040,128]{2,1,0:T(8,128)(2,1)S(1)}, bf16[2,1040,128]{2,1,0:T(8,128)(2,1)S(1)}, u32[]{:S(2)}, u32[]{:S(2)}) collective-permute-start(bf16[2,1040,128]{2,1,0:T(8,128)(2,1)S(1)} %collective-permute-done.6.refs_5_), channel_id=1, source_target_pairs={{0,2},{1,15},{2,4},{3,1},{4,6},{5,3},{6,8},{7,5},{8,10},{9,7},{10,... | collective-permute-start | bytes 1597448 | tf_op jit(solution)/shard_map/ppermute | solution.py:46
  17.5 0.7 %collective-permute-done.2 = bf16[1040,128]{1,0:T(8,128)(2,1)S(1)} collective-permute-done((bf16[1040,128]{1,0:T(8,128)(2,1)S(1)}, bf16[1040,128]{1,0:T(8,128)(2,1)S(1)}, u32[]{:S(2)}, u32[]{:S(2)}) %collective-permute-start.2) | collective-permute-done | bytes 266272 | tf_op jit(solution)/shard_map/ppermute | solution.py:38
  18.3 1.4 %collective-permute-start.3 = (bf16[4,1040,128]{2,1,0:T(8,128)(2,1)S(1)}, bf16[4,1040,128]{2,1,0:T(8,128)(2,1)S(1)}, u32[]{:S(2)}, u32[]{:S(2)}) collective-permute-start(bf16[4,1040,128]{2,1,0:T(8,128)(2,1)S(1)} %pad_maximum_fusion.refs_0_), channel_id=1, source_target_pairs={{0,64},{1,17},{16,80},{17,33},{32,96},{33,49},{48,112},{49,1},{64,... | collective-permute-start | bytes 3194888 | tf_op jit(solution)/shard_map/ppermute | solution.py:38
  19.7 1.5 %collective-permute-start.4 = (bf16[4,1040,128]{2,1,0:T(8,128)(2,1)S(1)}, bf16[4,1040,128]{2,1,0:T(8,128)(2,1)}, u32[]{:S(2)}, u32[]{:S(2)}) collective-permute-start(bf16[4,1040,128]{2,1,0:T(8,128)(2,1)S(1)} %pad_maximum_fusion.refs_0_), channel_id=1, source_target_pairs={{0,192},{1,49},{16,208},{17,1},{32,224},{33,17},{48,240},{49,33},{... | collective-permute-start | bytes 3194888 | tf_op jit(solution)/shard_map/ppermute | solution.py:38
  21.2 1.6 %collective-permute-start.5 = (bf16[4,1040,128]{2,1,0:T(8,128)(2,1)S(1)}, bf16[4,1040,128]{2,1,0:T(8,128)(2,1)}, u32[]{:S(2)}, u32[]{:S(2)}) collective-permute-start(bf16[4,1040,128]{2,1,0:T(8,128)(2,1)S(1)} %pad_maximum_fusion.refs_0_), channel_id=1, source_target_pairs={{0,128},{1,33},{16,144},{17,49},{32,160},{33,1},{48,176},{49,17},{... | collective-permute-start | bytes 3194888 | tf_op jit(solution)/shard_map/ppermute | solution.py:38
  22.7 0.9 %collective-permute-done.7.refs_6_ = bf16[2,1040,128]{2,1,0:T(8,128)(2,1)S(1)} collective-permute-done((bf16[2,1040,128]{2,1,0:T(8,128)(2,1)S(1)}, bf16[2,1040,128]{2,1,0:T(8,128)(2,1)S(1)}, u32[]{:S(2)}, u32[]{:S(2)}) %collective-permute-start.7) | collective-permute-done | bytes 532512 | tf_op jit(solution)/shard_map/ppermute | solution.py:46
  23.7 0.8 %copy-done.2 = bf16[2,1040,128]{2,1,0:T(8,128)(2,1)} copy-done((bf16[2,1040,128]{2,1,0:T(8,128)(2,1)}, bf16[2,1040,128]{2,1,0:T(8,128)(2,1)S(1)}, u32[]{:S(2)}) %copy-start.2) | copy-done | bytes 532504
  24.5 2.8 %collective-permute-start.10 = (bf16[2,1040,128]{2,1,0:T(8,128)(2,1)S(1)}, bf16[2,1040,128]{2,1,0:T(8,128)(2,1)}, u32[]{:S(2)}, u32[]{:S(2)}) collective-permute-start(bf16[2,1040,128]{2,1,0:T(8,128)(2,1)S(1)} %collective-permute-done.7.refs_6_), channel_id=1, source_target_pairs={{0,1},{1,0},{2,3},{3,2},{4,5},{5,4},{6,7},{7,6},{8,9},{9,8},{10,11... | collective-permute-start | bytes 1597448 | tf_op jit(solution)/shard_map/ppermute | solution.py:50
  27.9 0.7 %slice_select_fusion = bf16[1,1040,128]{2,1,0:T(8,128)(2,1)} fusion(bf16[2,1040,128]{2,1,0:T(8,128)(2,1)S(1)} %collective-permute-done.7.refs_6_, pred[]{:T(512)S(6)} %eq.3), kind=kLoop, calls=%fused_computation.1 | loop fusion | flops 133120 | bytes 798721 | tf_op jit(solution)/shard_map/jit(_where)/select_n | solution.py:381
  29.0 1.0 %collective-permute-start.12 = (bf16[1,1040,128]{2,1,0:T(8,128)(2,1)}, bf16[1,1040,128]{2,1,0:T(8,128)(2,1)S(1)}, u32[]{:S(2)}, u32[]{:S(2)}) collective-permute-start(bf16[1,1040,128]{2,1,0:T(8,128)(2,1)} %slice_select_fusion), channel_id=1, source_target_pairs={{0,4},{1,13},{2,6},{3,15},{4,8},{5,1},{6,10},{7,3},{8,12},{9,5},{1... | collective-permute-start | bytes 798728 | tf_op jit(solution)/shard_map/ppermute | solution.py:46
  30.1 7.3 %collective-permute-done.9.refs_7_ = bf16[2,1040,128]{2,1,0:T(8,128)(2,1)} collective-permute-done((bf16[2,1040,128]{2,1,0:T(8,128)(2,1)S(1)}, bf16[2,1040,128]{2,1,0:T(8,128)(2,1)}, u32[]{:S(2)}, u32[]{:S(2)}) %collective-permute-start.9) | collective-permute-done | bytes 532512 | tf_op jit(solution)/shard_map/ppermute | solution.py:46
  37.9 2.0 %collective-permute-done.12.refs_11_ = bf16[1,1040,128]{2,1,0:T(8,128)(2,1)S(1)} collective-permute-done((bf16[1,1040,128]{2,1,0:T(8,128)(2,1)}, bf16[1,1040,128]{2,1,0:T(8,128)(2,1)S(1)}, u32[]{:S(2)}, u32[]{:S(2)}) %collective-permute-start.12) | collective-permute-done | bytes 266272 | tf_op jit(solution)/shard_map/ppermute | solution.py:46
  39.9 2.4 %collective-permute-start.13 = (bf16[1,1040,128]{2,1,0:T(8,128)(2,1)S(1)}, bf16[1,1040,128]{2,1,0:T(8,128)(2,1)S(1)}, u32[]{:S(2)}, u32[]{:S(2)}) collective-permute-start(bf16[1,1040,128]{2,1,0:T(8,128)(2,1)S(1)} %collective-permute-done.12.refs_11_), channel_id=1, source_target_pairs={{0,1},{1,0},{2,3},{3,2},{4,5},{5,4},{6,7},{7,6},{8,9},{9,8},{10,11... | collective-permute-start | bytes 798728 | tf_op jit(solution)/shard_map/ppermute | solution.py:50
  42.2 2.3 %collective-permute-done.4.refs_1_.refs_2_ = bf16[4,1040,128]{2,1,0:T(8,128)(2,1)} collective-permute-done((bf16[4,1040,128]{2,1,0:T(8,128)(2,1)S(1)}, bf16[4,1040,128]{2,1,0:T(8,128)(2,1)}, u32[]{:S(2)}, u32[]{:S(2)}) %collective-permute-start.4) | collective-permute-done | bytes 1064992 | tf_op jit(solution)/shard_map/ppermute | solution.py:38
  44.5 1.9 %collective-permute-done.5.refs_2_.refs_3_ = bf16[4,1040,128]{2,1,0:T(8,128)(2,1)} collective-permute-done((bf16[4,1040,128]{2,1,0:T(8,128)(2,1)S(1)}, bf16[4,1040,128]{2,1,0:T(8,128)(2,1)}, u32[]{:S(2)}, u32[]{:S(2)}) %collective-permute-start.5) | collective-permute-done | bytes 1064992 | tf_op jit(solution)/shard_map/ppermute | solution.py:38
  46.5 6.8 %multiply.1 = (f32[16,128,128]{2,1,0:T(8,128)}, f32[16,128,128]{2,1,0:T(8,128)}) custom-call(s32[16,128]{1,0:T(8,128)S(1)} %pad.4.keep, f32[8,128]{1,0:T(8,128)S(1)} %marker.1.marked, bf16[4,1040,128]{2,1,0:T(8,128)(2,1)S(1)} %pad_maximum_fusion.refs_0_, bf16[4,1040,128]{2,1,0:T(8,128)(2,1)S(1)} %collective-permute-done.3.refs_0_.refs_1_, ...), custom_call_target="tpu_custom_call" | custom-call | tf_op jit(solution)/shard_map/multiply/pallas_call | solution.py:297
  53.9 2.4 %collective-permute-done.14.other = f32[16,128,128]{2,1,0:T(8,128)S(1)} collective-permute-done((f32[16,128,128]{2,1,0:T(8,128)}, f32[16,128,128]{2,1,0:T(8,128)S(1)}, u32[]{:S(2)}, u32[]{:S(2)}) %collective-permute-start.14) | collective-permute-done | bytes 1048608 | tf_op jit(solution)/shard_map/ppermute | solution.py:50
  56.3 2.0 %finish.1 = bf16[1024,256]{1,0:T(8,128)(2,1)} custom-call(s32[8,2]{1,0:T(8,128)S(1)} %copy.12.keep_in, f32[16,128,128]{2,1,0:T(8,128)} %get-tuple-element.19.own, f32[16,128,128]{2,1,0:T(8,128)S(1)} %collective-permute-done.14.other), custom_call_target="tpu_custom_call" | custom-call | tf_op jit(solution)/shard_map/finish/pallas_call | solution.py:352
  (27 shorter events, 2.4 us)
Async XLA Ops:
  1.3 12.7 %collective-permute-start.6 = (bf16[2,1040,128]{2,1,0:T(8,128)(2,1)S(1)}, bf16[2,1040,128]{2,1,0:T(8,128)(2,1)S(1)}, u32[]{:S(2)}, u32[]{:S(2)}) collective-permute-start(bf16[2,1040,128]{2,1,0:T(8,128)(2,1)S(1)} %get-tuple-element.14.refs_4_), channel_id=1, source_target_pairs={{0,2},{1,15},{2,4},{3,1},{4,6},{5,3},{6,8},{7,5},{8,10},{9,7},{10,... | collective-permute-start | bytes 1597448 | tf_op jit(solution)/shard_map/ppermute | solution.py:46
  7.8 9.6 %collective-permute-start = (bf16[1040,128]{1,0:T(8,128)(2,1)S(1)}, bf16[1040,128]{1,0:T(8,128)(2,1)S(1)}, u32[]{:S(2)}, u32[]{:S(2)}) collective-permute-start(bf16[1040,128]{1,0:T(8,128)(2,1)S(1)} %get-tuple-element.13), channel_id=1, source_target_pairs={{0,16},{1,65},{16,32},{17,81},{32,48},{33,97},{48,0},{49,113},{64,... | collective-permute-start | bytes 798728 | tf_op jit(solution)/shard_map/ppermute | solution.py:38
  9.0 8.4 %collective-permute-start.1 = (bf16[1040,128]{1,0:T(8,128)(2,1)S(1)}, bf16[1040,128]{1,0:T(8,128)(2,1)S(1)}, u32[]{:S(2)}, u32[]{:S(2)}) collective-permute-start(bf16[1040,128]{1,0:T(8,128)(2,1)S(1)} %get-tuple-element.13), channel_id=1, source_target_pairs={{0,48},{1,193},{16,0},{17,209},{32,16},{33,225},{48,32},{49,241},{... | collective-permute-start | bytes 798728 | tf_op jit(solution)/shard_map/ppermute | solution.py:38
  10.5 7.6 %collective-permute-start.2 = (bf16[1040,128]{1,0:T(8,128)(2,1)S(1)}, bf16[1040,128]{1,0:T(8,128)(2,1)S(1)}, u32[]{:S(2)}, u32[]{:S(2)}) collective-permute-start(bf16[1040,128]{1,0:T(8,128)(2,1)S(1)} %get-tuple-element.13), channel_id=1, source_target_pairs={{0,32},{1,129},{16,48},{17,145},{32,0},{33,161},{48,16},{49,177},{... | collective-permute-start | bytes 798728 | tf_op jit(solution)/shard_map/ppermute | solution.py:38
  14.0 4.2 %copy-start = (bf16[2,1040,128]{2,1,0:T(8,128)(2,1)}, bf16[2,1040,128]{2,1,0:T(8,128)(2,1)S(1)}, u32[]{:S(2)}) copy-start(bf16[2,1040,128]{2,1,0:T(8,128)(2,1)S(1)} %collective-permute-done.6.refs_5_) | copy-start | bytes 1597444
  14.0 9.6 %collective-permute-start.7 = (bf16[2,1040,128]{2,1,0:T(8,128)(2,1)S(1)}, bf16[2,1040,128]{2,1,0:T(8,128)(2,1)S(1)}, u32[]{:S(2)}, u32[]{:S(2)}) collective-permute-start(bf16[2,1040,128]{2,1,0:T(8,128)(2,1)S(1)} %collective-permute-done.6.refs_5_), channel_id=1, source_target_pairs={{0,2},{1,15},{2,4},{3,1},{4,6},{5,3},{6,8},{7,5},{8,10},{9,7},{10,... | collective-permute-start | bytes 1597448 | tf_op jit(solution)/shard_map/ppermute | solution.py:46
  17.4 6.2 %collective-permute-start.8 = (bf16[2,1040,128]{2,1,0:T(8,128)(2,1)S(1)}, bf16[2,1040,128]{2,1,0:T(8,128)(2,1)S(1)}, u32[]{:S(2)}, u32[]{:S(2)}) collective-permute-start(bf16[2,1040,128]{2,1,0:T(8,128)(2,1)S(1)} %collective-permute-done.6.refs_5_), channel_id=1, source_target_pairs={{0,1},{1,0},{2,3},{3,2},{4,5},{5,4},{6,7},{7,6},{8,9},{9,8},{10,11... | collective-permute-start | bytes 1597448 | tf_op jit(solution)/shard_map/ppermute | solution.py:50
  18.1 11.8 %copy-start.4 = (s32[8,16,4]{1,2,0:T(4,128)S(1)}, s32[8,16,4]{1,2,0:T(4,128)}, u32[]{:S(2)}) copy-start(s32[8,16,4]{1,2,0:T(4,128)} %param.14) | copy-start | bytes 6148
  18.3 24.0 %collective-permute-start.3 = (bf16[4,1040,128]{2,1,0:T(8,128)(2,1)S(1)}, bf16[4,1040,128]{2,1,0:T(8,128)(2,1)S(1)}, u32[]{:S(2)}, u32[]{:S(2)}) collective-permute-start(bf16[4,1040,128]{2,1,0:T(8,128)(2,1)S(1)} %pad_maximum_fusion.refs_0_), channel_id=1, source_target_pairs={{0,64},{1,17},{16,80},{17,33},{32,96},{33,49},{48,112},{49,1},{64,... | collective-permute-start | bytes 3194888 | tf_op jit(solution)/shard_map/ppermute | solution.py:38
  19.7 24.9 %collective-permute-start.4 = (bf16[4,1040,128]{2,1,0:T(8,128)(2,1)S(1)}, bf16[4,1040,128]{2,1,0:T(8,128)(2,1)}, u32[]{:S(2)}, u32[]{:S(2)}) collective-permute-start(bf16[4,1040,128]{2,1,0:T(8,128)(2,1)S(1)} %pad_maximum_fusion.refs_0_), channel_id=1, source_target_pairs={{0,192},{1,49},{16,208},{17,1},{32,224},{33,17},{48,240},{49,33},{... | collective-permute-start | bytes 3194888 | tf_op jit(solution)/shard_map/ppermute | solution.py:38
  21.2 25.3 %collective-permute-start.5 = (bf16[4,1040,128]{2,1,0:T(8,128)(2,1)S(1)}, bf16[4,1040,128]{2,1,0:T(8,128)(2,1)}, u32[]{:S(2)}, u32[]{:S(2)}) collective-permute-start(bf16[4,1040,128]{2,1,0:T(8,128)(2,1)S(1)} %pad_maximum_fusion.refs_0_), channel_id=1, source_target_pairs={{0,128},{1,33},{16,144},{17,49},{32,160},{33,1},{48,176},{49,17},{... | collective-permute-start | bytes 3194888 | tf_op jit(solution)/shard_map/ppermute | solution.py:38
  23.7 0.8 %copy-start.2 = (bf16[2,1040,128]{2,1,0:T(8,128)(2,1)}, bf16[2,1040,128]{2,1,0:T(8,128)(2,1)S(1)}, u32[]{:S(2)}) copy-start(bf16[2,1040,128]{2,1,0:T(8,128)(2,1)S(1)} %collective-permute-done.8.refs_8_) | copy-start | bytes 1597444
  24.5 4.5 %collective-permute-start.10 = (bf16[2,1040,128]{2,1,0:T(8,128)(2,1)S(1)}, bf16[2,1040,128]{2,1,0:T(8,128)(2,1)}, u32[]{:S(2)}, u32[]{:S(2)}) collective-permute-start(bf16[2,1040,128]{2,1,0:T(8,128)(2,1)S(1)} %collective-permute-done.7.refs_6_), channel_id=1, source_target_pairs={{0,1},{1,0},{2,3},{3,2},{4,5},{5,4},{6,7},{7,6},{8,9},{9,8},{10,11... | collective-permute-start | bytes 1597448 | tf_op jit(solution)/shard_map/ppermute | solution.py:50
  27.3 10.0 %collective-permute-start.9 = (bf16[2,1040,128]{2,1,0:T(8,128)(2,1)S(1)}, bf16[2,1040,128]{2,1,0:T(8,128)(2,1)}, u32[]{:S(2)}, u32[]{:S(2)}) collective-permute-start(bf16[2,1040,128]{2,1,0:T(8,128)(2,1)S(1)} %collective-permute-done.7.refs_6_), channel_id=1, source_target_pairs={{0,2},{1,15},{2,4},{3,1},{4,6},{5,3},{6,8},{7,5},{8,10},{9,7},{10,... | collective-permute-start | bytes 1597448 | tf_op jit(solution)/shard_map/ppermute | solution.py:46
  29.0 10.9 %collective-permute-start.12 = (bf16[1,1040,128]{2,1,0:T(8,128)(2,1)}, bf16[1,1040,128]{2,1,0:T(8,128)(2,1)S(1)}, u32[]{:S(2)}, u32[]{:S(2)}) collective-permute-start(bf16[1,1040,128]{2,1,0:T(8,128)(2,1)} %slice_select_fusion), channel_id=1, source_target_pairs={{0,4},{1,13},{2,6},{3,15},{4,8},{5,1},{6,10},{7,3},{8,12},{9,5},{1... | collective-permute-start | bytes 798728 | tf_op jit(solution)/shard_map/ppermute | solution.py:46
  30.0 16.4 %copy-start.1 = (bf16[2,1040,128]{2,1,0:T(8,128)(2,1)S(1)}, bf16[2,1040,128]{2,1,0:T(8,128)(2,1)}, u32[]{:S(2)}) copy-start(bf16[2,1040,128]{2,1,0:T(8,128)(2,1)} %copy-done) | copy-start | bytes 1597444
  30.0 16.4 %copy-start.3 = (bf16[2,1040,128]{2,1,0:T(8,128)(2,1)S(1)}, bf16[2,1040,128]{2,1,0:T(8,128)(2,1)}, u32[]{:S(2)}) copy-start(bf16[2,1040,128]{2,1,0:T(8,128)(2,1)} %copy-done.2) | copy-start | bytes 1597444
  37.4 9.1 %collective-permute-start.11 = (bf16[2,1040,128]{2,1,0:T(8,128)(2,1)}, bf16[2,1040,128]{2,1,0:T(8,128)(2,1)S(1)}, u32[]{:S(2)}, u32[]{:S(2)}) collective-permute-start(bf16[2,1040,128]{2,1,0:T(8,128)(2,1)} %collective-permute-done.9.refs_7_), channel_id=1, source_target_pairs={{0,1},{1,0},{2,3},{3,2},{4,5},{5,4},{6,7},{7,6},{8,9},{9,8},{10,11... | collective-permute-start | bytes 1597448 | tf_op jit(solution)/shard_map/ppermute | solution.py:50
  39.9 6.6 %collective-permute-start.13 = (bf16[1,1040,128]{2,1,0:T(8,128)(2,1)S(1)}, bf16[1,1040,128]{2,1,0:T(8,128)(2,1)S(1)}, u32[]{:S(2)}, u32[]{:S(2)}) collective-permute-start(bf16[1,1040,128]{2,1,0:T(8,128)(2,1)S(1)} %collective-permute-done.12.refs_11_), channel_id=1, source_target_pairs={{0,1},{1,0},{2,3},{3,2},{4,5},{5,4},{6,7},{7,6},{8,9},{9,8},{10,11... | collective-permute-start | bytes 798728 | tf_op jit(solution)/shard_map/ppermute | solution.py:50
  46.5 7.4 %copy-start.5 = (s32[8,2]{0,1:T(2,128)S(1)}, s32[8,2]{0,1:T(2,128)}, u32[]{:S(2)}) copy-start(s32[8,2]{0,1:T(2,128)} %param.15) | copy-start | bytes 196
  53.3 3.0 %collective-permute-start.14 = (f32[16,128,128]{2,1,0:T(8,128)}, f32[16,128,128]{2,1,0:T(8,128)S(1)}, u32[]{:S(2)}, u32[]{:S(2)}) collective-permute-start(f32[16,128,128]{2,1,0:T(8,128)} %get-tuple-element.20), channel_id=1, source_target_pairs={{0,1},{1,0},{2,3},{3,2},{4,5},{5,4},{6,7},{7,6},{8,9},{9,8},{10,11... | collective-permute-start | bytes 3145736 | tf_op jit(solution)/shard_map/ppermute | solution.py:50

commit v6 on v5

--- a/solution.py
+++ b/solution.py
@@ -15,15 +15,15 @@
 DATA = HALF * BLK
 ROWS = DATA + META
 MOST = 64
-PICKS = 8
+PICKS = 10
 NEAR = 16
 LISTS = 80
-STEP = 8
+STEP = 16
 BUCKETS = 32
 ITEMS = 2
 NONE = 128
-DELTA = (0, SIDE - 1, 1, 2)
-STEPS = (1, -1, 2)
+DELTA = (0, 2, SIDE - 1, 1)
+STEPS = (2, 1, -1)
 
 
 def move_a(value, distance, phase):
@@ -204,8 +204,9 @@
         keys[p] = jnp.where(valid, base + slot * 128.0 + found, none)
         count = count + jnp.where(valid, 1.0, 0.0)
     count = jnp.sum(count, axis=0, keepdims=True)
-    list_v[0:1, :] = count.astype(jnp.int32)
-    largest = jnp.max(count).astype(jnp.int32)
+    most = jnp.max(count, axis=1, keepdims=True)
+    last_lane = lax.broadcasted_iota(jnp.int32, (1, BLK), 1) == BLK - 1
+    list_v[0:1, :] = jnp.where(last_lane, most, count).astype(jnp.int32)
 
     def pick(j):
         least = keys[0]
@@ -223,6 +224,7 @@
     )
     first_part.start()
     first_part.wait()
+    largest = lists[0, BLK - 1]
 
     @pl.when(largest > PICKS)
     def _():
@@ -262,7 +264,7 @@
 
     for b in range(BUCKETS):
         pairs = [blocks_of(lists[1 + j, b]) for j in range(ITEMS)]
-        acc[b] = jnp.dot(
+        acc[b // CB, b % CB] = jnp.dot(
             jnp.concatenate([left for left, _ in pairs], axis=1),
             jnp.concatenate([right for _, right in pairs], axis=0),
             preferred_element_type=jnp.float32,
@@ -272,18 +274,15 @@
         for j in range(STEP):
             code = flat[i * STEP + j]
             left, right = blocks_of(code // BUCKETS)
-            acc[code % BUCKETS] += jnp.dot(left, right, preferred_element_type=jnp.float32)
+            b = code % BUCKETS
+            acc[b // CB, b % CB] += jnp.dot(left, right, preferred_element_type=jnp.float32)
         return carry
 
     lax.fori_loop(0, (total + STEP - 1) // STEP, step, 0)
-    keeping = []
-    for n, (out, base) in enumerate(((send, 2 * (1 - core)), (own, 2 * core))):
-        for r in range(RB):
-            keeping.append(
-                pltpu.make_async_copy(
-                    acc.at[pl.ds(r * CB + base, 2)], out.at[pl.ds(2 * r, 2)], out_sem.at[n, r]
-                )
-            )
+    keeping = [
+        pltpu.make_async_copy(acc.at[:, pl.ds(base, 2)], out, out_sem.at[n])
+        for n, (out, base) in enumerate(((send, 2 * (1 - core)), (own, 2 * core)))
+    ]
     for copy in keeping:
         copy.start()
     for copy in keeping:
@@ -293,7 +292,7 @@
 def partial_sums(keep, a_parts, b_parts):
     vmem = pl.BlockSpec(memory_space=pltpu.VMEM)
     anywhere = pl.BlockSpec(memory_space=pl.ANY)
-    half = jax.ShapeDtypeStruct((2 * RB, BLK, BLK), jnp.float32)
+    half = jax.ShapeDtypeStruct((RB, 2, BLK, BLK), jnp.float32)
     return pl.pallas_call(
         multiply,
         out_shape=(half, pltpu.HBM(half.shape, half.dtype)),
@@ -304,7 +303,7 @@
             pltpu.VMEM((16, DATA, BLK), jnp.bfloat16),
             pltpu.VMEM((16, META, BLK), jnp.bfloat16),
             pltpu.VMEM((16, META, BLK), jnp.bfloat16),
-            pltpu.VMEM((BUCKETS, BLK, BLK), jnp.float32),
+            pltpu.VMEM((RB, CB, BLK, BLK), jnp.float32),
             pltpu.VMEM((16, HALF, BLK), jnp.float32),
             pltpu.VMEM((LISTS, BLK), jnp.int32),
             pltpu.SMEM((LISTS, BLK), jnp.int32),
@@ -312,7 +311,7 @@
             pltpu.SemaphoreType.DMA((13,)),
             pltpu.SemaphoreType.DMA((13,)),
             pltpu.SemaphoreType.DMA((2,)),
-            pltpu.SemaphoreType.DMA((2, RB)),
+            pltpu.SemaphoreType.DMA((2,)),
         ],
         compiler_params=pltpu.CompilerParams(vmem_limit_bytes=28 * 1024 * 1024),
         name="multiply",
@@ -324,7 +323,7 @@
     keeps.start()
     copies = [
         pltpu.make_async_copy(
-            source.at[pl.ds(4 * r, 4)], held.at[i, pl.ds(4 * r, 4)], sem.at[i, r]
+            source.at[pl.ds(2 * r, 2)], held.at[i, pl.ds(2 * r, 2)], sem.at[i, r]
         )
         for r in range(RB // 2)
         for i, source in enumerate((own, other))
@@ -337,7 +336,8 @@
         copies[2 * r].wait()
         copies[2 * r + 1].wait()
         for b in range(4 * r, 4 * r + 4):
-            total = (held[0, b] + held[1, b]) * keep[b // 2, b % 2].astype(jnp.float32)
+            at = (b // 2, b % 2)
+            total = (held[0, *at] + held[1, *at]) * keep[at].astype(jnp.float32)
             cols = slice(b % 2 * BLK, (b % 2 + 1) * BLK)
             made[b // 2 * BLK : (b // 2 + 1) * BLK, cols] = total.astype(jnp.bfloat16)
         rows = pl.ds(2 * r * BLK, 2 * BLK)
@@ -355,7 +355,7 @@
         in_specs=[anywhere] * 3,
         out_specs=anywhere,
         scratch_shapes=[
-            pltpu.VMEM((2, 2 * RB, BLK, BLK), jnp.float32),
+            pltpu.VMEM((2, RB, 2, BLK, BLK), jnp.float32),
             pltpu.VMEM((RB * BLK, 2 * BLK), jnp.bfloat16),
             pltpu.SMEM((RB, 2), jnp.int32),
             pltpu.SemaphoreType.DMA((2, RB // 2)),

time: 59.1 us -> 58.4 us (0.988)
  waiting for transfers between devices: 19.9 us -> 16.5 us
  starting transfers between devices: 26.4 us -> 29.2 us
    ppermute x6, starting transfers between devices: 8.67 us -> 11.1 us  [move_a(): return lax.ppermute(value, ('row', 'layer'), pairs)]
    ppermute x4, waiting for transfers between devices: 12.2 us -> 10.5 us  [move_b(): return lax.ppermute(value, ('col', 'layer'), pairs)]
    ppermute x6, waiting for transfers between devices: 4.89 us -> 3.22 us  [move_a(): return lax.ppermute(value, ('row', 'layer'), pairs)]
where the time goes in v6:
time: 58.4 us; the launch traced here: 58 us
  starting transfers between devices  29.2 us (50%)
  waiting for transfers between devices  16.5 us (28%)
  Pallas kernels  10.3 us (18%)
  local copies, waits for them, and re-layouts  0.97 us (2%)
  other arithmetic  0.87 us (1%)
    ppermute x4, starting transfers between devices, move_b(): return lax.ppermute(value, ('col', 'layer'), pairs)  11.5 us
    ppermute x6, starting transfers between devices, move_a(): return lax.ppermute(value, ('row', 'layer'), pairs)  11.1 us
    ppermute x4, waiting for transfers between devices, move_b(): return lax.ppermute(value, ('col', 'layer'), pairs)  10.5 us
    pallas_call x1, Pallas kernels, partial_sums(): pl.pallas_call(multiply, out_shape=(half, pltpu.HBM(half.shape, half.dtyp...  6.94 us
    ppermute x5, starting transfers between devices, swap(): return lax.ppermute(value, 'layer', [(0, 1), (1, 0)])  6.53 us
    ppermute x6, waiting for transfers between devices, move_a(): return lax.ppermute(value, ('row', 'layer'), pairs)  3.22 us
    ppermute x5, waiting for transfers between devices, swap(): return lax.ppermute(value, 'layer', [(0, 1), (1, 0)])  2.8 us
    pallas_call x1, Pallas kernels, filtered(): pl.pallas_call(finish, out_shape=jax.ShapeDtypeStruct((RB * BLK, 2 * BLK)...  2 us
  transfers between devices with their start and end apart: 15, of which 9 were waited for; matrix products, arithmetic and copies ran while one was open for 2% of the time, Pallas kernels for 0%

profile of v6, /device:TPU:1, one launch (start us, length us, event | category | flops | bytes accessed | tf_op | source)
XLA Modules:
  0.0 58.0 jit_solution(7331777378954345776)
XLA Ops:
  0.0 1.3 %pack.1 = (bf16[1040,128]{1,0:T(8,128)(2,1)S(1)}, bf16[2,1040,128]{2,1,0:T(8,128)(2,1)S(1)}) custom-call(s32[1,1,16]{2,1,0:T(1,128)} %a_rows.1, s32[1,1,16]{2,1,0:T(1,128)} %a_cols.1, s32[2,1,8]{2,1,0:T(1,128)} %b_rows.1, s32[2,1,8]{2,1,0:T(1,128)} %b_cols.1, bf16[1,1,16,128,128]{4,3,2,1,0:T(8,128)(2,1)} %a_blocks.1, bf16[2,1,8,128,128]{4,3,2,1,0:T(8,128)(2,1)} %b_blocks.1), custom_call_target="tpu_custom_call" | custom-call | tf_op jit(solution)/shard_map/pack/pallas_call | solution.py:101
  1.3 6.5 %collective-permute-start.6 = (bf16[2,1040,128]{2,1,0:T(8,128)(2,1)S(1)}, bf16[2,1040,128]{2,1,0:T(8,128)(2,1)S(1)}, u32[]{:S(2)}, u32[]{:S(2)}) collective-permute-start(bf16[2,1040,128]{2,1,0:T(8,128)(2,1)S(1)} %get-tuple-element.14.refs_4_), channel_id=1, source_target_pairs={{0,2},{1,15},{2,4},{3,1},{4,6},{5,3},{6,8},{7,5},{8,10},{9,7},{10,... | collective-permute-start | bytes 1597448 | tf_op jit(solution)/shard_map/ppermute | solution.py:46
  7.8 2.7 %collective-permute-start = (bf16[1040,128]{1,0:T(8,128)(2,1)S(1)}, bf16[1040,128]{1,0:T(8,128)(2,1)S(1)}, u32[]{:S(2)}, u32[]{:S(2)}) collective-permute-start(bf16[1040,128]{1,0:T(8,128)(2,1)S(1)} %get-tuple-element.13), channel_id=1, source_target_pairs={{0,32},{1,129},{16,48},{17,145},{32,0},{33,161},{48,16},{49,177},{... | collective-permute-start | bytes 798728 | tf_op jit(solution)/shard_map/ppermute | solution.py:38
  10.9 2.4 %collective-permute-start.2 = (bf16[1040,128]{1,0:T(8,128)(2,1)S(1)}, bf16[1040,128]{1,0:T(8,128)(2,1)S(1)}, u32[]{:S(2)}, u32[]{:S(2)}) collective-permute-start(bf16[1040,128]{1,0:T(8,128)(2,1)S(1)} %get-tuple-element.13), channel_id=1, source_target_pairs={{0,48},{1,193},{16,0},{17,209},{32,16},{33,225},{48,32},{49,241},{... | collective-permute-start | bytes 798728 | tf_op jit(solution)/shard_map/ppermute | solution.py:38
  13.2 0.8 %collective-permute-done.6.refs_5_ = bf16[2,1040,128]{2,1,0:T(8,128)(2,1)S(1)} collective-permute-done((bf16[2,1040,128]{2,1,0:T(8,128)(2,1)S(1)}, bf16[2,1040,128]{2,1,0:T(8,128)(2,1)S(1)}, u32[]{:S(2)}, u32[]{:S(2)}) %collective-permute-start.6) | collective-permute-done | bytes 532512 | tf_op jit(solution)/shard_map/ppermute | solution.py:46
  14.0 3.4 %collective-permute-start.7 = (bf16[2,1040,128]{2,1,0:T(8,128)(2,1)S(1)}, bf16[2,1040,128]{2,1,0:T(8,128)(2,1)S(1)}, u32[]{:S(2)}, u32[]{:S(2)}) collective-permute-start(bf16[2,1040,128]{2,1,0:T(8,128)(2,1)S(1)} %collective-permute-done.6.refs_5_), channel_id=1, source_target_pairs={{0,2},{1,15},{2,4},{3,1},{4,6},{5,3},{6,8},{7,5},{8,10},{9,7},{10,... | collective-permute-start | bytes 1597448 | tf_op jit(solution)/shard_map/ppermute | solution.py:46
  17.7 3.0 %collective-permute-start.3 = (bf16[4,1040,128]{2,1,0:T(8,128)(2,1)S(1)}, bf16[4,1040,128]{2,1,0:T(8,128)(2,1)S(1)}, u32[]{:S(2)}, u32[]{:S(2)}) collective-permute-start(bf16[4,1040,128]{2,1,0:T(8,128)(2,1)S(1)} %pad_maximum_fusion.refs_0_), channel_id=1, source_target_pairs={{0,128},{1,33},{16,144},{17,49},{32,160},{33,1},{48,176},{49,17},{... | collective-permute-start | bytes 3194888 | tf_op jit(solution)/shard_map/ppermute | solution.py:38
  20.7 0.4 collective-permute-start.4
  21.1 2.3 %collective-permute-start.5 = (bf16[4,1040,128]{2,1,0:T(8,128)(2,1)S(1)}, bf16[4,1040,128]{2,1,0:T(8,128)(2,1)}, u32[]{:S(2)}, u32[]{:S(2)}) collective-permute-start(bf16[4,1040,128]{2,1,0:T(8,128)(2,1)S(1)} %pad_maximum_fusion.refs_0_), channel_id=1, source_target_pairs={{0,192},{1,49},{16,208},{17,1},{32,224},{33,17},{48,240},{49,33},{... | collective-permute-start | bytes 3194888 | tf_op jit(solution)/shard_map/ppermute | solution.py:38
  23.7 0.8 %copy-done.2 = bf16[2,1040,128]{2,1,0:T(8,128)(2,1)} copy-done((bf16[2,1040,128]{2,1,0:T(8,128)(2,1)}, bf16[2,1040,128]{2,1,0:T(8,128)(2,1)S(1)}, u32[]{:S(2)}) %copy-start.2) | copy-done | bytes 532504
  24.5 2.8 %collective-permute-start.10 = (bf16[2,1040,128]{2,1,0:T(8,128)(2,1)S(1)}, bf16[2,1040,128]{2,1,0:T(8,128)(2,1)}, u32[]{:S(2)}, u32[]{:S(2)}) collective-permute-start(bf16[2,1040,128]{2,1,0:T(8,128)(2,1)S(1)} %collective-permute-done.7.refs_6_), channel_id=1, source_target_pairs={{0,1},{1,0},{2,3},{3,2},{4,5},{5,4},{6,7},{7,6},{8,9},{9,8},{10,11... | collective-permute-start | bytes 1597448 | tf_op jit(solution)/shard_map/ppermute | solution.py:50
  27.3 0.6 collective-permute-start.9
  27.9 0.7 %slice_select_fusion = bf16[1,1040,128]{2,1,0:T(8,128)(2,1)} fusion(bf16[2,1040,128]{2,1,0:T(8,128)(2,1)S(1)} %collective-permute-done.7.refs_6_, pred[]{:T(512)S(6)} %eq.3), kind=kLoop, calls=%fused_computation.1 | loop fusion | flops 133120 | bytes 798721 | tf_op jit(solution)/shard_map/jit(_where)/select_n | solution.py:381
  28.6 0.4 collective-permute-done.10.refs_9_
  29.0 1.1 %collective-permute-start.12 = (bf16[1,1040,128]{2,1,0:T(8,128)(2,1)}, bf16[1,1040,128]{2,1,0:T(8,128)(2,1)S(1)}, u32[]{:S(2)}, u32[]{:S(2)}) collective-permute-start(bf16[1,1040,128]{2,1,0:T(8,128)(2,1)} %slice_select_fusion), channel_id=1, source_target_pairs={{0,4},{1,13},{2,6},{3,15},{4,8},{5,1},{6,10},{7,3},{8,12},{9,5},{1... | collective-permute-start | bytes 798728 | tf_op jit(solution)/shard_map/ppermute | solution.py:46
  30.1 7.5 %collective-permute-done.9.refs_7_ = bf16[2,1040,128]{2,1,0:T(8,128)(2,1)} collective-permute-done((bf16[2,1040,128]{2,1,0:T(8,128)(2,1)S(1)}, bf16[2,1040,128]{2,1,0:T(8,128)(2,1)}, u32[]{:S(2)}, u32[]{:S(2)}) %collective-permute-start.9) | collective-permute-done | bytes 532512 | tf_op jit(solution)/shard_map/ppermute | solution.py:46
  38.0 1.8 %collective-permute-done.12.refs_11_ = bf16[1,1040,128]{2,1,0:T(8,128)(2,1)S(1)} collective-permute-done((bf16[1,1040,128]{2,1,0:T(8,128)(2,1)}, bf16[1,1040,128]{2,1,0:T(8,128)(2,1)S(1)}, u32[]{:S(2)}, u32[]{:S(2)}) %collective-permute-start.12) | collective-permute-done | bytes 266272 | tf_op jit(solution)/shard_map/ppermute | solution.py:46
  39.8 2.3 %collective-permute-start.13 = (bf16[1,1040,128]{2,1,0:T(8,128)(2,1)S(1)}, bf16[1,1040,128]{2,1,0:T(8,128)(2,1)S(1)}, u32[]{:S(2)}, u32[]{:S(2)}) collective-permute-start(bf16[1,1040,128]{2,1,0:T(8,128)(2,1)S(1)} %collective-permute-done.12.refs_11_), channel_id=1, source_target_pairs={{0,1},{1,0},{2,3},{3,2},{4,5},{5,4},{6,7},{7,6},{8,9},{9,8},{10,11... | collective-permute-start | bytes 798728 | tf_op jit(solution)/shard_map/ppermute | solution.py:50
  42.1 2.8 %collective-permute-done.4.refs_1_.refs_2_ = bf16[4,1040,128]{2,1,0:T(8,128)(2,1)} collective-permute-done((bf16[4,1040,128]{2,1,0:T(8,128)(2,1)S(1)}, bf16[4,1040,128]{2,1,0:T(8,128)(2,1)}, u32[]{:S(2)}, u32[]{:S(2)}) %collective-permute-start.4) | collective-permute-done | bytes 1064992 | tf_op jit(solution)/shard_map/ppermute | solution.py:38
  44.9 0.4 collective-permute-done.5.refs_2_.refs_3_
  45.3 6.9 %multiply.1 = (f32[8,2,128,128]{3,2,1,0:T(8,128)}, f32[8,2,128,128]{3,2,1,0:T(8,128)}) custom-call(s32[16,128]{1,0:T(8,128)S(1)} %pad.4.keep, f32[8,128]{1,0:T(8,128)S(1)} %marker.1.marked, bf16[4,1040,128]{2,1,0:T(8,128)(2,1)S(1)} %pad_maximum_fusion.refs_0_, bf16[4,1040,128]{2,1,0:T(8,128)(2,1)S(1)} %collective-permute-done.3.refs_0_.refs_1_, ...), custom_call_target="tpu_custom_call" | custom-call | tf_op jit(solution)/shard_map/multiply/pallas_call | solution.py:296
  52.3 1.1 %collective-permute-start.14 = (f32[8,2,128,128]{3,2,1,0:T(8,128)}, f32[8,2,128,128]{3,2,1,0:T(8,128)S(1)}, u32[]{:S(2)}, u32[]{:S(2)}) collective-permute-start(f32[8,2,128,128]{3,2,1,0:T(8,128)} %get-tuple-element.20), channel_id=1, source_target_pairs={{0,1},{1,0},{2,3},{3,2},{4,5},{5,4},{6,7},{7,6},{8,9},{9,8},{10,11... | collective-permute-start | bytes 3145736 | tf_op jit(solution)/shard_map/ppermute | solution.py:50
  53.4 2.4 %collective-permute-done.14.other = f32[8,2,128,128]{3,2,1,0:T(8,128)S(1)} collective-permute-done((f32[8,2,128,128]{3,2,1,0:T(8,128)}, f32[8,2,128,128]{3,2,1,0:T(8,128)S(1)}, u32[]{:S(2)}, u32[]{:S(2)}) %collective-permute-start.14) | collective-permute-done | bytes 1048608 | tf_op jit(solution)/shard_map/ppermute | solution.py:50
  55.9 2.0 %finish.1 = bf16[1024,256]{1,0:T(8,128)(2,1)} custom-call(s32[8,2]{1,0:T(8,128)S(1)} %copy.12.keep_in, f32[8,2,128,128]{3,2,1,0:T(8,128)} %get-tuple-element.19.own, f32[8,2,128,128]{3,2,1,0:T(8,128)S(1)} %collective-permute-done.14.other), custom_call_target="tpu_custom_call" | custom-call | tf_op jit(solution)/shard_map/finish/pallas_call | solution.py:352
  (27 shorter events, 1.3 us)
Async XLA Ops:
  1.3 12.7 %collective-permute-start.6 = (bf16[2,1040,128]{2,1,0:T(8,128)(2,1)S(1)}, bf16[2,1040,128]{2,1,0:T(8,128)(2,1)S(1)}, u32[]{:S(2)}, u32[]{:S(2)}) collective-permute-start(bf16[2,1040,128]{2,1,0:T(8,128)(2,1)S(1)} %get-tuple-element.14.refs_4_), channel_id=1, source_target_pairs={{0,2},{1,15},{2,4},{3,1},{4,6},{5,3},{6,8},{7,5},{8,10},{9,7},{10,... | collective-permute-start | bytes 1597448 | tf_op jit(solution)/shard_map/ppermute | solution.py:46
  7.8 9.6 %collective-permute-start = (bf16[1040,128]{1,0:T(8,128)(2,1)S(1)}, bf16[1040,128]{1,0:T(8,128)(2,1)S(1)}, u32[]{:S(2)}, u32[]{:S(2)}) collective-permute-start(bf16[1040,128]{1,0:T(8,128)(2,1)S(1)} %get-tuple-element.13), channel_id=1, source_target_pairs={{0,32},{1,129},{16,48},{17,145},{32,0},{33,161},{48,16},{49,177},{... | collective-permute-start | bytes 798728 | tf_op jit(solution)/shard_map/ppermute | solution.py:38
  10.6 6.9 %collective-permute-start.1 = (bf16[1040,128]{1,0:T(8,128)(2,1)S(1)}, bf16[1040,128]{1,0:T(8,128)(2,1)S(1)}, u32[]{:S(2)}, u32[]{:S(2)}) collective-permute-start(bf16[1040,128]{1,0:T(8,128)(2,1)S(1)} %get-tuple-element.13), channel_id=1, source_target_pairs={{0,16},{1,65},{16,32},{17,81},{32,48},{33,97},{48,0},{49,113},{64,... | collective-permute-start | bytes 798728 | tf_op jit(solution)/shard_map/ppermute | solution.py:38
  10.9 6.7 %collective-permute-start.2 = (bf16[1040,128]{1,0:T(8,128)(2,1)S(1)}, bf16[1040,128]{1,0:T(8,128)(2,1)S(1)}, u32[]{:S(2)}, u32[]{:S(2)}) collective-permute-start(bf16[1040,128]{1,0:T(8,128)(2,1)S(1)} %get-tuple-element.13), channel_id=1, source_target_pairs={{0,48},{1,193},{16,0},{17,209},{32,16},{33,225},{48,32},{49,241},{... | collective-permute-start | bytes 798728 | tf_op jit(solution)/shard_map/ppermute | solution.py:38
  14.0 3.6 %copy-start = (bf16[2,1040,128]{2,1,0:T(8,128)(2,1)}, bf16[2,1040,128]{2,1,0:T(8,128)(2,1)S(1)}, u32[]{:S(2)}) copy-start(bf16[2,1040,128]{2,1,0:T(8,128)(2,1)S(1)} %collective-permute-done.6.refs_5_) | copy-start | bytes 1597444
  14.0 9.6 %collective-permute-start.7 = (bf16[2,1040,128]{2,1,0:T(8,128)(2,1)S(1)}, bf16[2,1040,128]{2,1,0:T(8,128)(2,1)S(1)}, u32[]{:S(2)}, u32[]{:S(2)}) collective-permute-start(bf16[2,1040,128]{2,1,0:T(8,128)(2,1)S(1)} %collective-permute-done.6.refs_5_), channel_id=1, source_target_pairs={{0,2},{1,15},{2,4},{3,1},{4,6},{5,3},{6,8},{7,5},{8,10},{9,7},{10,... | collective-permute-start | bytes 1597448 | tf_op jit(solution)/shard_map/ppermute | solution.py:46
  17.4 6.2 %collective-permute-start.8 = (bf16[2,1040,128]{2,1,0:T(8,128)(2,1)S(1)}, bf16[2,1040,128]{2,1,0:T(8,128)(2,1)S(1)}, u32[]{:S(2)}, u32[]{:S(2)}) collective-permute-start(bf16[2,1040,128]{2,1,0:T(8,128)(2,1)S(1)} %collective-permute-done.6.refs_5_), channel_id=1, source_target_pairs={{0,1},{1,0},{2,3},{3,2},{4,5},{5,4},{6,7},{7,6},{8,9},{9,8},{10,11... | collective-permute-start | bytes 1597448 | tf_op jit(solution)/shard_map/ppermute | solution.py:50
  17.5 12.5 %copy-start.4 = (s32[8,16,4]{1,2,0:T(4,128)S(1)}, s32[8,16,4]{1,2,0:T(4,128)}, u32[]{:S(2)}) copy-start(s32[8,16,4]{1,2,0:T(4,128)} %param.14) | copy-start | bytes 6148
  17.7 24.5 %collective-permute-start.3 = (bf16[4,1040,128]{2,1,0:T(8,128)(2,1)S(1)}, bf16[4,1040,128]{2,1,0:T(8,128)(2,1)S(1)}, u32[]{:S(2)}, u32[]{:S(2)}) collective-permute-start(bf16[4,1040,128]{2,1,0:T(8,128)(2,1)S(1)} %pad_maximum_fusion.refs_0_), channel_id=1, source_target_pairs={{0,128},{1,33},{16,144},{17,49},{32,160},{33,1},{48,176},{49,17},{... | collective-permute-start | bytes 3194888 | tf_op jit(solution)/shard_map/ppermute | solution.py:38
  20.7 24.2 %collective-permute-start.4 = (bf16[4,1040,128]{2,1,0:T(8,128)(2,1)S(1)}, bf16[4,1040,128]{2,1,0:T(8,128)(2,1)}, u32[]{:S(2)}, u32[]{:S(2)}) collective-permute-start(bf16[4,1040,128]{2,1,0:T(8,128)(2,1)S(1)} %pad_maximum_fusion.refs_0_), channel_id=1, source_target_pairs={{0,64},{1,17},{16,80},{17,33},{32,96},{33,49},{48,112},{49,1},{64,... | collective-permute-start | bytes 3194888 | tf_op jit(solution)/shard_map/ppermute | solution.py:38
  21.1 24.2 %collective-permute-start.5 = (bf16[4,1040,128]{2,1,0:T(8,128)(2,1)S(1)}, bf16[4,1040,128]{2,1,0:T(8,128)(2,1)}, u32[]{:S(2)}, u32[]{:S(2)}) collective-permute-start(bf16[4,1040,128]{2,1,0:T(8,128)(2,1)S(1)} %pad_maximum_fusion.refs_0_), channel_id=1, source_target_pairs={{0,192},{1,49},{16,208},{17,1},{32,224},{33,17},{48,240},{49,33},{... | collective-permute-start | bytes 3194888 | tf_op jit(solution)/shard_map/ppermute | solution.py:38
  23.7 0.8 %copy-start.2 = (bf16[2,1040,128]{2,1,0:T(8,128)(2,1)}, bf16[2,1040,128]{2,1,0:T(8,128)(2,1)S(1)}, u32[]{:S(2)}) copy-start(bf16[2,1040,128]{2,1,0:T(8,128)(2,1)S(1)} %collective-permute-done.8.refs_8_) | copy-start | bytes 1597444
  24.5 4.5 %collective-permute-start.10 = (bf16[2,1040,128]{2,1,0:T(8,128)(2,1)S(1)}, bf16[2,1040,128]{2,1,0:T(8,128)(2,1)}, u32[]{:S(2)}, u32[]{:S(2)}) collective-permute-start(bf16[2,1040,128]{2,1,0:T(8,128)(2,1)S(1)} %collective-permute-done.7.refs_6_), channel_id=1, source_target_pairs={{0,1},{1,0},{2,3},{3,2},{4,5},{5,4},{6,7},{7,6},{8,9},{9,8},{10,11... | collective-permute-start | bytes 1597448 | tf_op jit(solution)/shard_map/ppermute | solution.py:50
  27.3 10.4 %collective-permute-start.9 = (bf16[2,1040,128]{2,1,0:T(8,128)(2,1)S(1)}, bf16[2,1040,128]{2,1,0:T(8,128)(2,1)}, u32[]{:S(2)}, u32[]{:S(2)}) collective-permute-start(bf16[2,1040,128]{2,1,0:T(8,128)(2,1)S(1)} %collective-permute-done.7.refs_6_), channel_id=1, source_target_pairs={{0,2},{1,15},{2,4},{3,1},{4,6},{5,3},{6,8},{7,5},{8,10},{9,7},{10,... | collective-permute-start | bytes 1597448 | tf_op jit(solution)/shard_map/ppermute | solution.py:46
  29.0 10.9 %collective-permute-start.12 = (bf16[1,1040,128]{2,1,0:T(8,128)(2,1)}, bf16[1,1040,128]{2,1,0:T(8,128)(2,1)S(1)}, u32[]{:S(2)}, u32[]{:S(2)}) collective-permute-start(bf16[1,1040,128]{2,1,0:T(8,128)(2,1)} %slice_select_fusion), channel_id=1, source_target_pairs={{0,4},{1,13},{2,6},{3,15},{4,8},{5,1},{6,10},{7,3},{8,12},{9,5},{1... | collective-permute-start | bytes 798728 | tf_op jit(solution)/shard_map/ppermute | solution.py:46
  30.1 15.2 %copy-start.1 = (bf16[2,1040,128]{2,1,0:T(8,128)(2,1)S(1)}, bf16[2,1040,128]{2,1,0:T(8,128)(2,1)}, u32[]{:S(2)}) copy-start(bf16[2,1040,128]{2,1,0:T(8,128)(2,1)} %copy-done) | copy-start | bytes 1597444
  30.1 15.2 %copy-start.3 = (bf16[2,1040,128]{2,1,0:T(8,128)(2,1)S(1)}, bf16[2,1040,128]{2,1,0:T(8,128)(2,1)}, u32[]{:S(2)}) copy-start(bf16[2,1040,128]{2,1,0:T(8,128)(2,1)} %copy-done.2) | copy-start | bytes 1597444
  37.7 7.6 %collective-permute-start.11 = (bf16[2,1040,128]{2,1,0:T(8,128)(2,1)}, bf16[2,1040,128]{2,1,0:T(8,128)(2,1)S(1)}, u32[]{:S(2)}, u32[]{:S(2)}) collective-permute-start(bf16[2,1040,128]{2,1,0:T(8,128)(2,1)} %collective-permute-done.9.refs_7_), channel_id=1, source_target_pairs={{0,1},{1,0},{2,3},{3,2},{4,5},{5,4},{6,7},{7,6},{8,9},{9,8},{10,11... | collective-permute-start | bytes 1597448 | tf_op jit(solution)/shard_map/ppermute | solution.py:50
  39.8 5.5 %collective-permute-start.13 = (bf16[1,1040,128]{2,1,0:T(8,128)(2,1)S(1)}, bf16[1,1040,128]{2,1,0:T(8,128)(2,1)S(1)}, u32[]{:S(2)}, u32[]{:S(2)}) collective-permute-start(bf16[1,1040,128]{2,1,0:T(8,128)(2,1)S(1)} %collective-permute-done.12.refs_11_), channel_id=1, source_target_pairs={{0,1},{1,0},{2,3},{3,2},{4,5},{5,4},{6,7},{7,6},{8,9},{9,8},{10,11... | collective-permute-start | bytes 798728 | tf_op jit(solution)/shard_map/ppermute | solution.py:50
  45.3 8.1 %copy-start.5 = (s32[8,2]{0,1:T(2,128)S(1)}, s32[8,2]{0,1:T(2,128)}, u32[]{:S(2)}) copy-start(s32[8,2]{0,1:T(2,128)} %param.15) | copy-start | bytes 196
  52.3 3.6 %collective-permute-start.14 = (f32[8,2,128,128]{3,2,1,0:T(8,128)}, f32[8,2,128,128]{3,2,1,0:T(8,128)S(1)}, u32[]{:S(2)}, u32[]{:S(2)}) collective-permute-start(f32[8,2,128,128]{3,2,1,0:T(8,128)} %get-tuple-element.20), channel_id=1, source_target_pairs={{0,1},{1,0},{2,3},{3,2},{4,5},{5,4},{6,7},{7,6},{8,9},{9,8},{10,11... | collective-permute-start | bytes 3145736 | tf_op jit(solution)/shard_map/ppermute | solution.py:50
